TPU v7x, 32 devices: a whole 2x2x4 slice. The times are simulated.
32 devices in a mesh: section: 4 (over y, x), tile: 8 (over z, core).
Axes of the slice: x: 2, y: 2, z: 4, core: 2. Of those that a mesh axis runs over, the one named last changes fastest.
Arguments:
- cams: bfloat16 [4, 4096, 768], P(None, 'tile'), may hold values from -6 to 6
- vit_up: bfloat16 [4, 768, 1536], P('section'), may hold values from -0.21875 to 0.21875
- vit_down: bfloat16 [4, 1536, 768], P('section'), may hold values from -0.15625 to 0.15625
- proj: bfloat16 [768, 256], replicated, may hold values from -0.21875 to 0.21875
- frustum_tiles: bfloat16 [8, 8, 128, 128], P('tile'), may hold values from -0.4375 to 0.4375
- src_block: int32 [8, 8], P('tile'), may hold values from 0 to 3
- dst_block: int32 [8, 8], P('tile'), may hold values from 0 to 4
- live: int32 [8, 8], P('tile'), may hold values 0 or 1
- render_up: bfloat16 [256, 512], replicated, may hold values from -0.375 to 0.375
- render_down: bfloat16 [512, 256], replicated, may hold values from -0.25 to 0.25
- decode_up: bfloat16 [256, 512], replicated, may hold values from -0.375 to 0.375
- decode_down: bfloat16 [512, 256], replicated, may hold values from -0.25 to 0.25
- pred_grad: bfloat16 [4, 5120, 256], P('section', 'tile'), may hold values from -6 to 6
Outputs:
- prediction: bfloat16 [4, 5120, 256], P('section', 'tile')
- grad_proj: float32 [768, 256], replicated
- grad_render_up: float32 [256, 512], replicated
- grad_render_down: float32 [512, 256], replicated
- grad_decode_up: float32 [256, 512], replicated
- grad_decode_down: float32 [512, 256], replicated
All inputs are finite; a program needn't handle non-finite values. No bound on the sum of `live` on one device may be relied on, other than what follows from the above.
Results may differ from a plain program's by a relative error of at most 0.025.
Values may be sent and summed in bfloat16 or wider, within the bound.
No kernel may reach another device: no remote copies, remote signals or barrier semaphores. Data moves between devices by JAX's collectives and lax.ppermute only.
A program may use at most 128 MiB of HBM per device.

v0:
```python
import math

import jax
import jax.numpy as jnp
from jax import lax
from jax.sharding import PartitionSpec as P

eps = 1e-05


def encoder_layer(state, w_up, w_down):
    widened = state.astype(jnp.float32)
    scaling = lax.rsqrt(jnp.mean(widened * widened, axis=-1, keepdims=True) + eps)
    normed = (widened * scaling).astype(jnp.bfloat16)
    hidden = jax.nn.gelu(jnp.dot(normed, w_up, preferred_element_type=jnp.float32)).astype(
        jnp.bfloat16
    )
    return (widened + jnp.dot(hidden, w_down, preferred_element_type=jnp.float32)).astype(
        jnp.bfloat16
    )


def contract_rows(left, right):
    return lax.dot_general(
        left, right, (((0,), (0,)), ((), ())), preferred_element_type=jnp.float32
    )


def against_rows(left, right):
    return lax.dot_general(
        left, right, (((1,), (1,)), ((), ())), preferred_element_type=jnp.float32
    )


def heads_forward(bev_grid, weights):
    state = bev_grid
    stored = []
    for w_up, w_down in weights:
        scaling = lax.rsqrt(jnp.mean(state * state, axis=-1, keepdims=True) + eps)
        normed = (state * scaling).astype(jnp.bfloat16)
        preact = jnp.dot(normed, w_up, preferred_element_type=jnp.float32)
        hidden = jax.nn.gelu(preact).astype(jnp.bfloat16)
        stored.append((state, scaling, normed, preact, hidden))
        state = state + jnp.dot(hidden, w_down, preferred_element_type=jnp.float32)
    return (state.astype(jnp.bfloat16), stored)


def heads_backward(cotangent, stored, weights):
    grad_state = cotangent
    gradients = []
    for saved_block, pair in zip(stored[::-1], weights[::-1]):
        state, scaling, normed, preact, hidden = saved_block
        w_up, w_down = pair
        rounded = grad_state.astype(jnp.bfloat16)
        grad_down = contract_rows(hidden, rounded)
        grad_hidden = against_rows(rounded, w_down)
        gelu_slope = jax.jvp(jax.nn.gelu, (preact,), (jnp.ones_like(preact),))[1]
        grad_pre = (grad_hidden * gelu_slope).astype(jnp.bfloat16)
        grad_up = contract_rows(normed, grad_pre)
        grad_normed = against_rows(grad_pre, w_up)
        unit_rows = state * scaling
        grad_state = grad_state + scaling * (
            grad_normed - unit_rows * jnp.mean(grad_normed * unit_rows, axis=-1, keepdims=True)
        )
        gradients = [grad_up, grad_down] + gradients
    return (grad_state, gradients)


def on_device(
    cams,
    vit_up,
    vit_down,
    proj,
    frustum_tiles,
    src_block,
    dst_block,
    live,
    render_up,
    render_down,
    decode_up,
    decode_down,
    pred_grad,
):
    section_index = lax.axis_index("section")
    section_count = lax.axis_size("section")
    tile_count = lax.axis_size("tile")
    micro_count = cams.shape[0]
    block_rows = frustum_tiles.shape[-1]
    cam_blocks = cams.shape[1] // block_rows
    bev_blocks = pred_grad.shape[1] // block_rows
    channels = proj.shape[1]
    all_up, all_down = (
        lax.all_gather(vit_up, "section", axis=0, tiled=True),
        lax.all_gather(vit_down, "section", axis=0, tiled=True),
    )
    encoded = lax.dynamic_index_in_dim(cams, section_index, 0, keepdims=False)
    for layer_number in range(section_count):
        encoded = encoder_layer(encoded, all_up[layer_number], all_down[layer_number])
    projected = jnp.dot(encoded, proj, preferred_element_type=jnp.float32).astype(jnp.bfloat16)
    blocks = projected.reshape(cam_blocks, block_rows, channels)
    sources = src_block[0]
    targets = dst_block[0]
    alive_mask = live[0].astype(jnp.float32)[:, None, None]
    slot_tiles = frustum_tiles[0]
    chosen = jnp.take(blocks, sources, axis=0)
    pieces = (
        jnp.einsum("pij,pjc->pic", slot_tiles, chosen, preferred_element_type=jnp.float32)
        * alive_mask
    ).astype(jnp.bfloat16)
    arrived, arrived_targets = (
        lax.all_to_all(pieces, "tile", split_axis=0, concat_axis=0, tiled=True),
        lax.all_to_all(targets[:, None], "tile", split_axis=0, concat_axis=0, tiled=True),
    )
    target_pick = (arrived_targets == jnp.arange(bev_blocks, dtype=jnp.int32)[None, :]).astype(
        jnp.bfloat16
    )
    bev_grid = jnp.einsum(
        "db,dic->bic", target_pick, arrived, preferred_element_type=jnp.float32
    ).reshape(bev_blocks * block_rows, channels)
    weights = ((render_up, render_down), (decode_up, decode_down))
    prediction, stored = heads_forward(bev_grid, weights)
    scale_factor = 1.0 / math.sqrt(micro_count * bev_blocks * block_rows * tile_count)
    cotangent = pred_grad[0].astype(jnp.float32) * scale_factor
    grad_grid, gradients = heads_backward(cotangent, stored, weights)
    grad_blocks = grad_grid.reshape(bev_blocks, block_rows, channels)
    grad_pieces = jnp.take(grad_blocks, arrived_targets[:, 0], axis=0).astype(jnp.bfloat16)
    returned = lax.all_to_all(grad_pieces, "tile", split_axis=0, concat_axis=0, tiled=True)
    grad_chosen = (
        jnp.einsum("pij,pic->pjc", slot_tiles, returned, preferred_element_type=jnp.float32)
        * alive_mask
    )
    source_pick = (sources[:, None] == jnp.arange(cam_blocks, dtype=jnp.int32)[None, :]).astype(
        jnp.float32
    )
    grad_rows = jnp.einsum("pk,pjc->kjc", source_pick, grad_chosen, precision=lax.Precision.HIGHEST)
    grad_rows = grad_rows.reshape(cam_blocks * block_rows, channels).astype(jnp.bfloat16)
    grad_proj = contract_rows(encoded, grad_rows)
    totals = lax.psum(
        (grad_proj, gradients[0], gradients[1], gradients[2], gradients[3]), ("section", "tile")
    )
    return (prediction[None], totals[0], totals[1], totals[2], totals[3], totals[4])


def solution(mesh):
    placed = (
        P(None, "tile", None),
        P("section", None, None),
        P("section", None, None),
        P(),
        P("tile", None, None, None),
        P("tile", None),
        P("tile", None),
        P("tile", None),
        P(),
        P(),
        P(),
        P(),
        P("section", "tile", None),
    )
    return jax.shard_map(
        on_device,
        mesh=mesh,
        in_specs=placed,
        out_specs=(P("section", "tile", None), P(), P(), P(), P(), P()),
        check_vma=False,
    )
```

profile of v0, /device:TPU:0, one launch (start us, length us, event | category | flops | bytes accessed | tf_op | source)
XLA Modules:
  0.0 436.0 jit_solution(18360321079511560482)
XLA Ops:
  9.5 6.3 %all-to-all-start = ((s32[8,1,1]{2,1,0:T(1,128)}), s32[8,1,1]{2,1,0:T(1,128)S(1)}, u32[]{:S(2)}, u32[]{:S(2)}) async-start(s32[8,1,1]{2,1,0:T(1,128)} %copy.36), calls=%async_computation | async-start | bytes 8192 | tf_op jit(solution)/shard_map/all_to_all | solution.py:112
  17.2 91.7 %all-gather.3.cloned.1.call-done = bf16[4,768,1536]{2,1,0:T(8,128)(2,1)} async-done(((bf16[1,768,1536]{2,1,0:T(8,128)(2,1)}), bf16[4,768,1536]{2,1,0:T(8,128)(2,1)}) %all-gather.3.cloned.1.call-update) | async-done | bytes 9437200 | tf_op jit(solution)/shard_map/all_gather | solution.py:93
  108.9 98.2 %all-gather.5.cloned.1.call-done = bf16[4,1536,768]{2,1,0:T(8,128)(2,1)} async-done(((bf16[1,1536,768]{2,1,0:T(8,128)(2,1)}), bf16[4,1536,768]{2,1,0:T(8,128)(2,1)}) %all-gather.5.cloned.1.call-update) | async-done | bytes 9437200 | tf_op jit(solution)/shard_map/all_gather | solution.py:94
  207.1 6.1 %fusion.45 = (f32[512]{0:T(512)S(1)}, bf16[512,768]{1,0:T(8,128)(2,1)}) fusion(bf16[4,1536,768]{2,1,0:T(8,128)(2,1)} %all-gather.5.cloned.1.call-done, bf16[4,768,1536]{2,1,0:T(8,128)(2,1)} %all-gather.3.cloned.1.call-done, f32[512]{0:T(512)S(1)} %add_rsqrt_fusion.4, bf16[4,512,768]{2,1,0:T(8,128)(2,1)S(1)} %copy-done.21, s32[]{:T(128)S(6)} %select_n.44), kind=kOutput, calls=%fused_computation.74 | convolution fusion | flops 2426535424 | bytes 7083008 | tf_op jit(solution)/shard_map/dot_general | solution.py:18
  213.2 5.7 %fusion.48 = (f32[512]{0:T(512)S(1)}, bf16[512,768]{1,0:T(8,128)(2,1)S(1)}) fusion(bf16[4,1536,768]{2,1,0:T(8,128)(2,1)} %all-gather.5.cloned.1.call-done, bf16[4,768,1536]{2,1,0:T(8,128)(2,1)} %all-gather.3.cloned.1.call-done, bf16[512,768]{1,0:T(8,128)(2,1)} %get-tuple-element.12, f32[512]{0:T(512)S(1)} %add_rsqrt_fusion.3), kind=kOutput, calls=%fused_computation.77 | convolution fusion | flops 2426535424 | bytes 7081984 | tf_op jit(solution)/shard_map/dot_general | solution.py:18
  219.0 5.3 %fusion.51 = (f32[512]{0:T(512)S(1)}, bf16[512,768]{1,0:T(8,128)(2,1)S(1)}) fusion(bf16[4,1536,768]{2,1,0:T(8,128)(2,1)} %all-gather.5.cloned.1.call-done, bf16[4,768,1536]{2,1,0:T(8,128)(2,1)} %all-gather.3.cloned.1.call-done, bf16[512,768]{1,0:T(8,128)(2,1)S(1)} %get-tuple-element.14, f32[512]{0:T(512)S(1)} %add_rsqrt_fusion.2), kind=kOutput, calls=%fused_computation.80 | convolution fusion | flops 2426535424 | bytes 7081984 | tf_op jit(solution)/shard_map/dot_general | solution.py:18
  224.3 5.2 %fusion.53 = bf16[512,768]{1,0:T(8,128)(2,1)S(1)} fusion(bf16[512,768]{1,0:T(8,128)(2,1)S(1)} %get-tuple-element.16, bf16[4,1536,768]{2,1,0:T(8,128)(2,1)} %all-gather.5.cloned.1.call-done, bf16[4,768,1536]{2,1,0:T(8,128)(2,1)} %all-gather.3.cloned.1.call-done, f32[512]{0:T(512)S(1)} %add_rsqrt_fusion.1), kind=kOutput, calls=%fused_computation.82 | convolution fusion | flops 2425356288 | bytes 7079936 | tf_op jit(solution)/shard_map/dot_general | solution.py:18
  231.1 1.0 copy.38
  232.1 4.6 %all-to-all-start.1 = ((bf16[8,128,256]{2,1,0:T(8,128)(2,1)}), bf16[8,128,256]{2,1,0:T(8,128)(2,1)S(1)}, u32[]{:S(2)}, u32[]{:S(2)}) async-start(bf16[8,128,256]{2,1,0:T(8,128)(2,1)} %copy.38), calls=%async_computation.1 | async-start | bytes 1048576 | tf_op jit(solution)/shard_map/all_to_all | solution.py:111
  237.0 15.1 %all-to-all-done.1 = bf16[8,128,256]{2,1,0:T(8,128)(2,1)S(1)} async-done(((bf16[8,128,256]{2,1,0:T(8,128)(2,1)}), bf16[8,128,256]{2,1,0:T(8,128)(2,1)S(1)}, u32[]{:S(2)}, u32[]{:S(2)}) %all-to-all-start.1) | async-done | bytes 524320 | tf_op jit(solution)/shard_map/all_to_all | solution.py:111
  260.7 1.6 gather_fusion.1
  262.2 1.0 copy.42
  263.2 2.0 select_convert_fusion
  265.2 3.5 all-to-all-start.2
  268.8 1.2 fusion.151
  270.0 1.3 fusion.141
  271.3 1.5 fusion.105
  272.9 1.4 fusion.109
  274.3 9.7 %all-to-all-done.2 = bf16[8,128,256]{1,2,0:T(8,128)(2,1)S(1)} async-done(((bf16[8,128,256]{1,2,0:T(8,128)(2,1)}), bf16[8,128,256]{1,2,0:T(8,128)(2,1)S(1)}, u32[]{:S(2)}, u32[]{:S(2)}) %all-to-all-start.2) | async-done | bytes 524320 | tf_op jit(solution)/shard_map/all_to_all | solution.py:127
  285.9 1.3 fusion.150
  287.3 1.3 copy-done.7
  288.6 1.3 fusion.80
  289.9 134.2 %all-reduce.3.cloned.1.call-done = (f32[768,256]{1,0:T(8,128)}, f32[256,512]{1,0:T(8,128)}, f32[512,256]{1,0:T(8,128)}, f32[256,512]{1,0:T(8,128)}, f32[512,256]{1,0:T(8,128)}) async-done(((f32[768,256]{1,0:T(8,128)}, f32[256,512]{1,0:T(8,128)}, f32[512,256]{1,0:T(8,128)}, f32[256,512]{1,0:T(8,128)}, f32[512,256]{1,0:T(8,128)}), (f32[768,256]{1,0:T(8,128)}, f32[256,512]{1,0:T(8,128)}, f32[512,256]{1,0:T(8,128)}, ...) | async-done | bytes 2883600 | tf_op jit(solution)/shard_map/psum | solution.py:138
  424.1 2.2 copy.55
  (112 shorter events, 19.0 us)
Async XLA Ops:
  7.2 222.4 %copy-start = (bf16[768,256]{1,0:T(8,128)(2,1)S(1)}, bf16[768,256]{1,0:T(8,128)(2,1)}, u32[]{:S(2)}) copy-start(bf16[768,256]{1,0:T(8,128)(2,1)} %param.16) | copy-start | bytes 1179652
  7.2 101.7 %all-gather.3.cloned.1.call-start = ((), (), s32[]{:S(2)}) async-start(), calls=%async_computation.3 | async-start | bytes 11796480 | tf_op jit(solution)/shard_map/all_gather | solution.py:93
  7.2 8.6 %copy-start.21 = (bf16[4,512,768]{2,1,0:T(8,128)(2,1)S(1)}, bf16[4,512,768]{2,1,0:T(8,128)(2,1)}, u32[]{:S(2)}) copy-start(bf16[4,512,768]{2,1,0:T(8,128)(2,1)} %param.13) | copy-start | bytes 9437188
  7.9 8.2 %copy-start.22 = (s32[1,8]{1,0:T(1,128)S(1)}, s32[1,8]{1,0:T(1,128)}, u32[]{:S(2)}) copy-start(s32[1,8]{1,0:T(1,128)} %param.18) | copy-start | bytes 100
  7.9 8.7 %copy-start.30 = (s32[1,8]{1,0:T(1,128)S(1)}, s32[1,8]{1,0:T(1,128)}, u32[]{:S(2)}) copy-start(s32[1,8]{1,0:T(1,128)} %param.20) | copy-start | bytes 100
  7.9 199.2 %all-gather.5.cloned.1.call-start = ((), (), s32[]{:S(2)}) async-start(), calls=%async_computation.4 | async-start | bytes 11796480 | tf_op jit(solution)/shard_map/all_gather | solution.py:94
  9.5 222.6 %all-to-all-start = ((s32[8,1,1]{2,1,0:T(1,128)}), s32[8,1,1]{2,1,0:T(1,128)S(1)}, u32[]{:S(2)}, u32[]{:S(2)}) async-start(s32[8,1,1]{2,1,0:T(1,128)} %copy.36), calls=%async_computation | async-start | bytes 8192 | tf_op jit(solution)/shard_map/all_to_all | solution.py:112
  229.5 1.6 copy-start.1
  232.1 20.0 %all-to-all-start.1 = ((bf16[8,128,256]{2,1,0:T(8,128)(2,1)}), bf16[8,128,256]{2,1,0:T(8,128)(2,1)S(1)}, u32[]{:S(2)}, u32[]{:S(2)}) async-start(bf16[8,128,256]{2,1,0:T(8,128)(2,1)} %copy.38), calls=%async_computation.1 | async-start | bytes 1048576 | tf_op jit(solution)/shard_map/all_to_all | solution.py:111
  253.9 3.6 copy-start.8
  258.1 1.6 copy-start.3
  265.2 18.8 %all-to-all-start.2 = ((bf16[8,128,256]{1,2,0:T(8,128)(2,1)}), bf16[8,128,256]{1,2,0:T(8,128)(2,1)S(1)}, u32[]{:S(2)}, u32[]{:S(2)}) async-start(bf16[8,128,256]{1,2,0:T(8,128)(2,1)} %select_convert_fusion), calls=%async_computation.2 | async-start | bytes 1048576 | tf_op jit(solution)/shard_map/all_to_all | solution.py:127
  268.7 155.3 %all-reduce.3.cloned.1.call-start = ((), (), s32[]{:S(2)}) async-start(), calls=%async_computation.5 | async-start | bytes 5767168 | tf_op jit(solution)/shard_map/psum | solution.py:138
  268.8 2.5 copy-start.6
  268.8 2.5 copy-start.18
  271.3 1.5 copy-start.4
  271.3 1.5 copy-start.9
  272.9 11.2 %copy-start.20 = (bf16[1,8,128,128]{3,2,1,0:T(8,128)(2,1)S(1)}, bf16[1,8,128,128]{3,2,1,0:T(8,128)(2,1)}, u32[]{:S(2)}) copy-start(bf16[1,8,128,128]{3,2,1,0:T(8,128)(2,1)} %param.17) | copy-start | bytes 786436
  274.3 10.5 %copy-start.23 = (s32[1,8]{1,0:T(1,128)S(1)}, s32[1,8]{1,0:T(1,128)}, u32[]{:S(2)}) copy-start(s32[1,8]{1,0:T(1,128)} %param.18) | copy-start | bytes 100
  287.2 1.3 copy-start.29
  424.1 2.2 copy-start.16
  424.1 3.0 copy-start.15
  424.1 3.8 copy-start.14
  426.3 2.4 copy-start.13
  (14 other events, 15.2 us)
Sparse Core Ops, SparseCore 0:
  9.9 99.0 all-gather.2
  110.8 96.3 all-gather.4
  287.4 136.6 all-reduce.2
where the time goes:
time: 437 us; the launch traced here: 436 us
  waiting for transfers between devices  350 us (80%)
  matrix products  36.6 us (8%)
  local copies, waits for them, and re-layouts  15.3 us (4%)
  starting transfers between devices  14.5 us (3%)
  between operations  14.2 us (3%)
  other arithmetic  5.01 us (1%)
    psum x1, waiting for transfers between devices, on_device(): lax.psum((grad_proj, gradients[0], gradients[1], gradients[2], gradients[...  134 us
    all_gather x1, waiting for transfers between devices, on_device(): lax.all_gather(vit_down, 'section', axis=0, tiled=True)  98.2 us
    all_gather x1, waiting for transfers between devices, on_device(): lax.all_gather(vit_up, 'section', axis=0, tiled=True)  91.7 us
    dot_general x4, matrix products, encoder_layer(): jnp.dot(hidden, w_down, preferred_element_type=jnp.float32)  22.4 us
    all_to_all x1, waiting for transfers between devices, on_device(): lax.all_to_all(pieces, 'tile', split_axis=0, concat_axis=0, tiled=True)  15.1 us
    all_to_all x1, waiting for transfers between devices, on_device(): lax.all_to_all(grad_pieces, 'tile', split_axis=0, concat_axis=0, tiled=True)  9.74 us
    unnamed x69, local copies, waits for them, and re-layouts  9.72 us
  transfers between devices with their start and end apart: 6, of which 5 were waited for; matrix products, arithmetic and copies ran while one was open for 8% of the time, Pallas kernels for 0%

commit v1 on v0

v1 whole, which is shorter than its diff:
```python
import functools
import math

import jax
import jax.numpy as jnp
from jax import lax
from jax.experimental import pallas as pl
from jax.experimental.pallas import tpu as pltpu
from jax.sharding import PartitionSpec as P

eps = 1e-05
gelu_inner = math.sqrt(2.0 / math.pi)
gelu_cubic = 0.044715
vmem_bytes = 50 * 1024 * 1024


def gelu(value):
    inner = gelu_inner * (value + gelu_cubic * (value * value * value))
    half = 0.5 * value
    return half + half * jnp.tanh(inner)


def gelu_and_slope(value):
    square = value * value
    reach = jnp.tanh(gelu_inner * value * (1.0 + gelu_cubic * square))
    half = 0.5 * value
    up_to_one = 0.5 + 0.5 * reach
    slope = up_to_one + half * (1.0 - reach * reach) * (
        gelu_inner + (3.0 * gelu_inner * gelu_cubic) * square
    )
    return (value * up_to_one, slope)


def plain(left, right):
    return jnp.dot(left, right, preferred_element_type=jnp.float32)


def contract_rows(left, right):
    return lax.dot_general(
        left, right, (((0,), (0,)), ((), ())), preferred_element_type=jnp.float32
    )


def against_rows(left, right):
    return lax.dot_general(
        left, right, (((1,), (1,)), ((), ())), preferred_element_type=jnp.float32
    )


def encode_kernel(
    names,
    block_rows,
    place_ref,
    sources_ref,
    alive_ref,
    slot_of_ref,
    cams_ref,
    own_up_ref,
    own_down_ref,
    proj_ref,
    tiles_ref,
    *rest,
):
    parts = dict(zip(names, rest[: len(names)]))
    encoded_ref, pieces_ref = rest[len(names) : len(names) + 2]
    state, ups, downs, projected, state_sem, up_sems, down_sems = rest[len(names) + 2 :]
    section, core, zone = place_ref[0], place_ref[1], place_ref[2]
    layers, halves, half = ups.shape[:3]
    window = parts["x_up_window"].shape[0]
    missing = half - window

    load_state = pltpu.make_async_copy(cams_ref.at[section], state, state_sem)
    load_state.start()

    def pieces_of(relation, kind):
        found = []
        for side in ("", "other_"):
            at = core if side == "" else 1 - core
            name = f"{side}{relation}_{kind}"
            if name in parts:
                found.append((parts[name], at, 0, half))
            else:
                found.append((parts[name + "_window"], at, zone * missing, window))
                found.append((parts[name + "_missing"], at, (1 - zone) * window, missing))
        return found

    for layer in range(layers):
        for number, relation in enumerate(("own", "x", "y", "d")):

            @pl.when(jnp.bitwise_xor(section, layer) == number)
            def load(layer=layer, relation=relation):
                if relation == "own":
                    for at in range(halves):
                        pltpu.make_async_copy(
                            own_up_ref.at[:, pl.ds(at * half, half)],
                            ups.at[layer, at],
                            up_sems.at[layer],
                        ).start()
                        pltpu.make_async_copy(
                            own_down_ref.at[pl.ds(at * half, half)],
                            downs.at[layer, at],
                            down_sems.at[layer],
                        ).start()
                    return
                for kind, held, sems in (("up", ups, up_sems), ("down", downs, down_sems)):
                    for ref, at, first, count in pieces_of(relation, kind):
                        start = first if isinstance(first, int) else pl.multiple_of(first, 16)
                        pltpu.make_async_copy(
                            ref, held.at[layer, at, pl.ds(start, count)], sems.at[layer]
                        ).start()

    load_state.wait()
    for layer in range(layers):
        widened = state[...].astype(jnp.float32)
        scaling = lax.rsqrt(jnp.mean(widened * widened, axis=-1, keepdims=True) + eps)
        normed = (widened * scaling).astype(jnp.bfloat16)
        pltpu.make_async_copy(ups.at[layer], ups.at[layer], up_sems.at[layer]).wait()
        pltpu.make_async_copy(downs.at[layer], downs.at[layer], down_sems.at[layer]).wait()
        total = widened
        for at in range(halves):
            for first in range(0, half, half // 2):
                columns = pl.ds(first, half // 2)
                hidden = gelu(plain(normed, ups[layer, at, :, columns])).astype(jnp.bfloat16)
                total = total + plain(hidden, downs[layer, at, columns])
        state[...] = total.astype(jnp.bfloat16)
    encoded_ref[...] = state[...]
    projected[...] = plain(state[...], proj_ref[...]).astype(jnp.bfloat16)

    def slot(number, carry):
        first = pl.multiple_of(sources_ref[number] * block_rows, block_rows)
        piece = plain(tiles_ref[number], projected[pl.ds(first, block_rows)])
        piece = piece * alive_ref[number].astype(jnp.float32)
        pieces_ref[slot_of_ref[number]] = piece.astype(jnp.bfloat16)
        return carry

    lax.fori_loop(0, tiles_ref.shape[0], slot, 0, unroll=tiles_ref.shape[0] <= 8)


def encode(place, sources, alive, slot_of, cams, own_up, own_down, proj, tiles, parts):
    names = tuple(parts)
    tokens, width = cams.shape[1:]
    hidden = own_up.shape[1]
    layers = cams.shape[0]
    half = hidden // 2
    slots, block_rows = tiles.shape[:2]
    channels = proj.shape[1]
    smem = pl.BlockSpec(memory_space=pltpu.SMEM)
    vmem = pl.BlockSpec(memory_space=pltpu.VMEM)
    hbm = pl.BlockSpec(memory_space=pl.ANY)
    return pl.pallas_call(
        functools.partial(encode_kernel, names, block_rows),
        out_shape=(
            jax.ShapeDtypeStruct((tokens, width), jnp.bfloat16),
            jax.ShapeDtypeStruct((slots, block_rows, channels), jnp.bfloat16),
        ),
        in_specs=[smem] * 4 + [hbm] * 3 + [vmem] * 2 + [hbm] * len(names),
        out_specs=(vmem, vmem),
        scratch_shapes=[
            pltpu.VMEM((tokens, width), jnp.bfloat16),
            pltpu.VMEM((layers, 2, width, half), jnp.bfloat16),
            pltpu.VMEM((layers, 2, half, width), jnp.bfloat16),
            pltpu.VMEM((tokens, channels), jnp.bfloat16),
            pltpu.SemaphoreType.DMA,
            pltpu.SemaphoreType.DMA((layers,)),
            pltpu.SemaphoreType.DMA((layers,)),
        ],
        compiler_params=pltpu.CompilerParams(vmem_limit_bytes=vmem_bytes),
        name="encode",
    )(place, sources, alive, slot_of, cams, own_up, own_down, proj, tiles, *parts.values())


def heads_kernel(
    counts,
    scale_factor,
    targets_ref,
    render_up_ref,
    render_down_ref,
    decode_up_ref,
    decode_down_ref,
    pred_grad_ref,
    *rest,
):
    arrived = rest[: len(counts)]
    prediction_ref, gradients_ref = rest[len(counts) : len(counts) + 2]
    returns = rest[len(counts) + 2 : 2 * len(counts) + 2]
    (grid,) = rest[2 * len(counts) + 2 :]
    block_rows = arrived[0].shape[1]
    rows = grid.shape[0]

    grid[...] = jnp.zeros_like(grid)
    number = 0
    for ref, count in zip(arrived, counts):

        def add(at, carry, ref=ref, number=number):
            first = pl.multiple_of(targets_ref[number + at] * block_rows, block_rows)
            grid[pl.ds(first, block_rows)] += ref[at].astype(jnp.float32)
            return carry

        lax.fori_loop(0, count, add, 0, unroll=count <= 8)
        number += count

    weights = ((render_up_ref, render_down_ref), (decode_up_ref, decode_down_ref))
    state = grid[...]
    stored = []
    for w_up, w_down in weights:
        scaling = lax.rsqrt(jnp.mean(state * state, axis=-1, keepdims=True) + eps)
        normed = (state * scaling).astype(jnp.bfloat16)
        value, slope = gelu_and_slope(plain(normed, w_up[...]))
        hidden = value.astype(jnp.bfloat16)
        stored.append((state, scaling, normed, slope, hidden))
        state = state + plain(hidden, w_down[...])
    prediction_ref[...] = state.astype(jnp.bfloat16)

    grad_state = pred_grad_ref[...].astype(jnp.float32) * scale_factor
    width = gradients_ref.shape[-1]
    for block in (1, 0):
        state, scaling, normed, slope, hidden = stored[block]
        w_up, w_down = weights[block]
        rounded = grad_state.astype(jnp.bfloat16)
        grad_down = contract_rows(hidden, rounded).astype(jnp.bfloat16)
        grad_pre = (against_rows(rounded, w_down[...]) * slope).astype(jnp.bfloat16)
        grad_up = contract_rows(normed, grad_pre).astype(jnp.bfloat16)
        gradients_ref[4 * block] = grad_up[:, :width]
        gradients_ref[4 * block + 1] = grad_up[:, width:]
        gradients_ref[4 * block + 2] = grad_down[:width]
        gradients_ref[4 * block + 3] = grad_down[width:]
        grad_normed = against_rows(grad_pre, w_up[...])
        unit_rows = state * scaling
        grad_state = grad_state + scaling * (
            grad_normed - unit_rows * jnp.mean(grad_normed * unit_rows, axis=-1, keepdims=True)
        )
    grid[...] = grad_state
    number = 0
    for ref, count in zip(returns, counts):

        def give(at, carry, ref=ref, number=number):
            first = pl.multiple_of(targets_ref[number + at] * block_rows, block_rows)
            ref[at] = grid[pl.ds(first, block_rows)].astype(jnp.bfloat16)
            return carry

        lax.fori_loop(0, count, give, 0, unroll=count <= 8)
        number += count


def heads(targets, weights, pred_grad, arrived, scale_factor):
    rows, channels = pred_grad.shape
    smem = pl.BlockSpec(memory_space=pltpu.SMEM)
    vmem = pl.BlockSpec(memory_space=pltpu.VMEM)
    counts = tuple(part.shape[0] for part in arrived)
    return pl.pallas_call(
        functools.partial(heads_kernel, counts, scale_factor),
        out_shape=(
            jax.ShapeDtypeStruct((rows, channels), jnp.bfloat16),
            jax.ShapeDtypeStruct((8, channels, channels), jnp.bfloat16),
        )
        + tuple(jax.ShapeDtypeStruct(part.shape, jnp.bfloat16) for part in arrived),
        in_specs=[smem] + [vmem] * (5 + len(arrived)),
        out_specs=(vmem,) * (2 + len(arrived)),
        scratch_shapes=[pltpu.VMEM((rows, channels), jnp.float32)],
        compiler_params=pltpu.CompilerParams(vmem_limit_bytes=vmem_bytes),
        name="heads",
    )(targets, *weights, pred_grad, *arrived)


def proj_grad_kernel(
    counts, order_ref, sources_ref, alive_ref, tiles_ref, encoded_ref, *rest
):
    returned = rest[: len(counts)]
    gradient_ref = rest[len(counts)]
    (rows,) = rest[len(counts) + 1 :]
    block_rows = tiles_ref.shape[1]
    rows[...] = jnp.zeros_like(rows)
    number = 0
    for ref, count in zip(returned, counts):

        def add(at, carry, ref=ref, number=number):
            slot = order_ref[number + at]
            first = pl.multiple_of(sources_ref[slot] * block_rows, block_rows)
            product = contract_rows(tiles_ref[slot], ref[at])
            rows[pl.ds(first, block_rows)] += product * alive_ref[slot].astype(jnp.float32)
            return carry

        lax.fori_loop(0, count, add, 0, unroll=count <= 8)
        number += count
    total = contract_rows(encoded_ref[...], rows[...].astype(jnp.bfloat16))
    gradient_ref[...] = total.astype(jnp.bfloat16).reshape(gradient_ref.shape)


def proj_grad(order, sources, alive, tiles, encoded, returned):
    tokens, width = encoded.shape
    channels = returned[0].shape[-1]
    smem = pl.BlockSpec(memory_space=pltpu.SMEM)
    vmem = pl.BlockSpec(memory_space=pltpu.VMEM)
    counts = tuple(part.shape[0] for part in returned)
    return pl.pallas_call(
        functools.partial(proj_grad_kernel, counts),
        out_shape=jax.ShapeDtypeStruct((8, width // 8, channels), jnp.bfloat16),
        in_specs=[smem] * 3 + [vmem] * (2 + len(returned)),
        out_specs=vmem,
        scratch_shapes=[pltpu.VMEM((tokens, channels), jnp.float32)],
        compiler_params=pltpu.CompilerParams(vmem_limit_bytes=vmem_bytes),
        name="proj_grad",
    )(order, sources, alive, tiles, encoded, *returned)


def to_section(array, flip):
    count = lax.axis_size("section")
    return lax.ppermute(array, "section", [(at, at ^ flip) for at in range(count)])


def to_tile(array, flip):
    count = lax.axis_size("tile")
    return lax.ppermute(array, "tile", [(at, at ^ flip) for at in range(count)])


def rows_from(array, first, count):
    return lax.dynamic_slice_in_dim(array, first, count, 0)


def gather_layers(own_up, own_down, core, zone):
    half = own_down.shape[0] // 2
    window = (half * 7 // 12 + 15) // 16 * 16
    missing = half - window
    shared = window - missing
    up = lax.dynamic_slice_in_dim(own_up, core * half, half, 1)
    down = lax.dynamic_slice_in_dim(own_down, core * half, half, 0)

    def swapped(array):
        return to_tile(rows_from(array, zone * shared, missing), 2)

    x_up = to_section(rows_from(up, zone * missing, window), 1)
    y_down = to_section(rows_from(down, zone * missing, window), 2)
    x_up, y_down, up, down = lax.optimization_barrier((x_up, y_down, up, down))
    d_down = to_section(y_down, 1)
    d_up = to_section(x_up, 2)
    parts = {
        "x_up_window": x_up,
        "y_down_window": y_down,
        "x_up_missing": swapped(x_up),
        "y_down_missing": swapped(y_down),
        "x_down": to_section(down, 1),
        "y_up": to_section(up, 2),
        "d_up_window": d_up,
        "d_down_window": d_down,
        "d_up_missing": swapped(d_up),
        "d_down_missing": swapped(d_down),
    }
    parts.update({"other_" + name: to_tile(part, 1) for name, part in parts.items()})
    return parts


def add_up(left, *others):
    total = left.astype(jnp.float32)
    for other in others:
        total = total + other.astype(jnp.float32)
    return total.astype(jnp.bfloat16)


def total_over_devices(array, section, core):
    count = lax.axis_size("section")
    chips = lax.axis_size("tile") // 2
    mine = rows_from(array, core * count, count)
    others = rows_from(array, (1 - core) * count, count)
    mine = add_up(mine, to_tile(others, 1))

    def pick(number):
        return lax.dynamic_index_in_dim(mine, number, 0, keepdims=False)

    share = add_up(
        pick(section), *[to_section(pick(section ^ flip), flip) for flip in (3, 1, 2)]
    )
    if chips == 4:
        share = add_up(share, *[to_tile(share, 2 * flip) for flip in (2, 3, 1)])
    else:
        groups = [[2 * chip + side for chip in range(chips)] for side in (0, 1)]
        share = lax.psum(share, "tile", axis_index_groups=groups)
    gathered = jnp.stack([share] + [to_section(share, flip) for flip in (1, 2, 3)])
    gathered = jnp.take(gathered, section ^ jnp.arange(count, dtype=jnp.int32), axis=0)
    swapped = to_tile(gathered, 1)
    first = jnp.where(core == 0, gathered, swapped)
    second = jnp.where(core == 0, swapped, gathered)
    return jnp.concatenate([first, second])


def on_device(
    cams,
    vit_up,
    vit_down,
    proj,
    frustum_tiles,
    src_block,
    dst_block,
    live,
    render_up,
    render_down,
    decode_up,
    decode_down,
    pred_grad,
):
    section = lax.axis_index("section").astype(jnp.int32)
    tile = lax.axis_index("tile").astype(jnp.int32)
    tile_count = lax.axis_size("tile")
    micro_count = cams.shape[0]
    core = tile % 2
    chip = tile // 2
    zone = chip % 2
    small = tile_count == 8
    slots = jnp.arange(tile_count, dtype=jnp.int32)
    if small:
        slot_of = (slots // 2 ^ chip) + 4 * ((slots ^ core) % 2)
        order = 2 * (slots // 2 ^ chip) + (slots % 2 ^ core)
    else:
        slot_of = slots
        order = slots

    all_targets = lax.all_gather(dst_block, "tile", axis=0, tiled=True)
    targets = jnp.take(jnp.take(all_targets, tile, axis=1), order)

    parts = gather_layers(vit_up[0], vit_down[0], core, zone)
    place = jnp.stack([section, core, zone])
    encoded, pieces = encode(
        place, src_block[0], live[0], slot_of, cams, vit_up[0], vit_down[0], proj,
        frustum_tiles[0], parts,
    )

    if small:
        crossed = to_tile(pieces[4:], 1)
        both = jnp.stack([pieces[:4], crossed], axis=1)
        far = {flip: to_tile(both[flip], 2 * flip) for flip in (2, 3, 1)}
        arrived = [both[0], far[1], far[2], far[3]]
    else:
        arrived = [lax.all_to_all(pieces, "tile", split_axis=0, concat_axis=0, tiled=True)]

    scale_factor = 1.0 / math.sqrt(micro_count * pred_grad.shape[1] * tile_count)
    weights = (render_up, render_down, decode_up, decode_down)
    prediction, gradients, *returns = heads(
        targets, weights, pred_grad[0], arrived, scale_factor
    )

    if small:
        back = {flip: to_tile(returns[flip], 2 * flip) for flip in (2, 3, 1)}
        back[0] = returns[0]
        returned = []
        for flip in range(4):
            returned += [back[flip][:1], to_tile(back[flip][1:], 1)]
    else:
        returned = [
            lax.all_to_all(returns[0], "tile", split_axis=0, concat_axis=0, tiled=True)
        ]
    head_total = total_over_devices(gradients, section, core).astype(jnp.float32)
    grad_proj = proj_grad(order, src_block[0], live[0], frustum_tiles[0], encoded, returned)
    proj_total = total_over_devices(grad_proj, section, core).astype(jnp.float32)

    def up_of(block):
        return jnp.concatenate([head_total[4 * block], head_total[4 * block + 1]], axis=1)

    def down_of(block):
        return jnp.concatenate([head_total[4 * block + 2], head_total[4 * block + 3]], axis=0)

    return (
        prediction[None],
        proj_total.reshape(proj.shape),
        up_of(0),
        down_of(0),
        up_of(1),
        down_of(1),
    )


def solution(mesh):
    placed = (
        P(None, "tile", None),
        P("section", None, None),
        P("section", None, None),
        P(),
        P("tile", None, None, None),
        P("tile", None),
        P("tile", None),
        P("tile", None),
        P(),
        P(),
        P(),
        P(),
        P("section", "tile", None),
    )
    return jax.shard_map(
        on_device,
        mesh=mesh,
        in_specs=placed,
        out_specs=(P("section", "tile", None), P(), P(), P(), P(), P()),
        check_vma=False,
    )
```

time: 437 us -> 210 us (0.48)
  waiting for transfers between devices: 350 us -> 99.5 us
  matrix products: 36.6 us -> 0 us
  starting transfers between devices: 14.5 us -> 50.9 us
  Pallas kernels: 0 us -> 27.1 us
  between operations: 14.2 us -> 1.21 us
  blocking collectives: 0 us -> 11.9 us
    all_gather x2 -> x0, waiting for transfers between devices: 190 us -> none  [the longest x1 98.2 us: on_device(): lax.all_gather(vit_down, 'section', axis=0, tiled=True)]
    psum x1 -> x0, waiting for transfers between devices: 134 us -> none  [on_device(): lax.psum((grad_proj, gradients[0], gradients[1], gradients[2], gradients[...]
    ppermute x0 -> x53, waiting for transfers between devices: none -> 99.5 us  [the longest x35 60.3 us: to_tile(): return lax.ppermute(array, 'tile', [(at, at ^ flip) for at in range(count)])]
    ppermute x0 -> x53, starting transfers between devices: none -> 50.9 us  [the longest x35 27.2 us: to_tile(): return lax.ppermute(array, 'tile', [(at, at ^ flip) for at in range(count)])]
    dot_general x22 -> x0, matrix products: 36.6 us -> none  [the longest x4 22.4 us: encoder_layer(): jnp.dot(hidden, w_down, preferred_element_type=jnp.float32)]
    pallas_call x0 -> x3, Pallas kernels: none -> 27.1 us  [the longest x1 21.1 us: encode(): pl.pallas_call(functools.partial(encode_kernel, names, block_rows), out_s...]
    all_to_all x3 -> x0, waiting for transfers between devices: 24.8 us -> none  [the longest x1 15.1 us: on_device(): lax.all_to_all(pieces, 'tile', split_axis=0, concat_axis=0, tiled=True)]
    all_to_all x3 -> x0, starting transfers between devices: 14.4 us -> none  [the longest x1 6.33 us: on_device(): lax.all_to_all(targets[:, None], 'tile', split_axis=0, concat_axis=0, til...]
  transfers between devices with their start and end apart: 6 -> 53, of which waited for: 5 -> 30; matrix products, arithmetic and copies ran while one was open for 8% -> 5% of each run, Pallas kernels for 0% -> 0%
where the time goes in v1:
time: 210 us
  waiting for transfers between devices  99.5 us (47%)
  starting transfers between devices  50.9 us (24%)
  Pallas kernels  27.1 us (13%)
  local copies, waits for them, and re-layouts  13.5 us (6%)
  blocking collectives  11.9 us (6%)
  other arithmetic  5.94 us (3%)
    ppermute x35, waiting for transfers between devices, to_tile(): return lax.ppermute(array, 'tile', [(at, at ^ flip) for at in range(count)])  60.3 us
    ppermute x18, waiting for transfers between devices, to_section(): lax.ppermute(array, 'section', [(at, at ^ flip) for at in range(count)])  39.2 us
    ppermute x35, starting transfers between devices, to_tile(): return lax.ppermute(array, 'tile', [(at, at ^ flip) for at in range(count)])  27.2 us
    ppermute x18, starting transfers between devices, to_section(): lax.ppermute(array, 'section', [(at, at ^ flip) for at in range(count)])  23.7 us
    pallas_call x1, Pallas kernels, encode(): pl.pallas_call(functools.partial(encode_kernel, names, block_rows), out_s...  21.1 us
    all_gather x1, blocking collectives, on_device(): all_targets = lax.all_gather(dst_block, 'tile', axis=0, tiled=True)  11.9 us
    dynamic_slice x8, local copies, waits for them, and re-layouts, rows_from(): return lax.dynamic_slice_in_dim(array, first, count, 0)  6.93 us
    pallas_call x1, Pallas kernels, heads(): pl.pallas_call(functools.partial(heads_kernel, counts, scale_factor), out...  4.67 us
  transfers between devices with their start and end apart: 53, of which 30 were waited for; matrix products, arithmetic and copies ran while one was open for 5% of the time, Pallas kernels for 0%

profile of v1, /device:TPU:0, one launch (start us, length us, event | category | flops | bytes accessed | tf_op | source)
XLA Modules:
  0.0 210.0 jit_solution(9978415119401625218)
XLA Ops:
  0.7 2.5 %dynamic-slice_bitcast_fusion.3 = bf16[448,768]{1,0:T(8,128)(2,1)} fusion(bf16[1,768,1536]{2,1,0:T(8,128)(2,1)} %param.14, s32[]{:T(128)S(6)} %select_n.188, s32[]{:T(128)S(6)} %select_n.190), kind=kLoop, calls=%fused_computation.8 | loop fusion | bytes 1376264 | tf_op jit(solution)/shard_map/dynamic_slice | solution.py:317
  3.2 2.9 %collective-permute-start = (bf16[448,768]{1,0:T(8,128)(2,1)}, bf16[448,768]{1,0:T(8,128)(2,1)S(1)}, u32[]{:S(2)}, u32[]{:S(2)}) collective-permute-start(bf16[448,768]{1,0:T(8,128)(2,1)} %dynamic-slice_bitcast_fusion.3), channel_id=1, source_target_pairs={{0,8},{8,0},{16,24},{24,16},{1,9},{9,1},{17,25},{25,17},{2,10},{10... | collective-permute-start | bytes 2064392 | tf_op jit(solution)/shard_map/ppermute | solution.py:308
  11.3 10.5 %collective-permute-done.rest_0_ = bf16[448,768]{1,0:T(8,128)(2,1)S(1)} collective-permute-done((bf16[448,768]{1,0:T(8,128)(2,1)}, bf16[448,768]{1,0:T(8,128)(2,1)S(1)}, u32[]{:S(2)}, u32[]{:S(2)}) %collective-permute-start) | collective-permute-done | bytes 688160 | tf_op jit(solution)/shard_map/ppermute | solution.py:308
  21.8 3.7 %collective-permute-done.1.rest_1_ = bf16[448,768]{1,0:T(8,128)(2,1)} collective-permute-done((bf16[448,768]{1,0:T(8,128)(2,1)}, bf16[448,768]{1,0:T(8,128)(2,1)}, u32[]{:S(2)}, u32[]{:S(2)}) %collective-permute-start.1) | collective-permute-done | bytes 688160 | tf_op jit(solution)/shard_map/ppermute | solution.py:308
  32.3 7.5 %collective-permute-done.2.rest_2_ = bf16[320,768]{1,0:T(8,128)(2,1)S(1)} collective-permute-done((bf16[320,768]{1,0:T(8,128)(2,1)S(1)}, bf16[320,768]{1,0:T(8,128)(2,1)S(1)}, u32[]{:S(2)}, u32[]{:S(2)}) %collective-permute-start.2) | collective-permute-done | bytes 491552 | tf_op jit(solution)/shard_map/ppermute | solution.py:313
  41.3 6.6 %collective-permute-done.3.rest_3_ = bf16[320,768]{1,0:T(8,128)(2,1)S(1)} collective-permute-done((bf16[320,768]{1,0:T(8,128)(2,1)S(1)}, bf16[320,768]{1,0:T(8,128)(2,1)S(1)}, u32[]{:S(2)}, u32[]{:S(2)}) %collective-permute-start.3) | collective-permute-done | bytes 491552 | tf_op jit(solution)/shard_map/ppermute | solution.py:313
  53.5 17.4 %collective-permute-done.4.rest_4_ = bf16[768,768]{1,0:T(8,128)(2,1)} collective-permute-done((bf16[768,768]{1,0:T(8,128)(2,1)S(1)}, bf16[768,768]{1,0:T(8,128)(2,1)}, u32[]{:S(2)}, u32[]{:S(2)}) %collective-permute-start.4) | collective-permute-done | bytes 1179680 | tf_op jit(solution)/shard_map/ppermute | solution.py:308
  74.2 11.6 %collective-permute-done.9.rest_9_ = bf16[320,768]{1,0:T(8,128)(2,1)S(1)} collective-permute-done((bf16[320,768]{1,0:T(8,128)(2,1)S(1)}, bf16[320,768]{1,0:T(8,128)(2,1)S(1)}, u32[]{:S(2)}, u32[]{:S(2)}) %collective-permute-start.9) | collective-permute-done | bytes 491552 | tf_op jit(solution)/shard_map/ppermute | solution.py:313
  89.8 21.1 %encode.1 = (bf16[512,768]{1,0:T(8,128)(2,1)}, bf16[8,128,256]{2,1,0:T(8,128)(2,1)}) custom-call(s32[3]{0:T(128)S(1)} %pad_add_fusion.place_ref, s32[8]{0:T(128)S(1)} %bitcast.82, s32[8]{0:T(128)S(1)} %bitcast.84, s32[8]{0:T(128)S(1)} %fusion.23.slot_of_ref, bf16[4,512,768]{2,1,0:T(8,128)(2,1)} %cams_ref.1, bf16[768,1536]{1,0:T(8,128)(2,1)} %bitcast.86, ...), custom_call_target="tpu_custom_call" | custom-call | tf_op jit(solution)/shard_map/encode/pallas_call | solution.py:150
  112.6 11.9 %all-gather = s32[8,1,8]{2,1,0:T(1,128)S(1)} all-gather(s32[1,1,8]{2,1,0:T(1,128)S(1)} %bitcast.97), channel_id=1, replica_groups=mesh['section'=4,'tile'=8] {'tile'}, dimensions={0}, use_global_device_ids=true | all-gather | bytes 288 | tf_op jit(solution)/shard_map/all_gather | solution.py:416
  125.7 4.3 %collective-permute-start.23 = (bf16[2,128,256]{2,1,0:T(8,128)(2,1)S(1)}, bf16[2,128,256]{2,1,0:T(8,128)(2,1)S(1)}, u32[]{:S(2)}, u32[]{:S(2)}) collective-permute-start(bf16[2,128,256]{2,1,0:T(8,128)(2,1)S(1)} %get-tuple-element.56), channel_id=1, source_target_pairs={{0,6},{1,7},{2,4},{3,5},{4,2},{5,3},{6,0},{7,1},{8,14},{9,15},{10,... | collective-permute-start | bytes 393224 | tf_op jit(solution)/shard_map/ppermute | solution.py:313
  130.0 2.5 %collective-permute-done.21.rest_1_ = bf16[2,128,256]{2,1,0:T(8,128)(2,1)S(1)} collective-permute-done((bf16[2,128,256]{2,1,0:T(8,128)(2,1)S(1)}, bf16[2,128,256]{2,1,0:T(8,128)(2,1)S(1)}, u32[]{:S(2)}, u32[]{:S(2)}) %collective-permute-start.21) | collective-permute-done | bytes 131104 | tf_op jit(solution)/shard_map/ppermute | solution.py:313
  132.5 6.1 %collective-permute-done.22.rest_2_ = bf16[2,128,256]{2,1,0:T(8,128)(2,1)S(1)} collective-permute-done((bf16[2,128,256]{2,1,0:T(8,128)(2,1)S(1)}, bf16[2,128,256]{2,1,0:T(8,128)(2,1)S(1)}, u32[]{:S(2)}, u32[]{:S(2)}) %collective-permute-start.22) | collective-permute-done | bytes 131104 | tf_op jit(solution)/shard_map/ppermute | solution.py:313
  138.6 4.7 %heads.1 = (bf16[640,256]{1,0:T(8,128)(2,1)}, bf16[8,256,256]{2,1,0:T(8,128)(2,1)S(1)}, bf16[2,128,256]{2,1,0:T(8,128)(2,1)S(1)}, bf16[2,128,256]{2,1,0:T(8,128)...) custom-call(s32[8]{0:T(128)S(1)} %get-tuple-element.41.targets_ref, ...), custom_call_target="tpu_custom_call" | custom-call | tf_op jit(solution)/shard_map/heads/pallas_call | solution.py:250
  143.3 2.7 %collective-permute-start.25 = (bf16[2,128,256]{2,1,0:T(8,128)(2,1)S(1)}, bf16[2,128,256]{2,1,0:T(8,128)(2,1)S(1)}, u32[]{:S(2)}, u32[]{:S(2)}) collective-permute-start(bf16[2,128,256]{2,1,0:T(8,128)(2,1)S(1)} %get-tuple-element.26), channel_id=1, source_target_pairs={{0,2},{1,3},{2,0},{3,1},{4,6},{5,7},{6,4},{7,5},{8,10},{9,11},{10,... | collective-permute-start | bytes 393224 | tf_op jit(solution)/shard_map/ppermute | solution.py:313
  146.2 2.4 %collective-permute-start.29 = (bf16[2,128,256]{2,1,0:T(8,128)(2,1)S(1)}, bf16[2,128,256]{2,1,0:T(8,128)(2,1)S(1)}, u32[]{:S(2)}, u32[]{:S(2)}) collective-permute-start(bf16[2,128,256]{2,1,0:T(8,128)(2,1)S(1)} %get-tuple-element.28), channel_id=1, source_target_pairs={{0,6},{1,7},{2,4},{3,5},{4,2},{5,3},{6,0},{7,1},{8,14},{9,15},{10,... | collective-permute-start | bytes 393224 | tf_op jit(solution)/shard_map/ppermute | solution.py:313
  150.1 8.4 %collective-permute-done.27 = bf16[2,128,256]{2,1,0:T(8,128)(2,1)S(1)} collective-permute-done((bf16[2,128,256]{2,1,0:T(8,128)(2,1)S(1)}, bf16[2,128,256]{2,1,0:T(8,128)(2,1)S(1)}, u32[]{:S(2)}, u32[]{:S(2)}) %collective-permute-start.27) | collective-permute-done | bytes 131104 | tf_op jit(solution)/shard_map/ppermute | solution.py:313
  164.1 2.4 %collective-permute-start.32 = (bf16[96,256]{1,0:T(8,128)(2,1)S(1)}, bf16[96,256]{1,0:T(8,128)(2,1)S(1)}, u32[]{:S(2)}, u32[]{:S(2)}) collective-permute-start(bf16[96,256]{1,0:T(8,128)(2,1)S(1)} %get-tuple-element.64), channel_id=1, source_target_pairs={{0,24},{8,16},{16,8},{24,0},{1,25},{9,17},{17,9},{25,1},{2,26},{10... | collective-permute-start | bytes 147464 | tf_op jit(solution)/shard_map/ppermute | solution.py:308
  169.4 2.8 %collective-permute-start.37 = (bf16[96,256]{1,0:T(8,128)(2,1)S(1)}, bf16[96,256]{1,0:T(8,128)(2,1)S(1)}, u32[]{:S(2)}, u32[]{:S(2)}) collective-permute-start(bf16[96,256]{1,0:T(8,128)(2,1)S(1)} %fusion.12), channel_id=1, source_target_pairs={{0,2},{1,3},{2,0},{3,1},{4,6},{5,7},{6,4},{7,5},{8,10},{9,11},{10,... | collective-permute-start | bytes 147464 | tf_op jit(solution)/shard_map/ppermute | solution.py:313
  179.1 2.5 %collective-permute-start.40 = (bf16[96,256]{1,0:T(8,128)(2,1)S(1)}, bf16[96,256]{1,0:T(8,128)(2,1)S(1)}, u32[]{:S(2)}, u32[]{:S(2)}) collective-permute-start(bf16[96,256]{1,0:T(8,128)(2,1)S(1)} %add_convert_fusion.3), channel_id=1, source_target_pairs={{0,24},{8,16},{16,8},{24,0},{1,25},{9,17},{17,9},{25,1},{2,26},{10... | collective-permute-start | bytes 147464 | tf_op jit(solution)/shard_map/ppermute | solution.py:308
  183.0 2.7 %collective-permute-start.48 = (bf16[256,256]{1,0:T(8,128)(2,1)S(1)}, bf16[256,256]{1,0:T(8,128)(2,1)S(1)}, u32[]{:S(2)}, u32[]{:S(2)}) collective-permute-start(bf16[256,256]{1,0:T(8,128)(2,1)S(1)} %fusion.2), channel_id=1, source_target_pairs={{0,2},{1,3},{2,0},{3,1},{4,6},{5,7},{6,4},{7,5},{8,10},{9,11},{10,... | collective-permute-start | bytes 393224 | tf_op jit(solution)/shard_map/ppermute | solution.py:313
  188.8 3.9 %collective-permute-done.47 = bf16[256,256]{1,0:T(8,128)(2,1)S(1)} collective-permute-done((bf16[256,256]{1,0:T(8,128)(2,1)S(1)}, bf16[256,256]{1,0:T(8,128)(2,1)S(1)}, u32[]{:S(2)}, u32[]{:S(2)}) %collective-permute-start.47) | collective-permute-done | bytes 131104 | tf_op jit(solution)/shard_map/ppermute | solution.py:313
  192.6 3.1 %collective-permute-done.46 = bf16[256,256]{1,0:T(8,128)(2,1)S(1)} collective-permute-done((bf16[256,256]{1,0:T(8,128)(2,1)S(1)}, bf16[256,256]{1,0:T(8,128)(2,1)S(1)}, u32[]{:S(2)}, u32[]{:S(2)}) %collective-permute-start.46) | collective-permute-done | bytes 131104 | tf_op jit(solution)/shard_map/ppermute | solution.py:313
  199.5 2.7 %collective-permute-done.51 = bf16[256,256]{1,0:T(8,128)(2,1)S(1)} collective-permute-done((bf16[256,256]{1,0:T(8,128)(2,1)S(1)}, bf16[256,256]{1,0:T(8,128)(2,1)S(1)}, u32[]{:S(2)}, u32[]{:S(2)}) %collective-permute-start.51) | collective-permute-done | bytes 131104 | tf_op jit(solution)/shard_map/ppermute | solution.py:308
  (169 shorter events, 62.0 us)
Async XLA Ops:
  3.2 18.5 %collective-permute-start = (bf16[448,768]{1,0:T(8,128)(2,1)}, bf16[448,768]{1,0:T(8,128)(2,1)S(1)}, u32[]{:S(2)}, u32[]{:S(2)}) collective-permute-start(bf16[448,768]{1,0:T(8,128)(2,1)} %dynamic-slice_bitcast_fusion.3), channel_id=1, source_target_pairs={{0,8},{8,0},{16,24},{24,16},{1,9},{9,1},{17,25},{25,17},{2,10},{10... | collective-permute-start | bytes 2064392 | tf_op jit(solution)/shard_map/ppermute | solution.py:308
  8.3 17.2 %collective-permute-start.1 = (bf16[448,768]{1,0:T(8,128)(2,1)}, bf16[448,768]{1,0:T(8,128)(2,1)}, u32[]{:S(2)}, u32[]{:S(2)}) collective-permute-start(bf16[448,768]{1,0:T(8,128)(2,1)} %dynamic-slice_bitcast_fusion.2), channel_id=1, source_target_pairs={{0,16},{8,24},{16,0},{24,8},{1,17},{9,25},{17,1},{25,9},{2,18},{10... | collective-permute-start | bytes 2064392 | tf_op jit(solution)/shard_map/ppermute | solution.py:308
  25.5 14.2 %collective-permute-start.2 = (bf16[320,768]{1,0:T(8,128)(2,1)S(1)}, bf16[320,768]{1,0:T(8,128)(2,1)S(1)}, u32[]{:S(2)}, u32[]{:S(2)}) collective-permute-start(bf16[320,768]{1,0:T(8,128)(2,1)S(1)} %constant_dynamic-slice_fusion.6), channel_id=1, source_target_pairs={{0,2},{1,3},{2,0},{3,1},{4,6},{5,7},{6,4},{7,5},{8,10},{9,11},{10,... | collective-permute-start | bytes 1474568 | tf_op jit(solution)/shard_map/ppermute | solution.py:313
  28.2 19.6 %collective-permute-start.3 = (bf16[320,768]{1,0:T(8,128)(2,1)S(1)}, bf16[320,768]{1,0:T(8,128)(2,1)S(1)}, u32[]{:S(2)}, u32[]{:S(2)}) collective-permute-start(bf16[320,768]{1,0:T(8,128)(2,1)S(1)} %constant_dynamic-slice_fusion.5), channel_id=1, source_target_pairs={{0,2},{1,3},{2,0},{3,1},{4,6},{5,7},{6,4},{7,5},{8,10},{9,11},{10,... | collective-permute-start | bytes 1474568 | tf_op jit(solution)/shard_map/ppermute | solution.py:313
  28.8 19.1 %collective-permute-start.6 = (bf16[448,768]{1,0:T(8,128)(2,1)S(1)}, bf16[448,768]{1,0:T(8,128)(2,1)S(1)}, u32[]{:S(2)}, u32[]{:S(2)}) collective-permute-start(bf16[448,768]{1,0:T(8,128)(2,1)S(1)} %collective-permute-done.rest_0_), channel_id=1, source_target_pairs={{0,16},{8,24},{16,0},{24,8},{1,17},{9,25},{17,1},{25,9},{2,18},{10... | collective-permute-start | bytes 2064392 | tf_op jit(solution)/shard_map/ppermute | solution.py:308
  30.3 18.7 %collective-permute-start.7 = (bf16[448,768]{1,0:T(8,128)(2,1)}, bf16[448,768]{1,0:T(8,128)(2,1)}, u32[]{:S(2)}, u32[]{:S(2)}) collective-permute-start(bf16[448,768]{1,0:T(8,128)(2,1)} %collective-permute-done.1.rest_1_), channel_id=1, source_target_pairs={{0,8},{8,0},{16,24},{24,16},{1,9},{9,1},{17,25},{25,17},{2,10},{10... | collective-permute-start | bytes 2064392 | tf_op jit(solution)/shard_map/ppermute | solution.py:308
  30.8 40.2 %collective-permute-start.4 = (bf16[768,768]{1,0:T(8,128)(2,1)S(1)}, bf16[768,768]{1,0:T(8,128)(2,1)}, u32[]{:S(2)}, u32[]{:S(2)}) collective-permute-start(bf16[768,768]{1,0:T(8,128)(2,1)S(1)} %get-tuple-element.20), channel_id=1, source_target_pairs={{0,8},{8,0},{16,24},{24,16},{1,9},{9,1},{17,25},{25,17},{2,10},{10... | collective-permute-start | bytes 3538952 | tf_op jit(solution)/shard_map/ppermute | solution.py:308
  39.8 31.2 %collective-permute-start.5 = (bf16[768,768]{1,0:T(8,128)(2,1)S(1)}, bf16[768,768]{1,0:T(8,128)(2,1)}, u32[]{:S(2)}, u32[]{:S(2)}) collective-permute-start(bf16[768,768]{1,0:T(8,128)(2,1)S(1)} %get-tuple-element.21), channel_id=1, source_target_pairs={{0,16},{8,24},{16,0},{24,8},{1,17},{9,25},{17,1},{25,9},{2,18},{10... | collective-permute-start | bytes 3538952 | tf_op jit(solution)/shard_map/ppermute | solution.py:308
  50.2 22.3 %collective-permute-start.13 = (bf16[320,768]{1,0:T(8,128)(2,1)S(1)}, bf16[320,768]{1,0:T(8,128)(2,1)S(1)}, u32[]{:S(2)}, u32[]{:S(2)}) collective-permute-start(bf16[320,768]{1,0:T(8,128)(2,1)S(1)} %collective-permute-done.3.rest_3_), channel_id=1, source_target_pairs={{0,1},{1,0},{2,3},{3,2},{4,5},{5,4},{6,7},{7,6},{8,9},{9,8},{10,11... | collective-permute-start | bytes 1474568 | tf_op jit(solution)/shard_map/ppermute | solution.py:313
  52.0 22.2 %collective-permute-start.8 = (bf16[320,768]{1,0:T(8,128)(2,1)S(1)}, bf16[320,768]{1,0:T(8,128)(2,1)S(1)}, u32[]{:S(2)}, u32[]{:S(2)}) collective-permute-start(bf16[320,768]{1,0:T(8,128)(2,1)S(1)} %constant_dynamic-slice_fusion.4), channel_id=1, source_target_pairs={{0,2},{1,3},{2,0},{3,1},{4,6},{5,7},{6,4},{7,5},{8,10},{9,11},{10,... | collective-permute-start | bytes 1474568 | tf_op jit(solution)/shard_map/ppermute | solution.py:313
  53.5 32.2 %collective-permute-start.16 = (bf16[448,768]{1,0:T(8,128)(2,1)S(1)}, bf16[448,768]{1,0:T(8,128)(2,1)S(1)}, u32[]{:S(2)}, u32[]{:S(2)}) collective-permute-start(bf16[448,768]{1,0:T(8,128)(2,1)S(1)} %collective-permute-done.6.rest_6_), channel_id=1, source_target_pairs={{0,1},{1,0},{2,3},{3,2},{4,5},{5,4},{6,7},{7,6},{8,9},{9,8},{10,11... | collective-permute-start | bytes 2064392 | tf_op jit(solution)/shard_map/ppermute | solution.py:313
  71.0 17.8 %collective-permute-start.14 = (bf16[768,768]{1,0:T(8,128)(2,1)}, bf16[768,768]{1,0:T(8,128)(2,1)}, u32[]{:S(2)}, u32[]{:S(2)}) collective-permute-start(bf16[768,768]{1,0:T(8,128)(2,1)} %collective-permute-done.4.rest_4_), channel_id=1, source_target_pairs={{0,1},{1,0},{2,3},{3,2},{4,5},{5,4},{6,7},{7,6},{8,9},{9,8},{10,11... | collective-permute-start | bytes 3538952 | tf_op jit(solution)/shard_map/ppermute | solution.py:313
  71.0 17.8 %collective-permute-start.15 = (bf16[768,768]{1,0:T(8,128)(2,1)}, bf16[768,768]{1,0:T(8,128)(2,1)}, u32[]{:S(2)}, u32[]{:S(2)}) collective-permute-start(bf16[768,768]{1,0:T(8,128)(2,1)} %collective-permute-done.5.rest_5_), channel_id=1, source_target_pairs={{0,1},{1,0},{2,3},{3,2},{4,5},{5,4},{6,7},{7,6},{8,9},{9,8},{10,11... | collective-permute-start | bytes 3538952 | tf_op jit(solution)/shard_map/ppermute | solution.py:313
  72.6 13.2 %collective-permute-start.9 = (bf16[320,768]{1,0:T(8,128)(2,1)S(1)}, bf16[320,768]{1,0:T(8,128)(2,1)S(1)}, u32[]{:S(2)}, u32[]{:S(2)}) collective-permute-start(bf16[320,768]{1,0:T(8,128)(2,1)S(1)} %constant_dynamic-slice_fusion.3), channel_id=1, source_target_pairs={{0,2},{1,3},{2,0},{3,1},{4,6},{5,7},{6,4},{7,5},{8,10},{9,11},{10,... | collective-permute-start | bytes 1474568 | tf_op jit(solution)/shard_map/ppermute | solution.py:313
  74.2 13.1 %collective-permute-start.17 = (bf16[448,768]{1,0:T(8,128)(2,1)}, bf16[448,768]{1,0:T(8,128)(2,1)}, u32[]{:S(2)}, u32[]{:S(2)}) collective-permute-start(bf16[448,768]{1,0:T(8,128)(2,1)} %collective-permute-done.7.rest_7_), channel_id=1, source_target_pairs={{0,1},{1,0},{2,3},{3,2},{4,5},{5,4},{6,7},{7,6},{8,9},{9,8},{10,11... | collective-permute-start | bytes 2064392 | tf_op jit(solution)/shard_map/ppermute | solution.py:313
  112.2 13.3 %collective-permute-start.20 = (bf16[4,128,256]{2,1,0:T(8,128)(2,1)S(1)}, bf16[4,128,256]{2,1,0:T(8,128)(2,1)S(1)}, u32[]{:S(2)}, u32[]{:S(2)}) collective-permute-start(bf16[4,128,256]{2,1,0:T(8,128)(2,1)S(1)} %get-tuple-element.60), channel_id=1, source_target_pairs={{0,1},{1,0},{2,3},{3,2},{4,5},{5,4},{6,7},{7,6},{8,9},{9,8},{10,11... | collective-permute-start | bytes 786440 | tf_op jit(solution)/shard_map/ppermute | solution.py:313
  125.6 12.9 %collective-permute-start.22 = (bf16[2,128,256]{2,1,0:T(8,128)(2,1)S(1)}, bf16[2,128,256]{2,1,0:T(8,128)(2,1)S(1)}, u32[]{:S(2)}, u32[]{:S(2)}) collective-permute-start(bf16[2,128,256]{2,1,0:T(8,128)(2,1)S(1)} %get-tuple-element.59), channel_id=1, source_target_pairs={{0,4},{1,5},{2,6},{3,7},{4,0},{5,1},{6,2},{7,3},{8,12},{9,13},{10,... | collective-permute-start | bytes 393224 | tf_op jit(solution)/shard_map/ppermute | solution.py:313
  125.7 12.9 %collective-permute-start.23 = (bf16[2,128,256]{2,1,0:T(8,128)(2,1)S(1)}, bf16[2,128,256]{2,1,0:T(8,128)(2,1)S(1)}, u32[]{:S(2)}, u32[]{:S(2)}) collective-permute-start(bf16[2,128,256]{2,1,0:T(8,128)(2,1)S(1)} %get-tuple-element.56), channel_id=1, source_target_pairs={{0,6},{1,7},{2,4},{3,5},{4,2},{5,3},{6,0},{7,1},{8,14},{9,15},{10,... | collective-permute-start | bytes 393224 | tf_op jit(solution)/shard_map/ppermute | solution.py:313
  146.1 13.1 %collective-permute-start.24 = (bf16[1,128,256]{2,1,0:T(8,128)(2,1)S(1)}, bf16[1,128,256]{2,1,0:T(8,128)(2,1)S(1)}, u32[]{:S(2)}, u32[]{:S(2)}) collective-permute-start(bf16[1,128,256]{2,1,0:T(8,128)(2,1)S(1)} %get-tuple-element.73), channel_id=1, source_target_pairs={{0,1},{1,0},{2,3},{3,2},{4,5},{5,4},{6,7},{7,6},{8,9},{9,8},{10,11... | collective-permute-start | bytes 196616 | tf_op jit(solution)/shard_map/ppermute | solution.py:313
  146.1 12.4 %collective-permute-start.27 = (bf16[2,128,256]{2,1,0:T(8,128)(2,1)S(1)}, bf16[2,128,256]{2,1,0:T(8,128)(2,1)S(1)}, u32[]{:S(2)}, u32[]{:S(2)}) collective-permute-start(bf16[2,128,256]{2,1,0:T(8,128)(2,1)S(1)} %get-tuple-element.27), channel_id=1, source_target_pairs={{0,4},{1,5},{2,6},{3,7},{4,0},{5,1},{6,2},{7,3},{8,12},{9,13},{10,... | collective-permute-start | bytes 393224 | tf_op jit(solution)/shard_map/ppermute | solution.py:313
  146.2 12.4 %collective-permute-start.29 = (bf16[2,128,256]{2,1,0:T(8,128)(2,1)S(1)}, bf16[2,128,256]{2,1,0:T(8,128)(2,1)S(1)}, u32[]{:S(2)}, u32[]{:S(2)}) collective-permute-start(bf16[2,128,256]{2,1,0:T(8,128)(2,1)S(1)} %get-tuple-element.28), channel_id=1, source_target_pairs={{0,6},{1,7},{2,4},{3,5},{4,2},{5,3},{6,0},{7,1},{8,14},{9,15},{10,... | collective-permute-start | bytes 393224 | tf_op jit(solution)/shard_map/ppermute | solution.py:313
  150.0 9.2 %collective-permute-start.26 = (bf16[1,128,256]{2,1,0:T(8,128)(2,1)S(1)}, bf16[1,128,256]{2,1,0:T(8,128)(2,1)S(1)}, u32[]{:S(2)}, u32[]{:S(2)}) collective-permute-start(bf16[1,128,256]{2,1,0:T(8,128)(2,1)S(1)} %get-tuple-element.71), channel_id=1, source_target_pairs={{0,1},{1,0},{2,3},{3,2},{4,5},{5,4},{6,7},{7,6},{8,9},{9,8},{10,11... | collective-permute-start | bytes 196616 | tf_op jit(solution)/shard_map/ppermute | solution.py:313
  161.9 11.8 %collective-permute-start.42 = (bf16[4,256,256]{2,1,0:T(8,128)(2,1)S(1)}, bf16[4,256,256]{2,1,0:T(8,128)(2,1)S(1)}, u32[]{:S(2)}, u32[]{:S(2)}) collective-permute-start(bf16[4,256,256]{2,1,0:T(8,128)(2,1)S(1)} %constant_dynamic-slice_fusion.1), channel_id=1, source_target_pairs={{0,1},{1,0},{2,3},{3,2},{4,5},{5,4},{6,7},{7,6},{8,9},{9,8},{10,11... | collective-permute-start | bytes 1572872 | tf_op jit(solution)/shard_map/ppermute | solution.py:313
  187.3 8.4 %collective-permute-start.46 = (bf16[256,256]{1,0:T(8,128)(2,1)S(1)}, bf16[256,256]{1,0:T(8,128)(2,1)S(1)}, u32[]{:S(2)}, u32[]{:S(2)}) collective-permute-start(bf16[256,256]{1,0:T(8,128)(2,1)S(1)} %fusion.2), channel_id=1, source_target_pairs={{0,4},{1,5},{2,6},{3,7},{4,0},{5,1},{6,2},{7,3},{8,12},{9,13},{10,... | collective-permute-start | bytes 393224 | tf_op jit(solution)/shard_map/ppermute | solution.py:313
  (46 other events, 718.3 us)

commit v2 on v1

v2 whole, which is shorter than its diff:
```python
import functools
import math

import jax
import jax.numpy as jnp
from jax import lax
from jax.experimental import pallas as pl
from jax.experimental.pallas import tpu as pltpu
from jax.sharding import PartitionSpec as P

eps = 1e-05
gelu_inner = math.sqrt(2.0 / math.pi)
gelu_cubic = 0.044715
mebibyte = 1024 * 1024


def gelu(value):
    inner = gelu_inner * (value + gelu_cubic * (value * value * value))
    half = 0.5 * value
    return half + half * jnp.tanh(inner)


def gelu_and_slope(value):
    square = value * value
    reach = jnp.tanh(gelu_inner * value * (1.0 + gelu_cubic * square))
    half = 0.5 * value
    up_to_one = 0.5 + 0.5 * reach
    slope = up_to_one + half * (1.0 - reach * reach) * (
        gelu_inner + (3.0 * gelu_inner * gelu_cubic) * square
    )
    return (value * up_to_one, slope)


def plain(left, right):
    return jnp.dot(left, right, preferred_element_type=jnp.float32)


def contract_rows(left, right):
    return lax.dot_general(
        left, right, (((0,), (0,)), ((), ())), preferred_element_type=jnp.float32
    )


def against_rows(left, right):
    return lax.dot_general(
        left, right, (((1,), (1,)), ((), ())), preferred_element_type=jnp.float32
    )


def position():
    tile = lax.axis_index("tile")
    return (lax.axis_index("section"), tile, tile % 2, tile // 2 % 2)


def tile_of(number, tile, tiles):
    if tiles != 8:
        return number
    chip = jnp.bitwise_xor(number // 2, tile // 2)
    return 2 * chip + jnp.bitwise_xor(number % 2, tile % 2)


def encode_kernel(
    names,
    counts,
    sources_ref,
    alive_ref,
    table_ref,
    cams_ref,
    own_up_ref,
    own_down_ref,
    proj_ref,
    tiles_ref,
    *rest,
):
    parts = dict(zip(names, rest[: len(names)]))
    rest = rest[len(names) :]
    encoded_ref, targets_ref = rest[:2]
    pieces = rest[2 : 2 + len(counts)]
    state, ups, downs, projected, state_sem, up_sems, down_sems = rest[2 + len(counts) :]
    section, tile, core, zone = position()
    layers, halves, half = ups.shape[:3]
    alone = parts["x_up_own"].shape[0]
    shared = half - 2 * alone
    block_rows = tiles_ref.shape[1]

    load_state = pltpu.make_async_copy(cams_ref.at[section], state, state_sem)
    load_state.start()

    def at_own(kind, name, far, number):
        return (
            (kind, name, 0, alone, pl.multiple_of(zone * alone, 16)),
            (kind, far, number * alone, alone, pl.multiple_of((1 - zone) * alone, 16)),
        )

    where = {
        "x": (
            *at_own("up", "x_up_own", "first_far", 0),
            ("down", "x_pack", 0, half, 0),
            ("up", "x_pack", half, shared, 2 * alone),
        ),
        "y": (
            *at_own("down", "y_down_own", "first_far", 1),
            ("up", "y_pack", 0, half, 0),
            ("down", "y_pack", half, shared, 2 * alone),
        ),
        "d": (
            *at_own("up", "d_up_own", "second_far", 0),
            *at_own("down", "d_down_own", "second_far", 1),
            ("up", "d_shared", 0, shared, 2 * alone),
            ("down", "d_shared", shared, shared, 2 * alone),
        ),
    }
    held = {"up": (ups, up_sems), "down": (downs, down_sems)}

    for layer in range(layers):
        for number, relation in enumerate(("own", "x", "y", "d")):

            @pl.when(jnp.bitwise_xor(section, layer) == number)
            def load(layer=layer, relation=relation):
                if relation == "own":
                    for at in range(halves):
                        pltpu.make_async_copy(
                            own_up_ref.at[:, pl.ds(at * half, half)],
                            ups.at[layer, at],
                            up_sems.at[layer],
                        ).start()
                        pltpu.make_async_copy(
                            own_down_ref.at[pl.ds(at * half, half)],
                            downs.at[layer, at],
                            down_sems.at[layer],
                        ).start()
                    return
                for side, at in (("", core), ("other_", 1 - core)):
                    for kind, name, first, count, to in where[relation]:
                        kept, sems = held[kind]
                        pltpu.make_async_copy(
                            parts[side + name].at[pl.ds(first, count)],
                            kept.at[layer, at, pl.ds(to, count)],
                            sems.at[layer],
                        ).start()

    load_state.wait()
    for layer in range(layers):
        widened = state[...].astype(jnp.float32)
        scaling = lax.rsqrt(jnp.mean(widened * widened, axis=-1, keepdims=True) + eps)
        normed = (widened * scaling).astype(jnp.bfloat16)
        pltpu.make_async_copy(ups.at[layer], ups.at[layer], up_sems.at[layer]).wait()
        pltpu.make_async_copy(downs.at[layer], downs.at[layer], down_sems.at[layer]).wait()
        total = widened
        for at in range(halves):
            hidden = gelu(plain(normed, ups[layer, at])).astype(jnp.bfloat16)
            total = total + plain(hidden, downs[layer, at])
        state[...] = total.astype(jnp.bfloat16)
    encoded_ref[...] = state[...]
    projected[...] = plain(state[...], proj_ref[...]).astype(jnp.bfloat16)

    number = 0
    for ref, count in zip(pieces, counts):

        def slot(at, carry, ref=ref, number=number):
            tile_at = tile_of(number + at, tile, tiles_ref.shape[0])
            first = pl.multiple_of(sources_ref[tile_at] * block_rows, block_rows)
            piece = plain(tiles_ref[tile_at], projected[pl.ds(first, block_rows)])
            piece = piece * alive_ref[tile_at].astype(jnp.float32)
            ref[at] = piece.astype(jnp.bfloat16)
            targets_ref[number + at] = table_ref[jnp.bitwise_xor(tile_at, tile), tile]
            return carry

        lax.fori_loop(0, count, slot, 0, unroll=count <= 8)
        number += count


def encode(
    sources, alive, table, cams, own_up, own_down, proj, tiles, parts, counts
):
    names = tuple(parts)
    tokens, width = cams.shape[1:]
    hidden = own_up.shape[1]
    layers = cams.shape[0]
    half = hidden // 2
    block_rows = tiles.shape[1]
    channels = proj.shape[1]
    smem = pl.BlockSpec(memory_space=pltpu.SMEM)
    vmem = pl.BlockSpec(memory_space=pltpu.VMEM)
    hbm = pl.BlockSpec(memory_space=pl.ANY)
    return pl.pallas_call(
        functools.partial(encode_kernel, names, counts),
        out_shape=(
            jax.ShapeDtypeStruct((tokens, width), jnp.bfloat16),
            jax.ShapeDtypeStruct(sources.shape, jnp.int32),
        )
        + tuple(
            jax.ShapeDtypeStruct((count, block_rows, channels), jnp.bfloat16) for count in counts
        ),
        in_specs=[smem] * 3 + [hbm] * 3 + [vmem] * 2 + [hbm] * len(names),
        out_specs=(vmem, smem) + (vmem,) * len(counts),
        scratch_shapes=[
            pltpu.VMEM((tokens, width), jnp.bfloat16),
            pltpu.VMEM((layers, 2, width, half), jnp.bfloat16),
            pltpu.VMEM((layers, 2, half, width), jnp.bfloat16),
            pltpu.VMEM((tokens, channels), jnp.bfloat16),
            pltpu.SemaphoreType.DMA,
            pltpu.SemaphoreType.DMA((layers,)),
            pltpu.SemaphoreType.DMA((layers,)),
        ],
        compiler_params=pltpu.CompilerParams(vmem_limit_bytes=50 * mebibyte),
        name="encode",
    )(sources, alive, table, cams, own_up, own_down, proj, tiles, *parts.values())


def heads_kernel(
    counts,
    back_counts,
    scale_factor,
    targets_ref,
    render_up_ref,
    render_down_ref,
    decode_up_ref,
    decode_down_ref,
    pred_grad_ref,
    *rest,
):
    arrived = rest[: len(counts)]
    prediction_ref, gradients_ref = rest[len(counts) : len(counts) + 2]
    returns = rest[len(counts) + 2 : -7]
    grid = rest[-7]
    sems = rest[-1]
    loads = [
        pltpu.make_async_copy(source, held, sems.at[at])
        for at, (source, held) in enumerate(
            zip(
                (render_up_ref, render_down_ref, decode_up_ref, decode_down_ref, pred_grad_ref),
                rest[-6:-1],
            )
        )
    ]
    for load in loads:
        load.start()
    render_up_ref, render_down_ref, decode_up_ref, decode_down_ref, pred_grad_ref = rest[-6:-1]
    block_rows = arrived[0].shape[1]
    rows = grid.shape[0]

    grid[...] = jnp.zeros_like(grid)
    number = 0
    for ref, count in zip(arrived, counts):

        def add(at, carry, ref=ref, number=number):
            first = pl.multiple_of(targets_ref[number + at] * block_rows, block_rows)
            grid[pl.ds(first, block_rows)] += ref[at].astype(jnp.float32)
            return carry

        lax.fori_loop(0, count, add, 0, unroll=count <= 8)
        number += count

    for load in loads:
        load.wait()
    weights = ((render_up_ref, render_down_ref), (decode_up_ref, decode_down_ref))
    state = grid[...]
    stored = []
    for w_up, w_down in weights:
        scaling = lax.rsqrt(jnp.mean(state * state, axis=-1, keepdims=True) + eps)
        normed = (state * scaling).astype(jnp.bfloat16)
        value, slope = gelu_and_slope(plain(normed, w_up[...]))
        hidden = value.astype(jnp.bfloat16)
        stored.append((state, scaling, normed, slope, hidden))
        state = state + plain(hidden, w_down[...])
    prediction_ref[...] = state.astype(jnp.bfloat16)

    grad_state = pred_grad_ref[...].astype(jnp.float32) * scale_factor
    width = gradients_ref.shape[-1]
    for block in (1, 0):
        state, scaling, normed, slope, hidden = stored[block]
        w_up, w_down = weights[block]
        rounded = grad_state.astype(jnp.bfloat16)
        grad_down = contract_rows(hidden, rounded).astype(jnp.bfloat16)
        grad_pre = (against_rows(rounded, w_down[...]) * slope).astype(jnp.bfloat16)
        grad_up = contract_rows(normed, grad_pre).astype(jnp.bfloat16)
        gradients_ref[4 * block] = grad_up[:, :width]
        gradients_ref[4 * block + 1] = grad_up[:, width:]
        gradients_ref[4 * block + 2] = grad_down[:width]
        gradients_ref[4 * block + 3] = grad_down[width:]
        grad_normed = against_rows(grad_pre, w_up[...])
        unit_rows = state * scaling
        grad_state = grad_state + scaling * (
            grad_normed - unit_rows * jnp.mean(grad_normed * unit_rows, axis=-1, keepdims=True)
        )
    grid[...] = grad_state
    number = 0
    for ref, count in zip(returns, back_counts):

        def give(at, carry, ref=ref, number=number):
            first = pl.multiple_of(targets_ref[number + at] * block_rows, block_rows)
            ref[at] = grid[pl.ds(first, block_rows)].astype(jnp.bfloat16)
            return carry

        lax.fori_loop(0, count, give, 0, unroll=count <= 8)
        number += count


def heads(targets, weights, pred_grad, arrived, counts, back_counts, scale_factor):
    rows, channels = pred_grad.shape
    smem = pl.BlockSpec(memory_space=pltpu.SMEM)
    vmem = pl.BlockSpec(memory_space=pltpu.VMEM)
    block_rows = arrived[0].shape[1]
    return pl.pallas_call(
        functools.partial(heads_kernel, counts, back_counts, scale_factor),
        out_shape=(
            jax.ShapeDtypeStruct((rows, channels), jnp.bfloat16),
            jax.ShapeDtypeStruct((8, channels, channels), jnp.bfloat16),
        )
        + tuple(
            jax.ShapeDtypeStruct((count, block_rows, channels), jnp.bfloat16)
            for count in back_counts
        ),
        in_specs=[smem] + [pl.BlockSpec(memory_space=pl.ANY)] * 5 + [vmem] * len(arrived),
        out_specs=(vmem,) * (2 + len(back_counts)),
        scratch_shapes=[
            pltpu.VMEM((rows, channels), jnp.float32),
            *[pltpu.VMEM(weight.shape, weight.dtype) for weight in weights],
            pltpu.VMEM(pred_grad.shape, pred_grad.dtype),
            pltpu.SemaphoreType.DMA((5,)),
        ],
        compiler_params=pltpu.CompilerParams(vmem_limit_bytes=50 * mebibyte),
        name="heads",
    )(targets, *weights, pred_grad, *arrived)


def proj_grad_kernel(
    counts, sources_ref, alive_ref, tiles_ref, encoded_ref, *rest
):
    returned = rest[: len(counts)]
    gradient_ref = rest[len(counts)]
    (rows,) = rest[len(counts) + 1 :]
    block_rows = tiles_ref.shape[1]
    rows[...] = jnp.zeros_like(rows)
    number = 0
    for ref, count in zip(returned, counts):

        def add(at, carry, ref=ref, number=number):
            slot = tile_of(number + at, lax.axis_index("tile"), tiles_ref.shape[0])
            first = pl.multiple_of(sources_ref[slot] * block_rows, block_rows)
            product = contract_rows(tiles_ref[slot], ref[at])
            rows[pl.ds(first, block_rows)] += product * alive_ref[slot].astype(jnp.float32)
            return carry

        lax.fori_loop(0, count, add, 0, unroll=count <= 8)
        number += count
    total = contract_rows(encoded_ref[...], rows[...].astype(jnp.bfloat16))
    gradient_ref[...] = total.astype(jnp.bfloat16).reshape(gradient_ref.shape)


def proj_grad(sources, alive, tiles, encoded, returned, counts):
    tokens, width = encoded.shape
    channels = returned[0].shape[-1]
    smem = pl.BlockSpec(memory_space=pltpu.SMEM)
    vmem = pl.BlockSpec(memory_space=pltpu.VMEM)
    return pl.pallas_call(
        functools.partial(proj_grad_kernel, counts),
        out_shape=jax.ShapeDtypeStruct((8, width // 8, channels), jnp.bfloat16),
        in_specs=[smem] * 2 + [vmem] * (2 + len(returned)),
        out_specs=vmem,
        scratch_shapes=[pltpu.VMEM((tokens, channels), jnp.float32)],
        compiler_params=pltpu.CompilerParams(vmem_limit_bytes=16 * mebibyte),
        name="proj_grad",
    )(sources, alive, tiles, encoded, *returned)


def to_section(array, flip):
    count = lax.axis_size("section")
    return lax.ppermute(array, "section", [(at, at ^ flip) for at in range(count)])


def to_tile(array, flip):
    count = lax.axis_size("tile")
    return lax.ppermute(array, "tile", [(at, at ^ flip) for at in range(count)])


def rows_from(array, first, count):
    return lax.dynamic_slice_in_dim(array, first, count, 0)


def cut_kernel(plan, up_ref, down_ref, *rest):
    outputs, sems = rest[:-1], rest[-1]
    _, _, core, zone = position()
    half = down_ref.shape[0] // 2
    copies = []
    for number, (kind, first, step, count, to) in enumerate(plan[0]):
        start = pl.multiple_of(first + step * zone, 16)
        if kind == "up":
            source = up_ref.at[pl.ds(start, count), pl.ds(pl.multiple_of(core * half, 128), half)]
        else:
            source = down_ref.at[pl.ds(pl.multiple_of(core * half + start, 16), count)]
        output, row = to
        copies.append(
            pltpu.make_async_copy(
                source, outputs[output].at[pl.ds(row, count)], sems.at[number]
            )
        )
    for copy in copies:
        copy.start()
    for copy in copies:
        copy.wait()


def cut(up, down, plan, rows):
    width = down.shape[1]
    hbm = pl.BlockSpec(memory_space=pl.ANY)
    vmem = pl.BlockSpec(memory_space=pltpu.VMEM)
    return pl.pallas_call(
        functools.partial(cut_kernel, (plan,)),
        out_shape=tuple(jax.ShapeDtypeStruct((count, width), up.dtype) for count in rows),
        in_specs=[hbm, hbm],
        out_specs=(vmem,) * len(rows),
        scratch_shapes=[pltpu.SemaphoreType.DMA((len(plan),))],
        compiler_params=pltpu.CompilerParams(vmem_limit_bytes=60 * mebibyte),
        name="cut",
    )(up, down)


def gather_layers(own_up, own_down, dst_block):
    half = own_down.shape[0] // 2
    shared = half // 8 // 16 * 16
    alone = (half - shared) // 2
    x_up, y_down = cut(
        own_up,
        own_down,
        (("up", 0, alone, alone, (0, 0)), ("down", 0, alone, alone, (1, 0))),
        (alone, alone),
    )
    down_pack, up_pack, both_shared = cut(
        own_up,
        own_down,
        (
            ("down", 0, 0, half, (0, 0)),
            ("up", 2 * alone, 0, shared, (0, half)),
            ("up", 0, 0, half, (1, 0)),
            ("down", 2 * alone, 0, shared, (1, half)),
            ("up", 2 * alone, 0, shared, (2, 0)),
            ("down", 2 * alone, 0, shared, (2, shared)),
        ),
        (half + shared, half + shared, 2 * shared),
    )
    x_up = to_section(x_up, 1)
    y_down = to_section(y_down, 2)
    table, both_shared = lax.optimization_barrier((dst_block, both_shared))
    flip = 1
    while flip < lax.axis_size("tile"):
        table = jnp.concatenate([table, to_tile(table, flip)])
        flip *= 2
    x_up, y_down, both_shared, table = lax.optimization_barrier(
        (x_up, y_down, both_shared, table)
    )
    d_down = to_section(y_down, 1)
    d_up = to_section(x_up, 2)
    first_far = to_tile(jnp.concatenate([x_up, y_down]), 2)
    d_shared = to_section(both_shared, 3)
    d_up, d_down, down_pack, up_pack = lax.optimization_barrier(
        (d_up, d_down, down_pack, up_pack)
    )
    first_far, second_sent = lax.optimization_barrier(
        (first_far, jnp.concatenate([d_up, d_down]))
    )
    second_far = to_tile(second_sent, 2)
    x_pack = to_section(down_pack, 1)
    y_pack = to_section(up_pack, 2)
    x_pack, y_pack, second_far = lax.optimization_barrier((x_pack, y_pack, second_far))
    parts = {
        "x_up_own": x_up,
        "y_down_own": y_down,
        "d_shared": d_shared,
        "first_far": first_far,
        "d_up_own": d_up,
        "d_down_own": d_down,
        "x_pack": x_pack,
        "y_pack": y_pack,
        "second_far": second_far,
    }
    parts.update({"other_" + name: to_tile(part, 1) for name, part in parts.items()})
    return parts, table


def add_up(left, *others):
    total = left.astype(jnp.float32)
    for other in others:
        total = total + other.astype(jnp.float32)
    return total.astype(jnp.bfloat16)


def section_share(array, section, core):
    count = lax.axis_size("section")
    mine = rows_from(array, core * count, count)
    others = rows_from(array, (1 - core) * count, count)
    mine = add_up(mine, to_tile(others, 1))

    def pick(number):
        return lax.dynamic_index_in_dim(mine, number, 0, keepdims=False)

    return (pick(section), *[to_section(pick(section ^ flip), flip) for flip in (3, 1, 2)])


def chips_shares(share):
    chips = lax.axis_size("tile") // 2
    if chips == 4:
        return (share, *[to_tile(share, 2 * flip) for flip in (2, 3, 1)])
    groups = [[2 * chip + side for chip in range(chips)] for side in (0, 1)]
    return (lax.psum(share, "tile", axis_index_groups=groups),)


def section_shares(share):
    return (share, *[to_section(share, flip) for flip in (1, 2, 3)])


def with_other_core(shares):
    gathered = jnp.stack(shares)
    return (gathered, to_tile(gathered, 1))


def unpack_kernel(gathered_ref, swapped_ref, *outputs):
    section, _, core, _ = position()
    count, rows, columns = gathered_ref.shape
    for side in range(2):
        for number in range(count):
            at = jnp.bitwise_xor(section, number)
            values = jnp.where(
                core == side,
                gathered_ref[at].astype(jnp.float32),
                swapped_ref[at].astype(jnp.float32),
            )
            if len(outputs) == 1:
                outputs[0][pl.ds((side * count + number) * rows, rows)] = values
            elif number < 2:
                outputs[2 * side][:, pl.ds(number * columns, columns)] = values
            else:
                outputs[2 * side + 1][pl.ds((number - 2) * rows, rows)] = values


def unpack(gathered, swapped, shapes):
    vmem = pl.BlockSpec(memory_space=pltpu.VMEM)
    return pl.pallas_call(
        unpack_kernel,
        out_shape=tuple(jax.ShapeDtypeStruct(shape, jnp.float32) for shape in shapes),
        in_specs=[vmem, vmem],
        out_specs=(vmem,) * len(shapes),
        compiler_params=pltpu.CompilerParams(vmem_limit_bytes=16 * mebibyte),
        name="unpack",
    )(gathered, swapped)


def on_device(
    cams,
    vit_up,
    vit_down,
    proj,
    frustum_tiles,
    src_block,
    dst_block,
    live,
    render_up,
    render_down,
    decode_up,
    decode_down,
    pred_grad,
):
    section, _, core, _ = position()
    tile_count = lax.axis_size("tile")
    micro_count = cams.shape[0]
    small = tile_count == 8
    if small:
        pairs = (2, 2, 2, 2)
        singles = (1,) * 8
    else:
        pairs = singles = (tile_count,)

    def cross(sent):
        if not small:
            return [lax.all_to_all(sent[0], "tile", split_axis=0, concat_axis=0, tiled=True)]
        moved = {0: sent[0]}
        for flip in (2, 3, 1):
            moved[flip] = to_tile(sent[flip], 2 * flip)
        return [moved[flip] for flip in range(4)]

    def over(moved):
        if not small:
            return moved
        found = []
        for part in moved:
            found += [part, to_tile(part[1:], 1)]
        return found

    parts, table = gather_layers(vit_up[0], vit_down[0], dst_block)
    encoded, targets, *pieces = encode(
        src_block[0], live[0], table, cams, vit_up[0], vit_down[0], proj,
        frustum_tiles[0], parts, pairs,
    )
    arrived = over(cross(pieces))

    scale_factor = 1.0 / math.sqrt(micro_count * pred_grad.shape[1] * tile_count)
    weights = (render_up, render_down, decode_up, decode_down)
    prediction, gradients, *returns = heads(
        targets, weights, pred_grad[0], arrived, singles, pairs, scale_factor
    )

    moved = cross(returns)
    head_shares = section_share(gradients, section, core)
    moved, head_shares = lax.optimization_barrier((moved, head_shares))
    returned = over(moved)
    head_shares = chips_shares(add_up(*head_shares))
    grad_proj = proj_grad(
        src_block[0], live[0], frustum_tiles[0], encoded, returned, singles
    )
    proj_shares = section_share(grad_proj, section, core)
    proj_shares = chips_shares(add_up(*proj_shares))
    head_shares = section_shares(add_up(*head_shares))
    proj_shares = section_shares(add_up(*proj_shares))
    head_shares = with_other_core(head_shares)
    grads = unpack(
        *head_shares,
        (render_up.shape, render_down.shape, decode_up.shape, decode_down.shape),
    )
    (grad_proj,) = unpack(*with_other_core(proj_shares), (proj.shape,))
    return (prediction[None], grad_proj, *grads)


def solution(mesh):
    placed = (
        P(None, "tile", None),
        P("section", None, None),
        P("section", None, None),
        P(),
        P("tile", None, None, None),
        P("tile", None),
        P("tile", None),
        P("tile", None),
        P(),
        P(),
        P(),
        P(),
        P("section", "tile", None),
    )
    return jax.shard_map(
        on_device,
        mesh=mesh,
        in_specs=placed,
        out_specs=(P("section", "tile", None), P(), P(), P(), P(), P()),
        check_vma=False,
    )
```

time: 210 us -> 181 us (0.86)
  blocking collectives: 11.9 us -> 0 us
  waiting for transfers between devices: 99.5 us -> 87.8 us
  local copies, waits for them, and re-layouts: 13.5 us -> 6 us
  other arithmetic: 5.94 us -> 1.7 us
  Pallas kernels: 27.1 us -> 31.3 us
    all_gather x1 -> x0, blocking collectives: 11.9 us -> none  [on_device(): all_targets = lax.all_gather(dst_block, 'tile', axis=0, tiled=True)]
    ppermute x35 -> x38, waiting for transfers between devices: 60.3 us -> 49.3 us  [to_tile(): return lax.ppermute(array, 'tile', [(at, at ^ flip) for at in range(count)])]
    dynamic_slice x8 -> x2, local copies, waits for them, and re-layouts: 6.93 us -> 0.06 us  [rows_from(): return lax.dynamic_slice_in_dim(array, first, count, 0)]
    pallas_call x2 -> x6, Pallas kernels: 25.8 us -> 30.1 us  [the longest x1 17 us: encode(): pl.pallas_call(functools.partial(encode_kernel, names, counts), out_shape...]
    ppermute x35 -> x38, starting transfers between devices: 27.2 us -> 31.5 us  [to_tile(): return lax.ppermute(array, 'tile', [(at, at ^ flip) for at in range(count)])]
    unnamed x34 -> x60, local copies, waits for them, and re-layouts: 1.93 us -> 5.83 us
    concatenate x5, other arithmetic: 3.4 us -> 0.17 us  [the longest x1 0.07 us: gather_layers(): first_far = to_tile(jnp.concatenate([x_up, y_down]), 2)]
    ppermute x18 -> x19, starting transfers between devices: 23.7 us -> 21.1 us  [to_section(): lax.ppermute(array, 'section', [(at, at ^ flip) for at in range(count)])]
  transfers between devices with their start and end apart: 53 -> 57, of which waited for: 30 -> 30; matrix products, arithmetic and copies ran while one was open for 5% -> 1% of each run, Pallas kernels for 0% -> 2%
where the time goes in v2:
time: 181 us
  waiting for transfers between devices  87.8 us (49%)
  starting transfers between devices  52.6 us (29%)
  Pallas kernels  31.3 us (17%)
  local copies, waits for them, and re-layouts  6 us (3%)
    ppermute x38, waiting for transfers between devices, to_tile(): return lax.ppermute(array, 'tile', [(at, at ^ flip) for at in range(count)])  49.3 us
    ppermute x19, waiting for transfers between devices, to_section(): lax.ppermute(array, 'section', [(at, at ^ flip) for at in range(count)])  38.5 us
    ppermute x38, starting transfers between devices, to_tile(): return lax.ppermute(array, 'tile', [(at, at ^ flip) for at in range(count)])  31.5 us
    ppermute x19, starting transfers between devices, to_section(): lax.ppermute(array, 'section', [(at, at ^ flip) for at in range(count)])  21.1 us
    pallas_call x1, Pallas kernels, encode(): pl.pallas_call(functools.partial(encode_kernel, names, counts), out_shape...  17 us
    unnamed x60, local copies, waits for them, and re-layouts  5.83 us
    pallas_call x2, Pallas kernels, cut(): pl.pallas_call(functools.partial(cut_kernel, (plan,)), out_shape=tuple((j...  5.62 us
    pallas_call x1, Pallas kernels, heads(): pl.pallas_call(functools.partial(heads_kernel, counts, back_counts, scale...  5.08 us
  transfers between devices with their start and end apart: 57, of which 30 were waited for; matrix products, arithmetic and copies ran while one was open for 1% of the time, Pallas kernels for 2%

profile of v2, /device:TPU:0, one launch (start us, length us, event | category | flops | bytes accessed | tf_op | source)
XLA Modules:
  0.0 180.5 jit_solution(4334771997752555271)
XLA Ops:
  0.6 2.2 %cut.2 = (bf16[336,768]{1,0:T(8,128)(2,1)}, bf16[336,768]{1,0:T(8,128)(2,1)}) custom-call(bf16[768,1536]{1,0:T(8,128)(2,1)} %bitcast.39, bf16[1536,768]{1,0:T(8,128)(2,1)} %bitcast.42), custom_call_target="tpu_custom_call" | custom-call | tf_op jit(solution)/shard_map/cut/pallas_call | solution.py:409
  2.8 3.0 %collective-permute-start = (bf16[336,768]{1,0:T(8,128)(2,1)}, bf16[336,768]{1,0:T(8,128)(2,1)S(1)}, u32[]{:S(2)}, u32[]{:S(2)}) collective-permute-start(bf16[336,768]{1,0:T(8,128)(2,1)} %get-tuple-element.50), channel_id=1, source_target_pairs={{0,8},{8,0},{16,24},{24,16},{1,9},{9,1},{17,25},{25,17},{2,10},{10... | collective-permute-start | bytes 1548296 | tf_op jit(solution)/shard_map/ppermute | solution.py:370
  7.4 3.4 %cut.3 = (bf16[864,768]{1,0:T(8,128)(2,1)}, bf16[864,768]{1,0:T(8,128)(2,1)}, bf16[192,768]{1,0:T(8,128)(2,1)}) custom-call(bf16[768,1536]{1,0:T(8,128)(2,1)} %bitcast.40, bf16[1536,768]{1,0:T(8,128)(2,1)} %bitcast.43), custom_call_target="tpu_custom_call" | custom-call | tf_op jit(solution)/shard_map/cut/pallas_call | solution.py:409
  13.6 2.0 %collective-permute-done.3 = s32[2,8]{1,0:T(2,128)S(1)} collective-permute-done((s32[2,8]{1,0:T(2,128)S(1)}, s32[2,8]{1,0:T(2,128)S(1)}, u32[]{:S(2)}, u32[]{:S(2)}) %collective-permute-start.3) | collective-permute-done | bytes 96 | tf_op jit(solution)/shard_map/ppermute | solution.py:375
  15.6 2.7 %collective-permute-start.4 = (s32[4,8]{1,0:T(4,128)S(1)}, s32[4,8]{1,0:T(4,128)S(1)}, u32[]{:S(2)}, u32[]{:S(2)}) collective-permute-start(s32[4,8]{1,0:T(4,128)S(1)} %pad_add_fusion.1), channel_id=1, source_target_pairs={{0,4},{1,5},{2,6},{3,7},{4,0},{5,1},{6,2},{7,3},{8,12},{9,13},{10,... | collective-permute-start | bytes 392 | tf_op jit(solution)/shard_map/ppermute | solution.py:375
  18.3 1.9 %collective-permute-done.4 = s32[4,8]{1,0:T(4,128)S(1)} collective-permute-done((s32[4,8]{1,0:T(4,128)S(1)}, s32[4,8]{1,0:T(4,128)S(1)}, u32[]{:S(2)}, u32[]{:S(2)}) %collective-permute-start.4) | collective-permute-done | bytes 160 | tf_op jit(solution)/shard_map/ppermute | solution.py:375
  23.1 10.5 %collective-permute-done.7.rest_4_ = bf16[336,768]{1,0:T(8,128)(2,1)S(1)} collective-permute-done((bf16[336,768]{1,0:T(8,128)(2,1)S(1)}, bf16[336,768]{1,0:T(8,128)(2,1)S(1)}, u32[]{:S(2)}, u32[]{:S(2)}) %collective-permute-start.7) | collective-permute-done | bytes 516128 | tf_op jit(solution)/shard_map/ppermute | solution.py:370
  35.9 7.5 %collective-permute-done.6.rest_3_ = bf16[672,768]{1,0:T(8,128)(2,1)S(1)} collective-permute-done((bf16[672,768]{1,0:T(8,128)(2,1)S(1)}, bf16[672,768]{1,0:T(8,128)(2,1)S(1)}, u32[]{:S(2)}, u32[]{:S(2)}) %collective-permute-start.6) | collective-permute-done | bytes 1032224 | tf_op jit(solution)/shard_map/ppermute | solution.py:375
  45.9 24.0 %collective-permute-done.5.rest_2_ = bf16[192,768]{1,0:T(8,128)(2,1)S(1)} collective-permute-done((bf16[192,768]{1,0:T(8,128)(2,1)S(1)}, bf16[192,768]{1,0:T(8,128)(2,1)S(1)}, u32[]{:S(2)}, u32[]{:S(2)}) %collective-permute-start.5) | collective-permute-done | bytes 294944 | tf_op jit(solution)/shard_map/ppermute | solution.py:370
  72.4 4.4 %collective-permute-done.16.rest_13_ = bf16[336,768]{1,0:T(8,128)(2,1)S(1)} collective-permute-done((bf16[336,768]{1,0:T(8,128)(2,1)S(1)}, bf16[336,768]{1,0:T(8,128)(2,1)S(1)}, u32[]{:S(2)}, u32[]{:S(2)}) %collective-permute-start.16) | collective-permute-done | bytes 516128 | tf_op jit(solution)/shard_map/ppermute | solution.py:375
  76.9 3.6 %collective-permute-done.17.rest_14_ = bf16[336,768]{1,0:T(8,128)(2,1)S(1)} collective-permute-done((bf16[336,768]{1,0:T(8,128)(2,1)S(1)}, bf16[336,768]{1,0:T(8,128)(2,1)S(1)}, u32[]{:S(2)}, u32[]{:S(2)}) %collective-permute-start.17) | collective-permute-done | bytes 516128 | tf_op jit(solution)/shard_map/ppermute | solution.py:375
  82.9 17.0 %encode.1 = (bf16[512,768]{1,0:T(8,128)(2,1)}, s32[8]{0:T(128)S(1)}, bf16[2,128,256]{2,1,0:T(8,128)(2,1)S(1)}, bf16[2,128,256]{2,1,0:T(8,128)(2,1)S(1)}, bf16[2,...) custom-call(s32[8]{0:T(128)S(1)} %bitcast.35, s32[8]{0:T(128)S(1)} %bitcast.37, ...), custom_call_target="tpu_custom_call" | custom-call | tf_op jit(solution)/shard_map/encode/pallas_call | solution.py:186
  100.4 2.6 %collective-permute-start.24 = (bf16[2,128,256]{2,1,0:T(8,128)(2,1)S(1)}, bf16[2,128,256]{2,1,0:T(8,128)(2,1)S(1)}, u32[]{:S(2)}, u32[]{:S(2)}) collective-permute-start(bf16[2,128,256]{2,1,0:T(8,128)(2,1)S(1)} %get-tuple-element.73), channel_id=1, source_target_pairs={{0,4},{1,5},{2,6},{3,7},{4,0},{5,1},{6,2},{7,3},{8,12},{9,13},{10,... | collective-permute-start | bytes 393224 | tf_op jit(solution)/shard_map/ppermute | solution.py:375
  104.4 3.9 %collective-permute-done.22.rest_2_ = bf16[2,128,256]{2,1,0:T(8,128)(2,1)S(1)} collective-permute-done((bf16[2,128,256]{2,1,0:T(8,128)(2,1)S(1)}, bf16[2,128,256]{2,1,0:T(8,128)(2,1)S(1)}, u32[]{:S(2)}, u32[]{:S(2)}) %collective-permute-start.22) | collective-permute-done | bytes 131104 | tf_op jit(solution)/shard_map/ppermute | solution.py:375
  108.9 4.3 %collective-permute-done.26.rest_6_ = bf16[2,128,256]{2,1,0:T(8,128)(2,1)S(1)} collective-permute-done((bf16[2,128,256]{2,1,0:T(8,128)(2,1)S(1)}, bf16[2,128,256]{2,1,0:T(8,128)(2,1)S(1)}, u32[]{:S(2)}, u32[]{:S(2)}) %collective-permute-start.26) | collective-permute-done | bytes 131104 | tf_op jit(solution)/shard_map/ppermute | solution.py:375
  116.0 5.1 %heads.1 = (bf16[640,256]{1,0:T(8,128)(2,1)}, bf16[8,256,256]{2,1,0:T(8,128)(2,1)S(1)}, bf16[2,128,256]{2,1,0:T(8,128)(2,1)S(1)}, bf16[2,128,256]{2,1,0:T(8,128)...) custom-call(s32[8]{0:T(128)S(1)} %get-tuple-element.70.targets_ref, ...), custom_call_target="tpu_custom_call" | custom-call | tf_op jit(solution)/shard_map/heads/pallas_call | solution.py:305
  123.3 2.5 %collective-permute-start.28 = (bf16[2,128,256]{2,1,0:T(8,128)(2,1)}, bf16[2,128,256]{2,1,0:T(8,128)(2,1)S(1)}, u32[]{:S(2)}, u32[]{:S(2)}) collective-permute-start(bf16[2,128,256]{2,1,0:T(8,128)(2,1)} %copy-done.14), channel_id=1, source_target_pairs={{0,2},{1,3},{2,0},{3,1},{4,6},{5,7},{6,4},{7,5},{8,10},{9,11},{10,... | collective-permute-start | bytes 393224 | tf_op jit(solution)/shard_map/ppermute | solution.py:375
  125.8 1.9 %collective-permute-start.29 = (bf16[2,128,256]{2,1,0:T(8,128)(2,1)}, bf16[2,128,256]{2,1,0:T(8,128)(2,1)S(1)}, u32[]{:S(2)}, u32[]{:S(2)}) collective-permute-start(bf16[2,128,256]{2,1,0:T(8,128)(2,1)} %copy-done.13), channel_id=1, source_target_pairs={{0,4},{1,5},{2,6},{3,7},{4,0},{5,1},{6,2},{7,3},{8,12},{9,13},{10,... | collective-permute-start | bytes 393224 | tf_op jit(solution)/shard_map/ppermute | solution.py:375
  134.0 4.9 %collective-permute-done.30.rest_6_ = bf16[2,128,256]{2,1,0:T(8,128)(2,1)S(1)} collective-permute-done((bf16[2,128,256]{2,1,0:T(8,128)(2,1)}, bf16[2,128,256]{2,1,0:T(8,128)(2,1)S(1)}, u32[]{:S(2)}, u32[]{:S(2)}) %collective-permute-start.30) | collective-permute-done | bytes 131104 | tf_op jit(solution)/shard_map/ppermute | solution.py:375
  143.2 4.1 %collective-permute-start.50 = (bf16[256,256]{1,0:T(8,128)(2,1)S(1)}, bf16[256,256]{1,0:T(8,128)(2,1)S(1)}, u32[]{:S(2)}, u32[]{:S(2)}) collective-permute-start(bf16[256,256]{1,0:T(8,128)(2,1)S(1)} %add_convert_fusion.3), channel_id=1, source_target_pairs={{0,4},{1,5},{2,6},{3,7},{4,0},{5,1},{6,2},{7,3},{8,12},{9,13},{10,... | collective-permute-start | bytes 393224 | tf_op jit(solution)/shard_map/ppermute | solution.py:375
  150.0 7.0 %collective-permute-done.50 = bf16[256,256]{1,0:T(8,128)(2,1)S(1)} collective-permute-done((bf16[256,256]{1,0:T(8,128)(2,1)S(1)}, bf16[256,256]{1,0:T(8,128)(2,1)S(1)}, u32[]{:S(2)}, u32[]{:S(2)}) %collective-permute-start.50) | collective-permute-done | bytes 131104 | tf_op jit(solution)/shard_map/ppermute | solution.py:375
  163.6 2.6 %collective-permute-start.44 = (bf16[96,256]{1,0:T(8,128)(2,1)S(1)}, bf16[96,256]{1,0:T(8,128)(2,1)S(1)}, u32[]{:S(2)}, u32[]{:S(2)}) collective-permute-start(bf16[96,256]{1,0:T(8,128)(2,1)S(1)} %fusion.2), channel_id=1, source_target_pairs={{0,6},{1,7},{2,4},{3,5},{4,2},{5,3},{6,0},{7,1},{8,14},{9,15},{10,... | collective-permute-start | bytes 147464 | tf_op jit(solution)/shard_map/ppermute | solution.py:375
  167.3 2.1 %collective-permute-done.44 = bf16[96,256]{1,0:T(8,128)(2,1)S(1)} collective-permute-done((bf16[96,256]{1,0:T(8,128)(2,1)S(1)}, bf16[96,256]{1,0:T(8,128)(2,1)S(1)}, u32[]{:S(2)}, u32[]{:S(2)}) %collective-permute-start.44) | collective-permute-done | bytes 49184 | tf_op jit(solution)/shard_map/ppermute | solution.py:375
  171.6 2.3 %collective-permute-start.48 = (bf16[96,256]{1,0:T(8,128)(2,1)S(1)}, bf16[96,256]{1,0:T(8,128)(2,1)S(1)}, u32[]{:S(2)}, u32[]{:S(2)}) collective-permute-start(bf16[96,256]{1,0:T(8,128)(2,1)S(1)} %add_convert_fusion.4), channel_id=1, source_target_pairs={{0,24},{8,16},{16,8},{24,0},{1,25},{9,17},{17,9},{25,1},{2,26},{10... | collective-permute-start | bytes 147464 | tf_op jit(solution)/shard_map/ppermute | solution.py:370
  (182 shorter events, 53.9 us)
Async XLA Ops:
  2.8 17.4 %collective-permute-start = (bf16[336,768]{1,0:T(8,128)(2,1)}, bf16[336,768]{1,0:T(8,128)(2,1)S(1)}, u32[]{:S(2)}, u32[]{:S(2)}) collective-permute-start(bf16[336,768]{1,0:T(8,128)(2,1)} %get-tuple-element.50), channel_id=1, source_target_pairs={{0,8},{8,0},{16,24},{24,16},{1,9},{9,1},{17,25},{25,17},{2,10},{10... | collective-permute-start | bytes 1548296 | tf_op jit(solution)/shard_map/ppermute | solution.py:370
  5.8 14.4 %collective-permute-start.1 = (bf16[336,768]{1,0:T(8,128)(2,1)}, bf16[336,768]{1,0:T(8,128)(2,1)S(1)}, u32[]{:S(2)}, u32[]{:S(2)}) collective-permute-start(bf16[336,768]{1,0:T(8,128)(2,1)} %get-tuple-element.51), channel_id=1, source_target_pairs={{0,16},{8,24},{16,0},{24,8},{1,17},{9,25},{17,1},{25,9},{2,18},{10... | collective-permute-start | bytes 1548296 | tf_op jit(solution)/shard_map/ppermute | solution.py:370
  20.4 23.0 %collective-permute-start.6 = (bf16[672,768]{1,0:T(8,128)(2,1)S(1)}, bf16[672,768]{1,0:T(8,128)(2,1)S(1)}, u32[]{:S(2)}, u32[]{:S(2)}) collective-permute-start(bf16[672,768]{1,0:T(8,128)(2,1)S(1)} %pad_maximum_fusion), channel_id=1, source_target_pairs={{0,2},{1,3},{2,0},{3,1},{4,6},{5,7},{6,4},{7,5},{8,10},{9,11},{10,... | collective-permute-start | bytes 3096584 | tf_op jit(solution)/shard_map/ppermute | solution.py:375
  22.0 11.5 %collective-permute-start.7 = (bf16[336,768]{1,0:T(8,128)(2,1)S(1)}, bf16[336,768]{1,0:T(8,128)(2,1)S(1)}, u32[]{:S(2)}, u32[]{:S(2)}) collective-permute-start(bf16[336,768]{1,0:T(8,128)(2,1)S(1)} %collective-permute-done.rest_0_), channel_id=1, source_target_pairs={{0,16},{8,24},{16,0},{24,8},{1,17},{9,25},{17,1},{25,9},{2,18},{10... | collective-permute-start | bytes 1548296 | tf_op jit(solution)/shard_map/ppermute | solution.py:370
  22.5 11.7 %collective-permute-start.8 = (bf16[336,768]{1,0:T(8,128)(2,1)S(1)}, bf16[336,768]{1,0:T(8,128)(2,1)S(1)}, u32[]{:S(2)}, u32[]{:S(2)}) collective-permute-start(bf16[336,768]{1,0:T(8,128)(2,1)S(1)} %collective-permute-done.1.rest_1_), channel_id=1, source_target_pairs={{0,8},{8,0},{16,24},{24,16},{1,9},{9,1},{17,25},{25,17},{2,10},{10... | collective-permute-start | bytes 1548296 | tf_op jit(solution)/shard_map/ppermute | solution.py:370
  34.2 35.7 %collective-permute-start.10 = (bf16[864,768]{1,0:T(8,128)(2,1)}, bf16[864,768]{1,0:T(8,128)(2,1)S(1)}, u32[]{:S(2)}, u32[]{:S(2)}) collective-permute-start(bf16[864,768]{1,0:T(8,128)(2,1)} %get-tuple-element.65), channel_id=1, source_target_pairs={{0,16},{8,24},{16,0},{24,8},{1,17},{9,25},{17,1},{25,9},{2,18},{10... | collective-permute-start | bytes 3981320 | tf_op jit(solution)/shard_map/ppermute | solution.py:370
  35.3 35.1 %collective-permute-start.9 = (bf16[864,768]{1,0:T(8,128)(2,1)S(1)}, bf16[864,768]{1,0:T(8,128)(2,1)S(1)}, u32[]{:S(2)}, u32[]{:S(2)}) collective-permute-start(bf16[864,768]{1,0:T(8,128)(2,1)S(1)} %copy-done.28), channel_id=1, source_target_pairs={{0,8},{8,0},{16,24},{24,16},{1,9},{9,1},{17,25},{25,17},{2,10},{10... | collective-permute-start | bytes 3981320 | tf_op jit(solution)/shard_map/ppermute | solution.py:370
  43.4 27.0 %collective-permute-start.11 = (bf16[672,768]{1,0:T(8,128)(2,1)S(1)}, bf16[672,768]{1,0:T(8,128)(2,1)S(1)}, u32[]{:S(2)}, u32[]{:S(2)}) collective-permute-start(bf16[672,768]{1,0:T(8,128)(2,1)S(1)} %pad_maximum_fusion.1), channel_id=1, source_target_pairs={{0,2},{1,3},{2,0},{3,1},{4,6},{5,7},{6,4},{7,5},{8,10},{9,11},{10,... | collective-permute-start | bytes 3096584 | tf_op jit(solution)/shard_map/ppermute | solution.py:375
  45.0 24.9 %collective-permute-start.5 = (bf16[192,768]{1,0:T(8,128)(2,1)S(1)}, bf16[192,768]{1,0:T(8,128)(2,1)S(1)}, u32[]{:S(2)}, u32[]{:S(2)}) collective-permute-start(bf16[192,768]{1,0:T(8,128)(2,1)S(1)} %copy-done.29), channel_id=1, source_target_pairs={{0,24},{8,16},{16,8},{24,0},{1,25},{9,17},{17,9},{25,1},{2,26},{10... | collective-permute-start | bytes 884744 | tf_op jit(solution)/shard_map/ppermute | solution.py:370
  45.9 25.1 %collective-permute-start.12 = (bf16[336,768]{1,0:T(8,128)(2,1)S(1)}, bf16[336,768]{1,0:T(8,128)(2,1)S(1)}, u32[]{:S(2)}, u32[]{:S(2)}) collective-permute-start(bf16[336,768]{1,0:T(8,128)(2,1)S(1)} %collective-permute-done.rest_0_), channel_id=1, source_target_pairs={{0,1},{1,0},{2,3},{3,2},{4,5},{5,4},{6,7},{7,6},{8,9},{9,8},{10,11... | collective-permute-start | bytes 1548296 | tf_op jit(solution)/shard_map/ppermute | solution.py:375
  70.4 10.0 %collective-permute-start.18 = (bf16[864,768]{1,0:T(8,128)(2,1)S(1)}, bf16[864,768]{1,0:T(8,128)(2,1)S(1)}, u32[]{:S(2)}, u32[]{:S(2)}) collective-permute-start(bf16[864,768]{1,0:T(8,128)(2,1)S(1)} %collective-permute-done.9.rest_6_), channel_id=1, source_target_pairs={{0,1},{1,0},{2,3},{3,2},{4,5},{5,4},{6,7},{7,6},{8,9},{9,8},{10,11... | collective-permute-start | bytes 3981320 | tf_op jit(solution)/shard_map/ppermute | solution.py:375
  70.6 9.9 %collective-permute-start.19 = (bf16[864,768]{1,0:T(8,128)(2,1)S(1)}, bf16[864,768]{1,0:T(8,128)(2,1)S(1)}, u32[]{:S(2)}, u32[]{:S(2)}) collective-permute-start(bf16[864,768]{1,0:T(8,128)(2,1)S(1)} %collective-permute-done.10.rest_7_), channel_id=1, source_target_pairs={{0,1},{1,0},{2,3},{3,2},{4,5},{5,4},{6,7},{7,6},{8,9},{9,8},{10,11... | collective-permute-start | bytes 3981320 | tf_op jit(solution)/shard_map/ppermute | solution.py:375
  71.8 8.6 %collective-permute-start.15 = (bf16[672,768]{1,0:T(8,128)(2,1)S(1)}, bf16[672,768]{1,0:T(8,128)(2,1)S(1)}, u32[]{:S(2)}, u32[]{:S(2)}) collective-permute-start(bf16[672,768]{1,0:T(8,128)(2,1)S(1)} %collective-permute-done.6.rest_3_), channel_id=1, source_target_pairs={{0,1},{1,0},{2,3},{3,2},{4,5},{5,4},{6,7},{7,6},{8,9},{9,8},{10,11... | collective-permute-start | bytes 3096584 | tf_op jit(solution)/shard_map/ppermute | solution.py:375
  103.0 10.3 %collective-permute-start.26 = (bf16[2,128,256]{2,1,0:T(8,128)(2,1)S(1)}, bf16[2,128,256]{2,1,0:T(8,128)(2,1)S(1)}, u32[]{:S(2)}, u32[]{:S(2)}) collective-permute-start(bf16[2,128,256]{2,1,0:T(8,128)(2,1)S(1)} %get-tuple-element.74), channel_id=1, source_target_pairs={{0,6},{1,7},{2,4},{3,5},{4,2},{5,3},{6,0},{7,1},{8,14},{9,15},{10,... | collective-permute-start | bytes 393224 | tf_op jit(solution)/shard_map/ppermute | solution.py:375
  104.4 8.9 %collective-permute-start.21 = (bf16[1,128,256]{2,1,0:T(8,128)(2,1)S(1)}, bf16[1,128,256]{2,1,0:T(8,128)(2,1)S(1)}, u32[]{:S(2)}, u32[]{:S(2)}) collective-permute-start(bf16[1,128,256]{2,1,0:T(8,128)(2,1)S(1)} %slice.24), channel_id=1, source_target_pairs={{0,1},{1,0},{2,3},{3,2},{4,5},{5,4},{6,7},{7,6},{8,9},{9,8},{10,11... | collective-permute-start | bytes 196616 | tf_op jit(solution)/shard_map/ppermute | solution.py:375
  123.3 9.3 %collective-permute-start.28 = (bf16[2,128,256]{2,1,0:T(8,128)(2,1)}, bf16[2,128,256]{2,1,0:T(8,128)(2,1)S(1)}, u32[]{:S(2)}, u32[]{:S(2)}) collective-permute-start(bf16[2,128,256]{2,1,0:T(8,128)(2,1)} %copy-done.14), channel_id=1, source_target_pairs={{0,2},{1,3},{2,0},{3,1},{4,6},{5,7},{6,4},{7,5},{8,10},{9,11},{10,... | collective-permute-start | bytes 393224 | tf_op jit(solution)/shard_map/ppermute | solution.py:375
  127.8 11.1 %collective-permute-start.30 = (bf16[2,128,256]{2,1,0:T(8,128)(2,1)}, bf16[2,128,256]{2,1,0:T(8,128)(2,1)S(1)}, u32[]{:S(2)}, u32[]{:S(2)}) collective-permute-start(bf16[2,128,256]{2,1,0:T(8,128)(2,1)} %copy-done.12), channel_id=1, source_target_pairs={{0,6},{1,7},{2,4},{3,5},{4,2},{5,3},{6,0},{7,1},{8,14},{9,15},{10,... | collective-permute-start | bytes 393224 | tf_op jit(solution)/shard_map/ppermute | solution.py:375
  130.5 8.4 %collective-permute-start.32 = (bf16[256,256]{1,0:T(8,128)(2,1)S(1)}, bf16[256,256]{1,0:T(8,128)(2,1)S(1)}, u32[]{:S(2)}, u32[]{:S(2)}) collective-permute-start(bf16[256,256]{1,0:T(8,128)(2,1)S(1)} %get-tuple-element.96), channel_id=1, source_target_pairs={{0,24},{8,16},{16,8},{24,0},{1,25},{9,17},{17,9},{25,1},{2,26},{10... | collective-permute-start | bytes 393224 | tf_op jit(solution)/shard_map/ppermute | solution.py:370
  143.2 13.8 %collective-permute-start.50 = (bf16[256,256]{1,0:T(8,128)(2,1)S(1)}, bf16[256,256]{1,0:T(8,128)(2,1)S(1)}, u32[]{:S(2)}, u32[]{:S(2)}) collective-permute-start(bf16[256,256]{1,0:T(8,128)(2,1)S(1)} %add_convert_fusion.3), channel_id=1, source_target_pairs={{0,4},{1,5},{2,6},{3,7},{4,0},{5,1},{6,2},{7,3},{8,12},{9,13},{10,... | collective-permute-start | bytes 393224 | tf_op jit(solution)/shard_map/ppermute | solution.py:375
  147.3 10.3 %collective-permute-start.51 = (bf16[256,256]{1,0:T(8,128)(2,1)S(1)}, bf16[256,256]{1,0:T(8,128)(2,1)S(1)}, u32[]{:S(2)}, u32[]{:S(2)}) collective-permute-start(bf16[256,256]{1,0:T(8,128)(2,1)S(1)} %add_convert_fusion.3), channel_id=1, source_target_pairs={{0,6},{1,7},{2,4},{3,5},{4,2},{5,3},{6,0},{7,1},{8,14},{9,15},{10,... | collective-permute-start | bytes 393224 | tf_op jit(solution)/shard_map/ppermute | solution.py:375
  147.8 10.3 %collective-permute-start.52 = (bf16[256,256]{1,0:T(8,128)(2,1)S(1)}, bf16[256,256]{1,0:T(8,128)(2,1)S(1)}, u32[]{:S(2)}, u32[]{:S(2)}) collective-permute-start(bf16[256,256]{1,0:T(8,128)(2,1)S(1)} %add_convert_fusion.3), channel_id=1, source_target_pairs={{0,2},{1,3},{2,0},{3,1},{4,6},{5,7},{6,4},{7,5},{8,10},{9,11},{10,... | collective-permute-start | bytes 393224 | tf_op jit(solution)/shard_map/ppermute | solution.py:375
  148.0 11.8 %collective-permute-start.40 = (bf16[96,256]{1,0:T(8,128)(2,1)S(1)}, bf16[96,256]{1,0:T(8,128)(2,1)S(1)}, u32[]{:S(2)}, u32[]{:S(2)}) collective-permute-start(bf16[96,256]{1,0:T(8,128)(2,1)S(1)} %get-tuple-element.98), channel_id=1, source_target_pairs={{0,24},{8,16},{16,8},{24,0},{1,25},{9,17},{17,9},{25,1},{2,26},{10... | collective-permute-start | bytes 147464 | tf_op jit(solution)/shard_map/ppermute | solution.py:370
  148.7 13.0 %collective-permute-start.41 = (bf16[96,256]{1,0:T(8,128)(2,1)S(1)}, bf16[96,256]{1,0:T(8,128)(2,1)S(1)}, u32[]{:S(2)}, u32[]{:S(2)}) collective-permute-start(bf16[96,256]{1,0:T(8,128)(2,1)S(1)} %get-tuple-element.100), channel_id=1, source_target_pairs={{0,8},{8,0},{16,24},{24,16},{1,9},{9,1},{17,25},{25,17},{2,10},{10... | collective-permute-start | bytes 147464 | tf_op jit(solution)/shard_map/ppermute | solution.py:370
  166.7 12.4 %collective-permute-start.56 = (bf16[4,256,256]{2,1,0:T(8,128)(2,1)S(1)}, bf16[4,256,256]{2,1,0:T(8,128)(2,1)S(1)}, u32[]{:S(2)}, u32[]{:S(2)}) collective-permute-start(bf16[4,256,256]{2,1,0:T(8,128)(2,1)S(1)} %pad_maximum_fusion.2.gathered_ref), channel_id=1, source_target_pairs={{0,1},{1,0},{2,3},{3,2},{4,5},{5,4},{6,7},{7,6},{8,9},{9,8},{10,11... | collective-permute-start | bytes 1572872 | tf_op jit(solution)/shard_map/ppermute | solution.py:375
  (63 other events, 746.6 us)

commit v3 on v2

--- a/solution.py
+++ b/solution.py
@@ -79,35 +79,25 @@
     state, ups, downs, projected, state_sem, up_sems, down_sems = rest[2 + len(counts) :]
     section, tile, core, zone = position()
     layers, halves, half = ups.shape[:3]
-    alone = parts["x_up_own"].shape[0]
-    shared = half - 2 * alone
+    window = parts["x_up_window"].shape[0]
+    alone = half - window
     block_rows = tiles_ref.shape[1]
 
     load_state = pltpu.make_async_copy(cams_ref.at[section], state, state_sem)
     load_state.start()
 
-    def at_own(kind, name, far, number):
+    def windowed(kind, name, far, number):
         return (
-            (kind, name, 0, alone, pl.multiple_of(zone * alone, 16)),
-            (kind, far, number * alone, alone, pl.multiple_of((1 - zone) * alone, 16)),
+            (kind, name, 0, window, pl.multiple_of(zone * alone, 16)),
+            (kind, far, number * alone, alone, pl.multiple_of((1 - zone) * window, 16)),
         )
 
     where = {
-        "x": (
-            *at_own("up", "x_up_own", "first_far", 0),
-            ("down", "x_pack", 0, half, 0),
-            ("up", "x_pack", half, shared, 2 * alone),
-        ),
-        "y": (
-            *at_own("down", "y_down_own", "first_far", 1),
-            ("up", "y_pack", 0, half, 0),
-            ("down", "y_pack", half, shared, 2 * alone),
-        ),
+        "x": (*windowed("up", "x_up_window", "first_far", 0), ("down", "x_down", 0, half, 0)),
+        "y": (*windowed("down", "y_down_window", "first_far", 1), ("up", "y_up", 0, half, 0)),
         "d": (
-            *at_own("up", "d_up_own", "second_far", 0),
-            *at_own("down", "d_down_own", "second_far", 1),
-            ("up", "d_shared", 0, shared, 2 * alone),
-            ("down", "d_shared", shared, shared, 2 * alone),
+            *windowed("up", "d_up_window", "second_far", 0),
+            *windowed("down", "d_down_window", "second_far", 1),
         ),
     }
     held = {"up": (ups, up_sems), "down": (downs, down_sems)}
@@ -146,10 +136,12 @@
         normed = (widened * scaling).astype(jnp.bfloat16)
         pltpu.make_async_copy(ups.at[layer], ups.at[layer], up_sems.at[layer]).wait()
         pltpu.make_async_copy(downs.at[layer], downs.at[layer], down_sems.at[layer]).wait()
+        hidden = [
+            gelu(plain(normed, ups[layer, at])).astype(jnp.bfloat16) for at in range(halves)
+        ]
         total = widened
         for at in range(halves):
-            hidden = gelu(plain(normed, ups[layer, at])).astype(jnp.bfloat16)
-            total = total + plain(hidden, downs[layer, at])
+            total = total + plain(hidden[at], downs[layer, at])
         state[...] = total.astype(jnp.bfloat16)
     encoded_ref[...] = state[...]
     projected[...] = plain(state[...], proj_ref[...]).astype(jnp.bfloat16)
@@ -417,65 +409,58 @@
     )(up, down)
 
 
+def pick_missing(upper, lower, alone):
+    zone = position()[3]
+    return jnp.concatenate(
+        [
+            jnp.where(zone == 0, array[:alone], array[array.shape[0] - alone :])
+            for array in (upper, lower)
+        ]
+    )
+
+
 def gather_layers(own_up, own_down, dst_block):
     half = own_down.shape[0] // 2
-    shared = half // 8 // 16 * 16
-    alone = (half - shared) // 2
+    alone = half * 2 // 5 // 16 * 16
+    window = half - alone
     x_up, y_down = cut(
         own_up,
         own_down,
-        (("up", 0, alone, alone, (0, 0)), ("down", 0, alone, alone, (1, 0))),
-        (alone, alone),
-    )
-    down_pack, up_pack, both_shared = cut(
-        own_up,
-        own_down,
-        (
-            ("down", 0, 0, half, (0, 0)),
-            ("up", 2 * alone, 0, shared, (0, half)),
-            ("up", 0, 0, half, (1, 0)),
-            ("down", 2 * alone, 0, shared, (1, half)),
-            ("up", 2 * alone, 0, shared, (2, 0)),
-            ("down", 2 * alone, 0, shared, (2, shared)),
-        ),
-        (half + shared, half + shared, 2 * shared),
-    )
-    x_up = to_section(x_up, 1)
-    y_down = to_section(y_down, 2)
-    table, both_shared = lax.optimization_barrier((dst_block, both_shared))
+        (("up", 0, alone, window, (0, 0)), ("down", 0, alone, window, (1, 0))),
+        (window, window),
+    )
+    table, x_up = lax.optimization_barrier((dst_block, x_up))
     flip = 1
     while flip < lax.axis_size("tile"):
         table = jnp.concatenate([table, to_tile(table, flip)])
         flip *= 2
-    x_up, y_down, both_shared, table = lax.optimization_barrier(
-        (x_up, y_down, both_shared, table)
-    )
+    table, own_up, own_down = lax.optimization_barrier((table, own_up, own_down))
+    down, up = cut(
+        own_up, own_down, (("down", 0, 0, half, (0, 0)), ("up", 0, 0, half, (1, 0))), (half, half)
+    )
+    x_up = to_section(x_up, 1)
+    y_down = to_section(y_down, 2)
+    x_up, y_down, up, down = lax.optimization_barrier((x_up, y_down, up, down))
     d_down = to_section(y_down, 1)
     d_up = to_section(x_up, 2)
-    first_far = to_tile(jnp.concatenate([x_up, y_down]), 2)
-    d_shared = to_section(both_shared, 3)
-    d_up, d_down, down_pack, up_pack = lax.optimization_barrier(
-        (d_up, d_down, down_pack, up_pack)
-    )
-    first_far, second_sent = lax.optimization_barrier(
-        (first_far, jnp.concatenate([d_up, d_down]))
-    )
-    second_far = to_tile(second_sent, 2)
-    x_pack = to_section(down_pack, 1)
-    y_pack = to_section(up_pack, 2)
-    x_pack, y_pack, second_far = lax.optimization_barrier((x_pack, y_pack, second_far))
-    parts = {
-        "x_up_own": x_up,
-        "y_down_own": y_down,
-        "d_shared": d_shared,
-        "first_far": first_far,
-        "d_up_own": d_up,
-        "d_down_own": d_down,
-        "x_pack": x_pack,
-        "y_pack": y_pack,
-        "second_far": second_far,
-    }
+    first_far = to_tile(pick_missing(x_up, y_down, alone), 2)
+    other_x_up = to_tile(x_up, 1)
+    other_y_down = to_tile(y_down, 1)
+    other_x_up, other_y_down, down, up = lax.optimization_barrier(
+        (other_x_up, other_y_down, down, up)
+    )
+    x_down = to_section(down, 1)
+    y_up = to_section(up, 2)
+    first_far, d_up, d_down = lax.optimization_barrier((first_far, d_up, d_down))
+    second_far = to_tile(pick_missing(d_up, d_down, alone), 2)
+    parts = {"first_far": first_far, "d_up_window": d_up, "d_down_window": d_down}
     parts.update({"other_" + name: to_tile(part, 1) for name, part in parts.items()})
+    last = {"x_down": x_down, "y_up": y_up, "second_far": second_far}
+    parts, last = lax.optimization_barrier((parts, last))
+    parts.update(last)
+    parts.update({"other_" + name: to_tile(part, 1) for name, part in last.items()})
+    parts.update({"x_up_window": x_up, "y_down_window": y_down})
+    parts.update({"other_x_up_window": other_x_up, "other_y_down_window": other_y_down})
     return parts, table
 
 
@@ -498,12 +483,12 @@
     return (pick(section), *[to_section(pick(section ^ flip), flip) for flip in (3, 1, 2)])
 
 
-def chips_shares(share):
-    chips = lax.axis_size("tile") // 2
-    if chips == 4:
-        return (share, *[to_tile(share, 2 * flip) for flip in (2, 3, 1)])
-    groups = [[2 * chip + side for chip in range(chips)] for side in (0, 1)]
-    return (lax.psum(share, "tile", axis_index_groups=groups),)
+def chips_total(share):
+    flip = 2
+    while flip < lax.axis_size("tile"):
+        share = add_up(share, to_tile(share, flip))
+        flip *= 2
+    return share
 
 
 def section_shares(share):
@@ -574,16 +559,17 @@
     def cross(sent):
         if not small:
             return [lax.all_to_all(sent[0], "tile", split_axis=0, concat_axis=0, tiled=True)]
-        moved = {0: sent[0]}
-        for flip in (2, 3, 1):
-            moved[flip] = to_tile(sent[flip], 2 * flip)
-        return [moved[flip] for flip in range(4)]
+        over_near = to_tile(sent[0][1:], 1)
+        moved = {flip: to_tile(sent[flip], 2 * flip) for flip in (2, 3)}
+        over_near, nearest = lax.optimization_barrier((over_near, sent[1]))
+        moved[1] = to_tile(nearest, 2)
+        return [sent[0], over_near, *[moved[flip] for flip in (1, 2, 3)]]
 
     def over(moved):
         if not small:
             return moved
-        found = []
-        for part in moved:
+        found = moved[:2]
+        for part in moved[2:]:
             found += [part, to_tile(part[1:], 1)]
         return found
 
@@ -604,20 +590,19 @@
     head_shares = section_share(gradients, section, core)
     moved, head_shares = lax.optimization_barrier((moved, head_shares))
     returned = over(moved)
-    head_shares = chips_shares(add_up(*head_shares))
+    head_total = chips_total(add_up(*head_shares))
     grad_proj = proj_grad(
         src_block[0], live[0], frustum_tiles[0], encoded, returned, singles
     )
-    proj_shares = section_share(grad_proj, section, core)
-    proj_shares = chips_shares(add_up(*proj_shares))
-    head_shares = section_shares(add_up(*head_shares))
-    proj_shares = section_shares(add_up(*proj_shares))
-    head_shares = with_other_core(head_shares)
+    proj_total = chips_total(add_up(*section_share(grad_proj, section, core)))
+    head_shares = with_other_core(section_shares(head_total))
+    proj_shares = section_shares(proj_total)
     grads = unpack(
         *head_shares,
         (render_up.shape, render_down.shape, decode_up.shape, decode_down.shape),
     )
-    (grad_proj,) = unpack(*with_other_core(proj_shares), (proj.shape,))
+    grads, proj_shares = lax.optimization_barrier((grads, with_other_core(proj_shares)))
+    (grad_proj,) = unpack(*proj_shares, (proj.shape,))
     return (prediction[None], grad_proj, *grads)
 
 

time: 181 us -> 173 us (0.956)
  starting transfers between devices: 52.6 us -> 42.1 us
  waiting for transfers between devices: 87.8 us -> 93.6 us
  local copies, waits for them, and re-layouts: 6 us -> 3.99 us
    ppermute x38 -> x35, starting transfers between devices: 31.5 us -> 20.2 us  [to_tile(): return lax.ppermute(array, 'tile', [(at, at ^ flip) for at in range(count)])]
    ppermute x38 -> x35, waiting for transfers between devices: 49.3 us -> 60.1 us  [to_tile(): return lax.ppermute(array, 'tile', [(at, at ^ flip) for at in range(count)])]
    ppermute x19 -> x18, waiting for transfers between devices: 38.5 us -> 33.5 us  [to_section(): lax.ppermute(array, 'section', [(at, at ^ flip) for at in range(count)])]
    unnamed x60, local copies, waits for them, and re-layouts: 5.83 us -> 3.81 us
    ppermute x19 -> x18, starting transfers between devices: 21.1 us -> 21.9 us  [to_section(): lax.ppermute(array, 'section', [(at, at ^ flip) for at in range(count)])]
  transfers between devices with their start and end apart: 57 -> 53, of which waited for: 30 -> 32; matrix products, arithmetic and copies ran while one was open for 1% -> 0% of each run, Pallas kernels for 2% -> 3%
where the time goes in v3:
time: 173 us; the launch traced here: 172 us
  waiting for transfers between devices  93.6 us (54%)
  starting transfers between devices  42.1 us (24%)
  Pallas kernels  30.8 us (18%)
  local copies, waits for them, and re-layouts  3.99 us (2%)
    ppermute x35, waiting for transfers between devices, to_tile(): return lax.ppermute(array, 'tile', [(at, at ^ flip) for at in range(count)])  60.1 us
    ppermute x18, waiting for transfers between devices, to_section(): lax.ppermute(array, 'section', [(at, at ^ flip) for at in range(count)])  33.5 us
    ppermute x18, starting transfers between devices, to_section(): lax.ppermute(array, 'section', [(at, at ^ flip) for at in range(count)])  21.9 us
    ppermute x35, starting transfers between devices, to_tile(): return lax.ppermute(array, 'tile', [(at, at ^ flip) for at in range(count)])  20.2 us
    pallas_call x1, Pallas kernels, encode(): pl.pallas_call(functools.partial(encode_kernel, names, counts), out_shape...  16.5 us
    pallas_call x2, Pallas kernels, cut(): pl.pallas_call(functools.partial(cut_kernel, (plan,)), out_shape=tuple((j...  5.53 us
    pallas_call x1, Pallas kernels, heads(): pl.pallas_call(functools.partial(heads_kernel, counts, back_counts, scale...  5.08 us
    unnamed x60, local copies, waits for them, and re-layouts  3.81 us
  transfers between devices with their start and end apart: 53, of which 32 were waited for; matrix products, arithmetic and copies ran while one was open for 0% of the time, Pallas kernels for 3%

profile of v3, /device:TPU:0, one launch (start us, length us, event | category | flops | bytes accessed | tf_op | source)
XLA Modules:
  0.0 172.5 jit_solution(1394592547504013548)
XLA Ops:
  0.6 2.4 %cut.2 = (bf16[464,768]{1,0:T(8,128)(2,1)}, bf16[464,768]{1,0:T(8,128)(2,1)}) custom-call(bf16[768,1536]{1,0:T(8,128)(2,1)} %bitcast.39, bf16[1536,768]{1,0:T(8,128)(2,1)} %bitcast.42), custom_call_target="tpu_custom_call" | custom-call | tf_op jit(solution)/shard_map/cut/pallas_call | solution.py:401
  3.1 3.0 %collective-permute-start.3 = (bf16[464,768]{1,0:T(8,128)(2,1)}, bf16[464,768]{1,0:T(8,128)(2,1)S(1)}, u32[]{:S(2)}, u32[]{:S(2)}) collective-permute-start(bf16[464,768]{1,0:T(8,128)(2,1)} %get-tuple-element.73), channel_id=1, source_target_pairs={{0,8},{8,0},{16,24},{24,16},{1,9},{9,1},{17,25},{25,17},{2,10},{10... | collective-permute-start | bytes 2138120 | tf_op jit(solution)/shard_map/ppermute | solution.py:362
  8.8 1.6 collective-permute-start.1
  10.4 2.0 %collective-permute-done.1 = s32[2,8]{1,0:T(2,128)S(1)} collective-permute-done((s32[2,8]{1,0:T(2,128)S(1)}, s32[2,8]{1,0:T(2,128)S(1)}, u32[]{:S(2)}, u32[]{:S(2)}) %collective-permute-start.1) | collective-permute-done | bytes 96 | tf_op jit(solution)/shard_map/ppermute | solution.py:367
  12.4 2.7 %collective-permute-start.2 = (s32[4,8]{1,0:T(4,128)S(1)}, s32[4,8]{1,0:T(4,128)S(1)}, u32[]{:S(2)}, u32[]{:S(2)}) collective-permute-start(s32[4,8]{1,0:T(4,128)S(1)} %pad_add_fusion.1), channel_id=1, source_target_pairs={{0,4},{1,5},{2,6},{3,7},{4,0},{5,1},{6,2},{7,3},{8,12},{9,13},{10,... | collective-permute-start | bytes 392 | tf_op jit(solution)/shard_map/ppermute | solution.py:367
  15.0 1.9 %collective-permute-done.2 = s32[4,8]{1,0:T(4,128)S(1)} collective-permute-done((s32[4,8]{1,0:T(4,128)S(1)}, s32[4,8]{1,0:T(4,128)S(1)}, u32[]{:S(2)}, u32[]{:S(2)}) %collective-permute-start.2) | collective-permute-done | bytes 160 | tf_op jit(solution)/shard_map/ppermute | solution.py:367
  17.0 3.1 %cut.3 = (bf16[768,768]{1,0:T(8,128)(2,1)}, bf16[768,768]{1,0:T(8,128)(2,1)}) custom-call(bf16[768,1536]{1,0:T(8,128)(2,1)} %bitcast.40, bf16[1536,768]{1,0:T(8,128)(2,1)} %bitcast.43), custom_call_target="tpu_custom_call" | custom-call | tf_op jit(solution)/shard_map/cut/pallas_call | solution.py:401
  20.0 2.2 %collective-permute-done.3.rest_12_ = bf16[464,768]{1,0:T(8,128)(2,1)S(1)} collective-permute-done((bf16[464,768]{1,0:T(8,128)(2,1)}, bf16[464,768]{1,0:T(8,128)(2,1)S(1)}, u32[]{:S(2)}, u32[]{:S(2)}) %collective-permute-start.3) | collective-permute-done | bytes 712736 | tf_op jit(solution)/shard_map/ppermute | solution.py:362
  24.0 1.6 collective-permute-start.5
  30.9 14.1 %collective-permute-done.6.rest_1_ = bf16[464,768]{1,0:T(8,128)(2,1)S(1)} collective-permute-done((bf16[464,768]{1,0:T(8,128)(2,1)S(1)}, bf16[464,768]{1,0:T(8,128)(2,1)S(1)}, u32[]{:S(2)}, u32[]{:S(2)}) %collective-permute-start.6) | collective-permute-done | bytes 712736 | tf_op jit(solution)/shard_map/ppermute | solution.py:362
  48.9 2.2 %collective-permute-done.9.rest_4_ = bf16[464,768]{1,0:T(8,128)(2,1)S(1)} collective-permute-done((bf16[464,768]{1,0:T(8,128)(2,1)S(1)}, bf16[464,768]{1,0:T(8,128)(2,1)S(1)}, u32[]{:S(2)}, u32[]{:S(2)}) %collective-permute-start.9) | collective-permute-done | bytes 712736 | tf_op jit(solution)/shard_map/ppermute | solution.py:367
  51.1 18.9 %collective-permute-done.11.rest_6_ = bf16[608,768]{1,0:T(8,128)(2,1)S(1)} collective-permute-done((bf16[608,768]{1,0:T(8,128)(2,1)S(1)}, bf16[608,768]{1,0:T(8,128)(2,1)S(1)}, u32[]{:S(2)}, u32[]{:S(2)}) %collective-permute-start.11) | collective-permute-done | bytes 933920 | tf_op jit(solution)/shard_map/ppermute | solution.py:367
  71.2 5.3 %collective-permute-done.16.rest_9_ = bf16[608,768]{1,0:T(8,128)(2,1)S(1)} collective-permute-done((bf16[608,768]{1,0:T(8,128)(2,1)S(1)}, bf16[608,768]{1,0:T(8,128)(2,1)S(1)}, u32[]{:S(2)}, u32[]{:S(2)}) %collective-permute-start.16) | collective-permute-done | bytes 933920 | tf_op jit(solution)/shard_map/ppermute | solution.py:367
  78.3 16.5 %encode.1 = (bf16[512,768]{1,0:T(8,128)(2,1)}, s32[8]{0:T(128)S(1)}, bf16[2,128,256]{2,1,0:T(8,128)(2,1)S(1)}, bf16[2,128,256]{2,1,0:T(8,128)(2,1)S(1)}, bf16[2,...) custom-call(s32[8]{0:T(128)S(1)} %bitcast.35, s32[8]{0:T(128)S(1)} %bitcast.37, ...), custom_call_target="tpu_custom_call" | custom-call | tf_op jit(solution)/shard_map/encode/pallas_call | solution.py:178
  95.0 2.6 %collective-permute-start.22 = (bf16[2,128,256]{2,1,0:T(8,128)(2,1)S(1)}, bf16[2,128,256]{2,1,0:T(8,128)(2,1)S(1)}, u32[]{:S(2)}, u32[]{:S(2)}) collective-permute-start(bf16[2,128,256]{2,1,0:T(8,128)(2,1)S(1)} %get-tuple-element.104), channel_id=1, source_target_pairs={{0,4},{1,5},{2,6},{3,7},{4,0},{5,1},{6,2},{7,3},{8,12},{9,13},{10,... | collective-permute-start | bytes 393224 | tf_op jit(solution)/shard_map/ppermute | solution.py:367
  98.5 8.8 %collective-permute-done.22.rest_4_ = bf16[2,128,256]{2,1,0:T(8,128)(2,1)S(1)} collective-permute-done((bf16[2,128,256]{2,1,0:T(8,128)(2,1)S(1)}, bf16[2,128,256]{2,1,0:T(8,128)(2,1)S(1)}, u32[]{:S(2)}, u32[]{:S(2)}) %collective-permute-start.22) | collective-permute-done | bytes 131104 | tf_op jit(solution)/shard_map/ppermute | solution.py:367
  111.4 5.1 %heads.1 = (bf16[640,256]{1,0:T(8,128)(2,1)}, bf16[8,256,256]{2,1,0:T(8,128)(2,1)S(1)}, bf16[2,128,256]{2,1,0:T(8,128)(2,1)S(1)}, bf16[2,128,256]{2,1,0:T(8,128)...) custom-call(s32[8]{0:T(128)S(1)} %get-tuple-element.99.targets_ref, ...), custom_call_target="tpu_custom_call" | custom-call | tf_op jit(solution)/shard_map/heads/pallas_call | solution.py:297
  117.4 3.5 %collective-permute-start.28 = (bf16[2,128,256]{2,1,0:T(8,128)(2,1)}, bf16[2,128,256]{2,1,0:T(8,128)(2,1)S(1)}, u32[]{:S(2)}, u32[]{:S(2)}) collective-permute-start(bf16[2,128,256]{2,1,0:T(8,128)(2,1)} %copy-done.14), channel_id=1, source_target_pairs={{0,4},{1,5},{2,6},{3,7},{4,0},{5,1},{6,2},{7,3},{8,12},{9,13},{10,... | collective-permute-start | bytes 393224 | tf_op jit(solution)/shard_map/ppermute | solution.py:367
  124.3 6.8 %collective-permute-done.28.rest_4_ = bf16[2,128,256]{2,1,0:T(8,128)(2,1)S(1)} collective-permute-done((bf16[2,128,256]{2,1,0:T(8,128)(2,1)}, bf16[2,128,256]{2,1,0:T(8,128)(2,1)S(1)}, u32[]{:S(2)}, u32[]{:S(2)}) %collective-permute-start.28) | collective-permute-done | bytes 131104 | tf_op jit(solution)/shard_map/ppermute | solution.py:367
  131.9 4.1 %collective-permute-done.33 = bf16[256,256]{1,0:T(8,128)(2,1)S(1)} collective-permute-done((bf16[256,256]{1,0:T(8,128)(2,1)S(1)}, bf16[256,256]{1,0:T(8,128)(2,1)S(1)}, u32[]{:S(2)}, u32[]{:S(2)}) %collective-permute-start.33) | collective-permute-done | bytes 131104 | tf_op jit(solution)/shard_map/ppermute | solution.py:362
  148.0 5.9 %collective-permute-done.35 = bf16[256,256]{1,0:T(8,128)(2,1)S(1)} collective-permute-done((bf16[256,256]{1,0:T(8,128)(2,1)S(1)}, bf16[256,256]{1,0:T(8,128)(2,1)S(1)}, u32[]{:S(2)}, u32[]{:S(2)}) %collective-permute-start.35) | collective-permute-done | bytes 131104 | tf_op jit(solution)/shard_map/ppermute | solution.py:367
  155.3 2.2 %collective-permute-start.38 = (bf16[256,256]{1,0:T(8,128)(2,1)S(1)}, bf16[256,256]{1,0:T(8,128)(2,1)S(1)}, u32[]{:S(2)}, u32[]{:S(2)}) collective-permute-start(bf16[256,256]{1,0:T(8,128)(2,1)S(1)} %add_convert_fusion.2), channel_id=1, source_target_pairs={{0,24},{8,16},{16,8},{24,0},{1,25},{9,17},{17,9},{25,1},{2,26},{10... | collective-permute-start | bytes 393224 | tf_op jit(solution)/shard_map/ppermute | solution.py:362
  157.7 2.8 %collective-permute-done.36 = bf16[256,256]{1,0:T(8,128)(2,1)S(1)} collective-permute-done((bf16[256,256]{1,0:T(8,128)(2,1)S(1)}, bf16[256,256]{1,0:T(8,128)(2,1)S(1)}, u32[]{:S(2)}, u32[]{:S(2)}) %collective-permute-start.36) | collective-permute-done | bytes 131104 | tf_op jit(solution)/shard_map/ppermute | solution.py:362
  160.4 2.1 %collective-permute-done.37 = bf16[256,256]{1,0:T(8,128)(2,1)S(1)} collective-permute-done((bf16[256,256]{1,0:T(8,128)(2,1)S(1)}, bf16[256,256]{1,0:T(8,128)(2,1)S(1)}, u32[]{:S(2)}, u32[]{:S(2)}) %collective-permute-start.37) | collective-permute-done | bytes 131104 | tf_op jit(solution)/shard_map/ppermute | solution.py:362
  (179 shorter events, 49.8 us)
Async XLA Ops:
  3.1 19.2 %collective-permute-start.3 = (bf16[464,768]{1,0:T(8,128)(2,1)}, bf16[464,768]{1,0:T(8,128)(2,1)S(1)}, u32[]{:S(2)}, u32[]{:S(2)}) collective-permute-start(bf16[464,768]{1,0:T(8,128)(2,1)} %get-tuple-element.73), channel_id=1, source_target_pairs={{0,8},{8,0},{16,24},{24,16},{1,9},{9,1},{17,25},{25,17},{2,10},{10... | collective-permute-start | bytes 2138120 | tf_op jit(solution)/shard_map/ppermute | solution.py:362
  6.1 17.6 %collective-permute-start.4 = (bf16[464,768]{1,0:T(8,128)(2,1)}, bf16[464,768]{1,0:T(8,128)(2,1)S(1)}, u32[]{:S(2)}, u32[]{:S(2)}) collective-permute-start(bf16[464,768]{1,0:T(8,128)(2,1)} %get-tuple-element.74), channel_id=1, source_target_pairs={{0,16},{8,24},{16,0},{24,8},{1,17},{9,25},{17,1},{25,9},{2,18},{10... | collective-permute-start | bytes 2138120 | tf_op jit(solution)/shard_map/ppermute | solution.py:362
  24.0 22.5 %collective-permute-start.5 = (bf16[608,768]{1,0:T(8,128)(2,1)S(1)}, bf16[608,768]{1,0:T(8,128)(2,1)S(1)}, u32[]{:S(2)}, u32[]{:S(2)}) collective-permute-start(bf16[608,768]{1,0:T(8,128)(2,1)S(1)} %pad_maximum_fusion), channel_id=1, source_target_pairs={{0,2},{1,3},{2,0},{3,1},{4,6},{5,7},{6,4},{7,5},{8,10},{9,11},{10,... | collective-permute-start | bytes 2801672 | tf_op jit(solution)/shard_map/ppermute | solution.py:367
  26.1 18.8 %collective-permute-start.6 = (bf16[464,768]{1,0:T(8,128)(2,1)S(1)}, bf16[464,768]{1,0:T(8,128)(2,1)S(1)}, u32[]{:S(2)}, u32[]{:S(2)}) collective-permute-start(bf16[464,768]{1,0:T(8,128)(2,1)S(1)} %collective-permute-done.3.rest_12_), channel_id=1, source_target_pairs={{0,16},{8,24},{16,0},{24,8},{1,17},{9,25},{17,1},{25,9},{2,18},{10... | collective-permute-start | bytes 2138120 | tf_op jit(solution)/shard_map/ppermute | solution.py:362
  27.6 18.9 %collective-permute-start.7 = (bf16[464,768]{1,0:T(8,128)(2,1)S(1)}, bf16[464,768]{1,0:T(8,128)(2,1)S(1)}, u32[]{:S(2)}, u32[]{:S(2)}) collective-permute-start(bf16[464,768]{1,0:T(8,128)(2,1)S(1)} %collective-permute-done.4.rest_13_), channel_id=1, source_target_pairs={{0,8},{8,0},{16,24},{24,16},{1,9},{9,1},{17,25},{25,17},{2,10},{10... | collective-permute-start | bytes 2138120 | tf_op jit(solution)/shard_map/ppermute | solution.py:362
  28.8 41.7 %collective-permute-start.14 = (bf16[768,768]{1,0:T(8,128)(2,1)S(1)}, bf16[768,768]{1,0:T(8,128)(2,1)S(1)}, u32[]{:S(2)}, u32[]{:S(2)}) collective-permute-start(bf16[768,768]{1,0:T(8,128)(2,1)S(1)} %copy-done.29), channel_id=1, source_target_pairs={{0,8},{8,0},{16,24},{24,16},{1,9},{9,1},{17,25},{25,17},{2,10},{10... | collective-permute-start | bytes 3538952 | tf_op jit(solution)/shard_map/ppermute | solution.py:362
  29.8 40.7 %collective-permute-start.15 = (bf16[768,768]{1,0:T(8,128)(2,1)S(1)}, bf16[768,768]{1,0:T(8,128)(2,1)S(1)}, u32[]{:S(2)}, u32[]{:S(2)}) collective-permute-start(bf16[768,768]{1,0:T(8,128)(2,1)S(1)} %copy-done.28), channel_id=1, source_target_pairs={{0,16},{8,24},{16,0},{24,8},{1,17},{9,25},{17,1},{25,9},{2,18},{10... | collective-permute-start | bytes 3538952 | tf_op jit(solution)/shard_map/ppermute | solution.py:362
  46.8 23.2 %collective-permute-start.11 = (bf16[608,768]{1,0:T(8,128)(2,1)S(1)}, bf16[608,768]{1,0:T(8,128)(2,1)S(1)}, u32[]{:S(2)}, u32[]{:S(2)}) collective-permute-start(bf16[608,768]{1,0:T(8,128)(2,1)S(1)} %pad_maximum_fusion.1), channel_id=1, source_target_pairs={{0,2},{1,3},{2,0},{3,1},{4,6},{5,7},{6,4},{7,5},{8,10},{9,11},{10,... | collective-permute-start | bytes 2801672 | tf_op jit(solution)/shard_map/ppermute | solution.py:367
  47.4 22.6 %collective-permute-start.10 = (bf16[608,768]{1,0:T(8,128)(2,1)S(1)}, bf16[608,768]{1,0:T(8,128)(2,1)S(1)}, u32[]{:S(2)}, u32[]{:S(2)}) collective-permute-start(bf16[608,768]{1,0:T(8,128)(2,1)S(1)} %collective-permute-done.5.rest_2_), channel_id=1, source_target_pairs={{0,1},{1,0},{2,3},{3,2},{4,5},{5,4},{6,7},{7,6},{8,9},{9,8},{10,11... | collective-permute-start | bytes 2801672 | tf_op jit(solution)/shard_map/ppermute | solution.py:367
  70.5 5.9 %collective-permute-start.17 = (bf16[768,768]{1,0:T(8,128)(2,1)S(1)}, bf16[768,768]{1,0:T(8,128)(2,1)S(1)}, u32[]{:S(2)}, u32[]{:S(2)}) collective-permute-start(bf16[768,768]{1,0:T(8,128)(2,1)S(1)} %collective-permute-done.14.rest_7_), channel_id=1, source_target_pairs={{0,1},{1,0},{2,3},{3,2},{4,5},{5,4},{6,7},{7,6},{8,9},{9,8},{10,11... | collective-permute-start | bytes 3538952 | tf_op jit(solution)/shard_map/ppermute | solution.py:367
  95.0 12.3 %collective-permute-start.22 = (bf16[2,128,256]{2,1,0:T(8,128)(2,1)S(1)}, bf16[2,128,256]{2,1,0:T(8,128)(2,1)S(1)}, u32[]{:S(2)}, u32[]{:S(2)}) collective-permute-start(bf16[2,128,256]{2,1,0:T(8,128)(2,1)S(1)} %get-tuple-element.104), channel_id=1, source_target_pairs={{0,4},{1,5},{2,6},{3,7},{4,0},{5,1},{6,2},{7,3},{8,12},{9,13},{10,... | collective-permute-start | bytes 393224 | tf_op jit(solution)/shard_map/ppermute | solution.py:367
  97.6 9.7 %collective-permute-start.24 = (bf16[2,128,256]{2,1,0:T(8,128)(2,1)S(1)}, bf16[2,128,256]{2,1,0:T(8,128)(2,1)S(1)}, u32[]{:S(2)}, u32[]{:S(2)}) collective-permute-start(bf16[2,128,256]{2,1,0:T(8,128)(2,1)S(1)} %get-tuple-element.105), channel_id=1, source_target_pairs={{0,6},{1,7},{2,4},{3,5},{4,2},{5,3},{6,0},{7,1},{8,14},{9,15},{10,... | collective-permute-start | bytes 393224 | tf_op jit(solution)/shard_map/ppermute | solution.py:367
  97.8 10.8 %collective-permute-start.20 = (bf16[2,128,256]{2,1,0:T(8,128)(2,1)S(1)}, bf16[2,128,256]{2,1,0:T(8,128)(2,1)S(1)}, u32[]{:S(2)}, u32[]{:S(2)}) collective-permute-start(bf16[2,128,256]{2,1,0:T(8,128)(2,1)S(1)} %get-tuple-element.103), channel_id=1, source_target_pairs={{0,2},{1,3},{2,0},{3,1},{4,6},{5,7},{6,4},{7,5},{8,10},{9,11},{10,... | collective-permute-start | bytes 393224 | tf_op jit(solution)/shard_map/ppermute | solution.py:367
  117.4 13.7 %collective-permute-start.28 = (bf16[2,128,256]{2,1,0:T(8,128)(2,1)}, bf16[2,128,256]{2,1,0:T(8,128)(2,1)S(1)}, u32[]{:S(2)}, u32[]{:S(2)}) collective-permute-start(bf16[2,128,256]{2,1,0:T(8,128)(2,1)} %copy-done.14), channel_id=1, source_target_pairs={{0,4},{1,5},{2,6},{3,7},{4,0},{5,1},{6,2},{7,3},{8,12},{9,13},{10,... | collective-permute-start | bytes 393224 | tf_op jit(solution)/shard_map/ppermute | solution.py:367
  120.9 10.8 %collective-permute-start.29 = (bf16[2,128,256]{2,1,0:T(8,128)(2,1)}, bf16[2,128,256]{2,1,0:T(8,128)(2,1)S(1)}, u32[]{:S(2)}, u32[]{:S(2)}) collective-permute-start(bf16[2,128,256]{2,1,0:T(8,128)(2,1)} %copy-done.13), channel_id=1, source_target_pairs={{0,6},{1,7},{2,4},{3,5},{4,2},{5,3},{6,0},{7,1},{8,14},{9,15},{10,... | collective-permute-start | bytes 393224 | tf_op jit(solution)/shard_map/ppermute | solution.py:367
  122.1 9.8 %collective-permute-start.27 = (bf16[2,128,256]{2,1,0:T(8,128)(2,1)}, bf16[2,128,256]{2,1,0:T(8,128)(2,1)S(1)}, u32[]{:S(2)}, u32[]{:S(2)}) collective-permute-start(bf16[2,128,256]{2,1,0:T(8,128)(2,1)} %copy-done.12), channel_id=1, source_target_pairs={{0,2},{1,3},{2,0},{3,1},{4,6},{5,7},{6,4},{7,5},{8,10},{9,11},{10,... | collective-permute-start | bytes 393224 | tf_op jit(solution)/shard_map/ppermute | solution.py:367
  122.3 9.6 %collective-permute-start.31 = (bf16[256,256]{1,0:T(8,128)(2,1)S(1)}, bf16[256,256]{1,0:T(8,128)(2,1)S(1)}, u32[]{:S(2)}, u32[]{:S(2)}) collective-permute-start(bf16[256,256]{1,0:T(8,128)(2,1)S(1)} %get-tuple-element.136), channel_id=1, source_target_pairs={{0,24},{8,16},{16,8},{24,0},{1,25},{9,17},{17,9},{25,1},{2,26},{10... | collective-permute-start | bytes 393224 | tf_op jit(solution)/shard_map/ppermute | solution.py:362
  122.6 9.3 %collective-permute-start.32 = (bf16[256,256]{1,0:T(8,128)(2,1)S(1)}, bf16[256,256]{1,0:T(8,128)(2,1)S(1)}, u32[]{:S(2)}, u32[]{:S(2)}) collective-permute-start(bf16[256,256]{1,0:T(8,128)(2,1)S(1)} %get-tuple-element.135), channel_id=1, source_target_pairs={{0,8},{8,0},{16,24},{24,16},{1,9},{9,1},{17,25},{25,17},{2,10},{10... | collective-permute-start | bytes 393224 | tf_op jit(solution)/shard_map/ppermute | solution.py:362
  145.3 8.7 %collective-permute-start.35 = (bf16[256,256]{1,0:T(8,128)(2,1)S(1)}, bf16[256,256]{1,0:T(8,128)(2,1)S(1)}, u32[]{:S(2)}, u32[]{:S(2)}) collective-permute-start(bf16[256,256]{1,0:T(8,128)(2,1)S(1)} %add_convert_fusion.3), channel_id=1, source_target_pairs={{0,4},{1,5},{2,6},{3,7},{4,0},{5,1},{6,2},{7,3},{8,12},{9,13},{10,... | collective-permute-start | bytes 393224 | tf_op jit(solution)/shard_map/ppermute | solution.py:367
  147.1 10.5 %collective-permute-start.47 = (bf16[96,256]{1,0:T(8,128)(2,1)S(1)}, bf16[96,256]{1,0:T(8,128)(2,1)S(1)}, u32[]{:S(2)}, u32[]{:S(2)}) collective-permute-start(bf16[96,256]{1,0:T(8,128)(2,1)S(1)} %fusion.2), channel_id=1, source_target_pairs={{0,2},{1,3},{2,0},{3,1},{4,6},{5,7},{6,4},{7,5},{8,10},{9,11},{10,... | collective-permute-start | bytes 147464 | tf_op jit(solution)/shard_map/ppermute | solution.py:367
  154.0 6.4 %collective-permute-start.36 = (bf16[256,256]{1,0:T(8,128)(2,1)S(1)}, bf16[256,256]{1,0:T(8,128)(2,1)S(1)}, u32[]{:S(2)}, u32[]{:S(2)}) collective-permute-start(bf16[256,256]{1,0:T(8,128)(2,1)S(1)} %add_convert_fusion.2), channel_id=1, source_target_pairs={{0,8},{8,0},{16,24},{24,16},{1,9},{9,1},{17,25},{25,17},{2,10},{10... | collective-permute-start | bytes 393224 | tf_op jit(solution)/shard_map/ppermute | solution.py:362
  154.6 7.9 %collective-permute-start.37 = (bf16[256,256]{1,0:T(8,128)(2,1)S(1)}, bf16[256,256]{1,0:T(8,128)(2,1)S(1)}, u32[]{:S(2)}, u32[]{:S(2)}) collective-permute-start(bf16[256,256]{1,0:T(8,128)(2,1)S(1)} %add_convert_fusion.2), channel_id=1, source_target_pairs={{0,16},{8,24},{16,0},{24,8},{1,17},{9,25},{17,1},{25,9},{2,18},{10... | collective-permute-start | bytes 393224 | tf_op jit(solution)/shard_map/ppermute | solution.py:362
  155.3 7.3 %collective-permute-start.38 = (bf16[256,256]{1,0:T(8,128)(2,1)S(1)}, bf16[256,256]{1,0:T(8,128)(2,1)S(1)}, u32[]{:S(2)}, u32[]{:S(2)}) collective-permute-start(bf16[256,256]{1,0:T(8,128)(2,1)S(1)} %add_convert_fusion.2), channel_id=1, source_target_pairs={{0,24},{8,16},{16,8},{24,0},{1,25},{9,17},{17,9},{25,1},{2,26},{10... | collective-permute-start | bytes 393224 | tf_op jit(solution)/shard_map/ppermute | solution.py:362
  162.6 7.5 %collective-permute-start.39 = (bf16[4,256,256]{2,1,0:T(8,128)(2,1)S(1)}, bf16[4,256,256]{2,1,0:T(8,128)(2,1)S(1)}, u32[]{:S(2)}, u32[]{:S(2)}) collective-permute-start(bf16[4,256,256]{2,1,0:T(8,128)(2,1)S(1)} %pad_maximum_fusion.2.gathered_ref), channel_id=1, source_target_pairs={{0,1},{1,0},{2,3},{3,2},{4,5},{5,4},{6,7},{7,6},{8,9},{9,8},{10,11... | collective-permute-start | bytes 1572872 | tf_op jit(solution)/shard_map/ppermute | solution.py:367
  (59 other events, 503.4 us)

commit v4 on v3

--- a/solution.py
+++ b/solution.py
@@ -588,7 +588,9 @@
 
     moved = cross(returns)
     head_shares = section_share(gradients, section, core)
-    moved, head_shares = lax.optimization_barrier((moved, head_shares))
+    *tied, last_share = head_shares
+    moved, tied = lax.optimization_barrier((moved, tied))
+    head_shares = (*tied, last_share)
     returned = over(moved)
     head_total = chips_total(add_up(*head_shares))
     grad_proj = proj_grad(

time: 173 us -> 170 us (0.983)
  waiting for transfers between devices: 93.6 us -> 88.9 us
  starting transfers between devices: 42.1 us -> 44.3 us
    ppermute x18, waiting for transfers between devices: 33.5 us -> 30.3 us  [to_section(): lax.ppermute(array, 'section', [(at, at ^ flip) for at in range(count)])]
    ppermute x35, starting transfers between devices: 20.2 us -> 22.4 us  [to_tile(): return lax.ppermute(array, 'tile', [(at, at ^ flip) for at in range(count)])]
  transfers between devices with their start and end apart: 53 -> 53, of which waited for: 32 -> 31; matrix products, arithmetic and copies ran while one was open for 0% -> 0% of each run, Pallas kernels for 3% -> 3%
where the time goes in v4:
time: 170 us
  waiting for transfers between devices  88.9 us (52%)
  starting transfers between devices  44.3 us (26%)
  Pallas kernels  30.8 us (18%)
  local copies, waits for them, and re-layouts  3.99 us (2%)
    ppermute x35, waiting for transfers between devices, to_tile(): return lax.ppermute(array, 'tile', [(at, at ^ flip) for at in range(count)])  58.5 us
    ppermute x18, waiting for transfers between devices, to_section(): lax.ppermute(array, 'section', [(at, at ^ flip) for at in range(count)])  30.3 us
    ppermute x35, starting transfers between devices, to_tile(): return lax.ppermute(array, 'tile', [(at, at ^ flip) for at in range(count)])  22.4 us
    ppermute x18, starting transfers between devices, to_section(): lax.ppermute(array, 'section', [(at, at ^ flip) for at in range(count)])  21.9 us
    pallas_call x1, Pallas kernels, encode(): pl.pallas_call(functools.partial(encode_kernel, names, counts), out_shape...  16.5 us
    pallas_call x2, Pallas kernels, cut(): pl.pallas_call(functools.partial(cut_kernel, (plan,)), out_shape=tuple((j...  5.53 us
    pallas_call x1, Pallas kernels, heads(): pl.pallas_call(functools.partial(heads_kernel, counts, back_counts, scale...  5.08 us
    unnamed x60, local copies, waits for them, and re-layouts  3.81 us
  transfers between devices with their start and end apart: 53, of which 31 were waited for; matrix products, arithmetic and copies ran while one was open for 0% of the time, Pallas kernels for 3%

profile of v4, /device:TPU:0, one launch (start us, length us, event | category | flops | bytes accessed | tf_op | source)
XLA Modules:
  0.0 170.0 jit_solution(3217859910777892168)
XLA Ops:
  0.6 2.4 %cut.2 = (bf16[464,768]{1,0:T(8,128)(2,1)}, bf16[464,768]{1,0:T(8,128)(2,1)}) custom-call(bf16[768,1536]{1,0:T(8,128)(2,1)} %bitcast.39, bf16[1536,768]{1,0:T(8,128)(2,1)} %bitcast.42), custom_call_target="tpu_custom_call" | custom-call | tf_op jit(solution)/shard_map/cut/pallas_call | solution.py:401
  3.1 3.0 %collective-permute-start.3 = (bf16[464,768]{1,0:T(8,128)(2,1)}, bf16[464,768]{1,0:T(8,128)(2,1)S(1)}, u32[]{:S(2)}, u32[]{:S(2)}) collective-permute-start(bf16[464,768]{1,0:T(8,128)(2,1)} %get-tuple-element.72), channel_id=1, source_target_pairs={{0,8},{8,0},{16,24},{24,16},{1,9},{9,1},{17,25},{25,17},{2,10},{10... | collective-permute-start | bytes 2138120 | tf_op jit(solution)/shard_map/ppermute | solution.py:362
  10.4 2.0 %collective-permute-done.1 = s32[2,8]{1,0:T(2,128)S(1)} collective-permute-done((s32[2,8]{1,0:T(2,128)S(1)}, s32[2,8]{1,0:T(2,128)S(1)}, u32[]{:S(2)}, u32[]{:S(2)}) %collective-permute-start.1) | collective-permute-done | bytes 96 | tf_op jit(solution)/shard_map/ppermute | solution.py:367
  12.4 2.7 %collective-permute-start.2 = (s32[4,8]{1,0:T(4,128)S(1)}, s32[4,8]{1,0:T(4,128)S(1)}, u32[]{:S(2)}, u32[]{:S(2)}) collective-permute-start(s32[4,8]{1,0:T(4,128)S(1)} %pad_add_fusion.1), channel_id=1, source_target_pairs={{0,4},{1,5},{2,6},{3,7},{4,0},{5,1},{6,2},{7,3},{8,12},{9,13},{10,... | collective-permute-start | bytes 392 | tf_op jit(solution)/shard_map/ppermute | solution.py:367
  15.0 1.9 %collective-permute-done.2 = s32[4,8]{1,0:T(4,128)S(1)} collective-permute-done((s32[4,8]{1,0:T(4,128)S(1)}, s32[4,8]{1,0:T(4,128)S(1)}, u32[]{:S(2)}, u32[]{:S(2)}) %collective-permute-start.2) | collective-permute-done | bytes 160 | tf_op jit(solution)/shard_map/ppermute | solution.py:367
  17.0 3.1 %cut.3 = (bf16[768,768]{1,0:T(8,128)(2,1)}, bf16[768,768]{1,0:T(8,128)(2,1)}) custom-call(bf16[768,1536]{1,0:T(8,128)(2,1)} %bitcast.40, bf16[1536,768]{1,0:T(8,128)(2,1)} %bitcast.43), custom_call_target="tpu_custom_call" | custom-call | tf_op jit(solution)/shard_map/cut/pallas_call | solution.py:401
  20.0 2.2 %collective-permute-done.3.rest_12_ = bf16[464,768]{1,0:T(8,128)(2,1)S(1)} collective-permute-done((bf16[464,768]{1,0:T(8,128)(2,1)}, bf16[464,768]{1,0:T(8,128)(2,1)S(1)}, u32[]{:S(2)}, u32[]{:S(2)}) %collective-permute-start.3) | collective-permute-done | bytes 712736 | tf_op jit(solution)/shard_map/ppermute | solution.py:362
  30.9 14.1 %collective-permute-done.6.rest_1_ = bf16[464,768]{1,0:T(8,128)(2,1)S(1)} collective-permute-done((bf16[464,768]{1,0:T(8,128)(2,1)S(1)}, bf16[464,768]{1,0:T(8,128)(2,1)S(1)}, u32[]{:S(2)}, u32[]{:S(2)}) %collective-permute-start.6) | collective-permute-done | bytes 712736 | tf_op jit(solution)/shard_map/ppermute | solution.py:362
  48.9 2.2 %collective-permute-done.9.rest_4_ = bf16[464,768]{1,0:T(8,128)(2,1)S(1)} collective-permute-done((bf16[464,768]{1,0:T(8,128)(2,1)S(1)}, bf16[464,768]{1,0:T(8,128)(2,1)S(1)}, u32[]{:S(2)}, u32[]{:S(2)}) %collective-permute-start.9) | collective-permute-done | bytes 712736 | tf_op jit(solution)/shard_map/ppermute | solution.py:367
  51.1 18.9 %collective-permute-done.11.rest_6_ = bf16[608,768]{1,0:T(8,128)(2,1)S(1)} collective-permute-done((bf16[608,768]{1,0:T(8,128)(2,1)S(1)}, bf16[608,768]{1,0:T(8,128)(2,1)S(1)}, u32[]{:S(2)}, u32[]{:S(2)}) %collective-permute-start.11) | collective-permute-done | bytes 933920 | tf_op jit(solution)/shard_map/ppermute | solution.py:367
  71.2 5.3 %collective-permute-done.16.rest_9_ = bf16[608,768]{1,0:T(8,128)(2,1)S(1)} collective-permute-done((bf16[608,768]{1,0:T(8,128)(2,1)S(1)}, bf16[608,768]{1,0:T(8,128)(2,1)S(1)}, u32[]{:S(2)}, u32[]{:S(2)}) %collective-permute-start.16) | collective-permute-done | bytes 933920 | tf_op jit(solution)/shard_map/ppermute | solution.py:367
  78.3 16.5 %encode.1 = (bf16[512,768]{1,0:T(8,128)(2,1)}, s32[8]{0:T(128)S(1)}, bf16[2,128,256]{2,1,0:T(8,128)(2,1)S(1)}, bf16[2,128,256]{2,1,0:T(8,128)(2,1)S(1)}, bf16[2,...) custom-call(s32[8]{0:T(128)S(1)} %bitcast.35, s32[8]{0:T(128)S(1)} %bitcast.37, ...), custom_call_target="tpu_custom_call" | custom-call | tf_op jit(solution)/shard_map/encode/pallas_call | solution.py:178
  95.0 2.6 %collective-permute-start.22 = (bf16[2,128,256]{2,1,0:T(8,128)(2,1)S(1)}, bf16[2,128,256]{2,1,0:T(8,128)(2,1)S(1)}, u32[]{:S(2)}, u32[]{:S(2)}) collective-permute-start(bf16[2,128,256]{2,1,0:T(8,128)(2,1)S(1)} %get-tuple-element.103), channel_id=1, source_target_pairs={{0,4},{1,5},{2,6},{3,7},{4,0},{5,1},{6,2},{7,3},{8,12},{9,13},{10,... | collective-permute-start | bytes 393224 | tf_op jit(solution)/shard_map/ppermute | solution.py:367
  98.5 8.8 %collective-permute-done.22.rest_4_ = bf16[2,128,256]{2,1,0:T(8,128)(2,1)S(1)} collective-permute-done((bf16[2,128,256]{2,1,0:T(8,128)(2,1)S(1)}, bf16[2,128,256]{2,1,0:T(8,128)(2,1)S(1)}, u32[]{:S(2)}, u32[]{:S(2)}) %collective-permute-start.22) | collective-permute-done | bytes 131104 | tf_op jit(solution)/shard_map/ppermute | solution.py:367
  111.4 5.1 %heads.1 = (bf16[640,256]{1,0:T(8,128)(2,1)}, bf16[8,256,256]{2,1,0:T(8,128)(2,1)S(1)}, bf16[2,128,256]{2,1,0:T(8,128)(2,1)S(1)}, bf16[2,128,256]{2,1,0:T(8,128)...) custom-call(s32[8]{0:T(128)S(1)} %get-tuple-element.98.targets_ref, ...), custom_call_target="tpu_custom_call" | custom-call | tf_op jit(solution)/shard_map/heads/pallas_call | solution.py:297
  117.4 3.5 %collective-permute-start.28 = (bf16[2,128,256]{2,1,0:T(8,128)(2,1)}, bf16[2,128,256]{2,1,0:T(8,128)(2,1)S(1)}, u32[]{:S(2)}, u32[]{:S(2)}) collective-permute-start(bf16[2,128,256]{2,1,0:T(8,128)(2,1)} %copy-done.14), channel_id=1, source_target_pairs={{0,4},{1,5},{2,6},{3,7},{4,0},{5,1},{6,2},{7,3},{8,12},{9,13},{10,... | collective-permute-start | bytes 393224 | tf_op jit(solution)/shard_map/ppermute | solution.py:367
  124.3 6.8 %collective-permute-done.28.rest_4_ = bf16[2,128,256]{2,1,0:T(8,128)(2,1)S(1)} collective-permute-done((bf16[2,128,256]{2,1,0:T(8,128)(2,1)}, bf16[2,128,256]{2,1,0:T(8,128)(2,1)S(1)}, u32[]{:S(2)}, u32[]{:S(2)}) %collective-permute-start.28) | collective-permute-done | bytes 131104 | tf_op jit(solution)/shard_map/ppermute | solution.py:367
  135.3 3.1 %collective-permute-done.33 = bf16[256,256]{1,0:T(8,128)(2,1)S(1)} collective-permute-done((bf16[256,256]{1,0:T(8,128)(2,1)S(1)}, bf16[256,256]{1,0:T(8,128)(2,1)S(1)}, u32[]{:S(2)}, u32[]{:S(2)}) %collective-permute-start.33) | collective-permute-done | bytes 131104 | tf_op jit(solution)/shard_map/ppermute | solution.py:362
  138.5 2.1 %collective-permute-start.34 = (bf16[256,256]{1,0:T(8,128)(2,1)S(1)}, bf16[256,256]{1,0:T(8,128)(2,1)S(1)}, u32[]{:S(2)}, u32[]{:S(2)}) collective-permute-start(bf16[256,256]{1,0:T(8,128)(2,1)S(1)} %add_convert_fusion.4), channel_id=1, source_target_pairs={{0,2},{1,3},{2,0},{3,1},{4,6},{5,7},{6,4},{7,5},{8,10},{9,11},{10,... | collective-permute-start | bytes 393224 | tf_op jit(solution)/shard_map/ppermute | solution.py:367
  144.4 1.8 %collective-permute-start.35 = (bf16[256,256]{1,0:T(8,128)(2,1)S(1)}, bf16[256,256]{1,0:T(8,128)(2,1)S(1)}, u32[]{:S(2)}, u32[]{:S(2)}) collective-permute-start(bf16[256,256]{1,0:T(8,128)(2,1)S(1)} %add_convert_fusion.3), channel_id=1, source_target_pairs={{0,4},{1,5},{2,6},{3,7},{4,0},{5,1},{6,2},{7,3},{8,12},{9,13},{10,... | collective-permute-start | bytes 393224 | tf_op jit(solution)/shard_map/ppermute | solution.py:367
  147.2 5.1 %collective-permute-done.35 = bf16[256,256]{1,0:T(8,128)(2,1)S(1)} collective-permute-done((bf16[256,256]{1,0:T(8,128)(2,1)S(1)}, bf16[256,256]{1,0:T(8,128)(2,1)S(1)}, u32[]{:S(2)}, u32[]{:S(2)}) %collective-permute-start.35) | collective-permute-done | bytes 131104 | tf_op jit(solution)/shard_map/ppermute | solution.py:367
  153.6 2.3 %collective-permute-start.38 = (bf16[256,256]{1,0:T(8,128)(2,1)S(1)}, bf16[256,256]{1,0:T(8,128)(2,1)S(1)}, u32[]{:S(2)}, u32[]{:S(2)}) collective-permute-start(bf16[256,256]{1,0:T(8,128)(2,1)S(1)} %add_convert_fusion.2), channel_id=1, source_target_pairs={{0,24},{8,16},{16,8},{24,0},{1,25},{9,17},{17,9},{25,1},{2,26},{10... | collective-permute-start | bytes 393224 | tf_op jit(solution)/shard_map/ppermute | solution.py:362
  162.5 2.0 %collective-permute-start.51 = (bf16[96,256]{1,0:T(8,128)(2,1)S(1)}, bf16[96,256]{1,0:T(8,128)(2,1)S(1)}, u32[]{:S(2)}, u32[]{:S(2)}) collective-permute-start(bf16[96,256]{1,0:T(8,128)(2,1)S(1)} %add_convert_fusion.5), channel_id=1, source_target_pairs={{0,24},{8,16},{16,8},{24,0},{1,25},{9,17},{17,9},{25,1},{2,26},{10... | collective-permute-start | bytes 147464 | tf_op jit(solution)/shard_map/ppermute | solution.py:362
  165.6 1.9 %collective-permute-done.51 = bf16[96,256]{1,0:T(8,128)(2,1)S(1)} collective-permute-done((bf16[96,256]{1,0:T(8,128)(2,1)S(1)}, bf16[96,256]{1,0:T(8,128)(2,1)S(1)}, u32[]{:S(2)}, u32[]{:S(2)}) %collective-permute-start.51) | collective-permute-done | bytes 49184 | tf_op jit(solution)/shard_map/ppermute | solution.py:362
  (179 shorter events, 49.5 us)
Async XLA Ops:
  3.1 19.2 %collective-permute-start.3 = (bf16[464,768]{1,0:T(8,128)(2,1)}, bf16[464,768]{1,0:T(8,128)(2,1)S(1)}, u32[]{:S(2)}, u32[]{:S(2)}) collective-permute-start(bf16[464,768]{1,0:T(8,128)(2,1)} %get-tuple-element.72), channel_id=1, source_target_pairs={{0,8},{8,0},{16,24},{24,16},{1,9},{9,1},{17,25},{25,17},{2,10},{10... | collective-permute-start | bytes 2138120 | tf_op jit(solution)/shard_map/ppermute | solution.py:362
  6.1 17.6 %collective-permute-start.4 = (bf16[464,768]{1,0:T(8,128)(2,1)}, bf16[464,768]{1,0:T(8,128)(2,1)S(1)}, u32[]{:S(2)}, u32[]{:S(2)}) collective-permute-start(bf16[464,768]{1,0:T(8,128)(2,1)} %get-tuple-element.73), channel_id=1, source_target_pairs={{0,16},{8,24},{16,0},{24,8},{1,17},{9,25},{17,1},{25,9},{2,18},{10... | collective-permute-start | bytes 2138120 | tf_op jit(solution)/shard_map/ppermute | solution.py:362
  24.0 22.5 %collective-permute-start.5 = (bf16[608,768]{1,0:T(8,128)(2,1)S(1)}, bf16[608,768]{1,0:T(8,128)(2,1)S(1)}, u32[]{:S(2)}, u32[]{:S(2)}) collective-permute-start(bf16[608,768]{1,0:T(8,128)(2,1)S(1)} %pad_maximum_fusion), channel_id=1, source_target_pairs={{0,2},{1,3},{2,0},{3,1},{4,6},{5,7},{6,4},{7,5},{8,10},{9,11},{10,... | collective-permute-start | bytes 2801672 | tf_op jit(solution)/shard_map/ppermute | solution.py:367
  26.1 18.8 %collective-permute-start.6 = (bf16[464,768]{1,0:T(8,128)(2,1)S(1)}, bf16[464,768]{1,0:T(8,128)(2,1)S(1)}, u32[]{:S(2)}, u32[]{:S(2)}) collective-permute-start(bf16[464,768]{1,0:T(8,128)(2,1)S(1)} %collective-permute-done.3.rest_12_), channel_id=1, source_target_pairs={{0,16},{8,24},{16,0},{24,8},{1,17},{9,25},{17,1},{25,9},{2,18},{10... | collective-permute-start | bytes 2138120 | tf_op jit(solution)/shard_map/ppermute | solution.py:362
  27.6 18.9 %collective-permute-start.7 = (bf16[464,768]{1,0:T(8,128)(2,1)S(1)}, bf16[464,768]{1,0:T(8,128)(2,1)S(1)}, u32[]{:S(2)}, u32[]{:S(2)}) collective-permute-start(bf16[464,768]{1,0:T(8,128)(2,1)S(1)} %collective-permute-done.4.rest_13_), channel_id=1, source_target_pairs={{0,8},{8,0},{16,24},{24,16},{1,9},{9,1},{17,25},{25,17},{2,10},{10... | collective-permute-start | bytes 2138120 | tf_op jit(solution)/shard_map/ppermute | solution.py:362
  28.8 41.7 %collective-permute-start.14 = (bf16[768,768]{1,0:T(8,128)(2,1)S(1)}, bf16[768,768]{1,0:T(8,128)(2,1)S(1)}, u32[]{:S(2)}, u32[]{:S(2)}) collective-permute-start(bf16[768,768]{1,0:T(8,128)(2,1)S(1)} %copy-done.29), channel_id=1, source_target_pairs={{0,8},{8,0},{16,24},{24,16},{1,9},{9,1},{17,25},{25,17},{2,10},{10... | collective-permute-start | bytes 3538952 | tf_op jit(solution)/shard_map/ppermute | solution.py:362
  29.8 40.7 %collective-permute-start.15 = (bf16[768,768]{1,0:T(8,128)(2,1)S(1)}, bf16[768,768]{1,0:T(8,128)(2,1)S(1)}, u32[]{:S(2)}, u32[]{:S(2)}) collective-permute-start(bf16[768,768]{1,0:T(8,128)(2,1)S(1)} %copy-done.28), channel_id=1, source_target_pairs={{0,16},{8,24},{16,0},{24,8},{1,17},{9,25},{17,1},{25,9},{2,18},{10... | collective-permute-start | bytes 3538952 | tf_op jit(solution)/shard_map/ppermute | solution.py:362
  46.8 23.2 %collective-permute-start.11 = (bf16[608,768]{1,0:T(8,128)(2,1)S(1)}, bf16[608,768]{1,0:T(8,128)(2,1)S(1)}, u32[]{:S(2)}, u32[]{:S(2)}) collective-permute-start(bf16[608,768]{1,0:T(8,128)(2,1)S(1)} %pad_maximum_fusion.1), channel_id=1, source_target_pairs={{0,2},{1,3},{2,0},{3,1},{4,6},{5,7},{6,4},{7,5},{8,10},{9,11},{10,... | collective-permute-start | bytes 2801672 | tf_op jit(solution)/shard_map/ppermute | solution.py:367
  47.4 22.6 %collective-permute-start.10 = (bf16[608,768]{1,0:T(8,128)(2,1)S(1)}, bf16[608,768]{1,0:T(8,128)(2,1)S(1)}, u32[]{:S(2)}, u32[]{:S(2)}) collective-permute-start(bf16[608,768]{1,0:T(8,128)(2,1)S(1)} %collective-permute-done.5.rest_2_), channel_id=1, source_target_pairs={{0,1},{1,0},{2,3},{3,2},{4,5},{5,4},{6,7},{7,6},{8,9},{9,8},{10,11... | collective-permute-start | bytes 2801672 | tf_op jit(solution)/shard_map/ppermute | solution.py:367
  70.5 5.9 %collective-permute-start.17 = (bf16[768,768]{1,0:T(8,128)(2,1)S(1)}, bf16[768,768]{1,0:T(8,128)(2,1)S(1)}, u32[]{:S(2)}, u32[]{:S(2)}) collective-permute-start(bf16[768,768]{1,0:T(8,128)(2,1)S(1)} %collective-permute-done.14.rest_7_), channel_id=1, source_target_pairs={{0,1},{1,0},{2,3},{3,2},{4,5},{5,4},{6,7},{7,6},{8,9},{9,8},{10,11... | collective-permute-start | bytes 3538952 | tf_op jit(solution)/shard_map/ppermute | solution.py:367
  70.6 5.9 %collective-permute-start.18 = (bf16[768,768]{1,0:T(8,128)(2,1)S(1)}, bf16[768,768]{1,0:T(8,128)(2,1)S(1)}, u32[]{:S(2)}, u32[]{:S(2)}) collective-permute-start(bf16[768,768]{1,0:T(8,128)(2,1)S(1)} %collective-permute-done.15.rest_8_), channel_id=1, source_target_pairs={{0,1},{1,0},{2,3},{3,2},{4,5},{5,4},{6,7},{7,6},{8,9},{9,8},{10,11... | collective-permute-start | bytes 3538952 | tf_op jit(solution)/shard_map/ppermute | solution.py:367
  95.0 12.3 %collective-permute-start.22 = (bf16[2,128,256]{2,1,0:T(8,128)(2,1)S(1)}, bf16[2,128,256]{2,1,0:T(8,128)(2,1)S(1)}, u32[]{:S(2)}, u32[]{:S(2)}) collective-permute-start(bf16[2,128,256]{2,1,0:T(8,128)(2,1)S(1)} %get-tuple-element.103), channel_id=1, source_target_pairs={{0,4},{1,5},{2,6},{3,7},{4,0},{5,1},{6,2},{7,3},{8,12},{9,13},{10,... | collective-permute-start | bytes 393224 | tf_op jit(solution)/shard_map/ppermute | solution.py:367
  97.6 9.7 %collective-permute-start.24 = (bf16[2,128,256]{2,1,0:T(8,128)(2,1)S(1)}, bf16[2,128,256]{2,1,0:T(8,128)(2,1)S(1)}, u32[]{:S(2)}, u32[]{:S(2)}) collective-permute-start(bf16[2,128,256]{2,1,0:T(8,128)(2,1)S(1)} %get-tuple-element.104), channel_id=1, source_target_pairs={{0,6},{1,7},{2,4},{3,5},{4,2},{5,3},{6,0},{7,1},{8,14},{9,15},{10,... | collective-permute-start | bytes 393224 | tf_op jit(solution)/shard_map/ppermute | solution.py:367
  97.8 10.8 %collective-permute-start.20 = (bf16[2,128,256]{2,1,0:T(8,128)(2,1)S(1)}, bf16[2,128,256]{2,1,0:T(8,128)(2,1)S(1)}, u32[]{:S(2)}, u32[]{:S(2)}) collective-permute-start(bf16[2,128,256]{2,1,0:T(8,128)(2,1)S(1)} %get-tuple-element.102), channel_id=1, source_target_pairs={{0,2},{1,3},{2,0},{3,1},{4,6},{5,7},{6,4},{7,5},{8,10},{9,11},{10,... | collective-permute-start | bytes 393224 | tf_op jit(solution)/shard_map/ppermute | solution.py:367
  117.4 13.7 %collective-permute-start.28 = (bf16[2,128,256]{2,1,0:T(8,128)(2,1)}, bf16[2,128,256]{2,1,0:T(8,128)(2,1)S(1)}, u32[]{:S(2)}, u32[]{:S(2)}) collective-permute-start(bf16[2,128,256]{2,1,0:T(8,128)(2,1)} %copy-done.14), channel_id=1, source_target_pairs={{0,4},{1,5},{2,6},{3,7},{4,0},{5,1},{6,2},{7,3},{8,12},{9,13},{10,... | collective-permute-start | bytes 393224 | tf_op jit(solution)/shard_map/ppermute | solution.py:367
  120.9 10.2 %collective-permute-start.29 = (bf16[2,128,256]{2,1,0:T(8,128)(2,1)}, bf16[2,128,256]{2,1,0:T(8,128)(2,1)S(1)}, u32[]{:S(2)}, u32[]{:S(2)}) collective-permute-start(bf16[2,128,256]{2,1,0:T(8,128)(2,1)} %copy-done.13), channel_id=1, source_target_pairs={{0,6},{1,7},{2,4},{3,5},{4,2},{5,3},{6,0},{7,1},{8,14},{9,15},{10,... | collective-permute-start | bytes 393224 | tf_op jit(solution)/shard_map/ppermute | solution.py:367
  122.1 9.8 %collective-permute-start.27 = (bf16[2,128,256]{2,1,0:T(8,128)(2,1)}, bf16[2,128,256]{2,1,0:T(8,128)(2,1)S(1)}, u32[]{:S(2)}, u32[]{:S(2)}) collective-permute-start(bf16[2,128,256]{2,1,0:T(8,128)(2,1)} %copy-done.12), channel_id=1, source_target_pairs={{0,2},{1,3},{2,0},{3,1},{4,6},{5,7},{6,4},{7,5},{8,10},{9,11},{10,... | collective-permute-start | bytes 393224 | tf_op jit(solution)/shard_map/ppermute | solution.py:367
  122.3 9.6 %collective-permute-start.31 = (bf16[256,256]{1,0:T(8,128)(2,1)S(1)}, bf16[256,256]{1,0:T(8,128)(2,1)S(1)}, u32[]{:S(2)}, u32[]{:S(2)}) collective-permute-start(bf16[256,256]{1,0:T(8,128)(2,1)S(1)} %get-tuple-element.134), channel_id=1, source_target_pairs={{0,24},{8,16},{16,8},{24,0},{1,25},{9,17},{17,9},{25,1},{2,26},{10... | collective-permute-start | bytes 393224 | tf_op jit(solution)/shard_map/ppermute | solution.py:362
  122.6 9.3 %collective-permute-start.32 = (bf16[256,256]{1,0:T(8,128)(2,1)S(1)}, bf16[256,256]{1,0:T(8,128)(2,1)S(1)}, u32[]{:S(2)}, u32[]{:S(2)}) collective-permute-start(bf16[256,256]{1,0:T(8,128)(2,1)S(1)} %get-tuple-element.132), channel_id=1, source_target_pairs={{0,8},{8,0},{16,24},{24,16},{1,9},{9,1},{17,25},{25,17},{2,10},{10... | collective-permute-start | bytes 393224 | tf_op jit(solution)/shard_map/ppermute | solution.py:362
  132.6 5.8 %collective-permute-start.33 = (bf16[256,256]{1,0:T(8,128)(2,1)S(1)}, bf16[256,256]{1,0:T(8,128)(2,1)S(1)}, u32[]{:S(2)}, u32[]{:S(2)}) collective-permute-start(bf16[256,256]{1,0:T(8,128)(2,1)S(1)} %get-tuple-element.133), channel_id=1, source_target_pairs={{0,16},{8,24},{16,0},{24,8},{1,17},{9,25},{17,1},{25,9},{2,18},{10... | collective-permute-start | bytes 393224 | tf_op jit(solution)/shard_map/ppermute | solution.py:362
  144.4 7.9 %collective-permute-start.35 = (bf16[256,256]{1,0:T(8,128)(2,1)S(1)}, bf16[256,256]{1,0:T(8,128)(2,1)S(1)}, u32[]{:S(2)}, u32[]{:S(2)}) collective-permute-start(bf16[256,256]{1,0:T(8,128)(2,1)S(1)} %add_convert_fusion.3), channel_id=1, source_target_pairs={{0,4},{1,5},{2,6},{3,7},{4,0},{5,1},{6,2},{7,3},{8,12},{9,13},{10,... | collective-permute-start | bytes 393224 | tf_op jit(solution)/shard_map/ppermute | solution.py:367
  147.1 8.8 %collective-permute-start.47 = (bf16[96,256]{1,0:T(8,128)(2,1)S(1)}, bf16[96,256]{1,0:T(8,128)(2,1)S(1)}, u32[]{:S(2)}, u32[]{:S(2)}) collective-permute-start(bf16[96,256]{1,0:T(8,128)(2,1)S(1)} %fusion.2), channel_id=1, source_target_pairs={{0,2},{1,3},{2,0},{3,1},{4,6},{5,7},{6,4},{7,5},{8,10},{9,11},{10,... | collective-permute-start | bytes 147464 | tf_op jit(solution)/shard_map/ppermute | solution.py:367
  153.6 5.9 %collective-permute-start.38 = (bf16[256,256]{1,0:T(8,128)(2,1)S(1)}, bf16[256,256]{1,0:T(8,128)(2,1)S(1)}, u32[]{:S(2)}, u32[]{:S(2)}) collective-permute-start(bf16[256,256]{1,0:T(8,128)(2,1)S(1)} %add_convert_fusion.2), channel_id=1, source_target_pairs={{0,24},{8,16},{16,8},{24,0},{1,25},{9,17},{17,9},{25,1},{2,26},{10... | collective-permute-start | bytes 393224 | tf_op jit(solution)/shard_map/ppermute | solution.py:362
  159.5 8.1 %collective-permute-start.39 = (bf16[4,256,256]{2,1,0:T(8,128)(2,1)S(1)}, bf16[4,256,256]{2,1,0:T(8,128)(2,1)S(1)}, u32[]{:S(2)}, u32[]{:S(2)}) collective-permute-start(bf16[4,256,256]{2,1,0:T(8,128)(2,1)S(1)} %pad_maximum_fusion.2.gathered_ref), channel_id=1, source_target_pairs={{0,1},{1,0},{2,3},{3,2},{4,5},{5,4},{6,7},{7,6},{8,9},{9,8},{10,11... | collective-permute-start | bytes 1572872 | tf_op jit(solution)/shard_map/ppermute | solution.py:367
  (59 other events, 502.6 us)

commit v5 on v4

--- a/solution.py
+++ b/solution.py
@@ -495,6 +495,12 @@
     return (share, *[to_section(share, flip) for flip in (1, 2, 3)])
 
 
+def section_shares_doubled(share):
+    across = jnp.stack([share, to_section(share, 2)])
+    beside = to_section(across, 1)
+    return (across[0], beside[0], across[1], beside[1])
+
+
 def with_other_core(shares):
     gathered = jnp.stack(shares)
     return (gathered, to_tile(gathered, 1))
@@ -597,7 +603,7 @@
         src_block[0], live[0], frustum_tiles[0], encoded, returned, singles
     )
     proj_total = chips_total(add_up(*section_share(grad_proj, section, core)))
-    head_shares = with_other_core(section_shares(head_total))
+    head_shares = with_other_core(section_shares_doubled(head_total))
     proj_shares = section_shares(proj_total)
     grads = unpack(
         *head_shares,

time: 170 us -> 169 us (level)
  starting transfers between devices: 44.3 us -> 41 us
  waiting for transfers between devices: 88.9 us -> 90.9 us
    ppermute x18 -> x17, waiting for transfers between devices: 30.3 us -> 33.8 us  [to_section(): lax.ppermute(array, 'section', [(at, at ^ flip) for at in range(count)])]
    ppermute x18 -> x17, starting transfers between devices: 21.9 us -> 19.6 us  [to_section(): lax.ppermute(array, 'section', [(at, at ^ flip) for at in range(count)])]
  transfers between devices with their start and end apart: 53 -> 52, of which waited for: 31 -> 27; matrix products, arithmetic and copies ran while one was open for 0% -> 1% of each run, Pallas kernels for 3% -> 3%
where the time goes in v5:
time: 169 us
  waiting for transfers between devices  90.9 us (54%)
  starting transfers between devices  41 us (24%)
  Pallas kernels  30.8 us (18%)
  local copies, waits for them, and re-layouts  4.02 us (2%)
    ppermute x35, waiting for transfers between devices, to_tile(): return lax.ppermute(array, 'tile', [(at, at ^ flip) for at in range(count)])  57.1 us
    ppermute x17, waiting for transfers between devices, to_section(): lax.ppermute(array, 'section', [(at, at ^ flip) for at in range(count)])  33.8 us
    ppermute x35, starting transfers between devices, to_tile(): return lax.ppermute(array, 'tile', [(at, at ^ flip) for at in range(count)])  21.4 us
    ppermute x17, starting transfers between devices, to_section(): lax.ppermute(array, 'section', [(at, at ^ flip) for at in range(count)])  19.6 us
    pallas_call x1, Pallas kernels, encode(): pl.pallas_call(functools.partial(encode_kernel, names, counts), out_shape...  16.5 us
    pallas_call x2, Pallas kernels, cut(): pl.pallas_call(functools.partial(cut_kernel, (plan,)), out_shape=tuple((j...  5.53 us
    pallas_call x1, Pallas kernels, heads(): pl.pallas_call(functools.partial(heads_kernel, counts, back_counts, scale...  5.08 us
    unnamed x60, local copies, waits for them, and re-layouts  3.82 us
  transfers between devices with their start and end apart: 52, of which 27 were waited for; matrix products, arithmetic and copies ran while one was open for 1% of the time, Pallas kernels for 3%

profile of v5, /device:TPU:0, one launch (start us, length us, event | category | flops | bytes accessed | tf_op | source)
XLA Modules:
  0.0 168.8 jit_solution(4097677647699572984)
XLA Ops:
  0.6 2.4 %cut.2 = (bf16[464,768]{1,0:T(8,128)(2,1)}, bf16[464,768]{1,0:T(8,128)(2,1)}) custom-call(bf16[768,1536]{1,0:T(8,128)(2,1)} %bitcast.37, bf16[1536,768]{1,0:T(8,128)(2,1)} %bitcast.40), custom_call_target="tpu_custom_call" | custom-call | tf_op jit(solution)/shard_map/cut/pallas_call | solution.py:401
  3.1 3.0 %collective-permute-start.3 = (bf16[464,768]{1,0:T(8,128)(2,1)}, bf16[464,768]{1,0:T(8,128)(2,1)S(1)}, u32[]{:S(2)}, u32[]{:S(2)}) collective-permute-start(bf16[464,768]{1,0:T(8,128)(2,1)} %get-tuple-element.72), channel_id=1, source_target_pairs={{0,8},{8,0},{16,24},{24,16},{1,9},{9,1},{17,25},{25,17},{2,10},{10... | collective-permute-start | bytes 2138120 | tf_op jit(solution)/shard_map/ppermute | solution.py:362
  10.4 2.0 %collective-permute-done.1 = s32[2,8]{1,0:T(2,128)S(1)} collective-permute-done((s32[2,8]{1,0:T(2,128)S(1)}, s32[2,8]{1,0:T(2,128)S(1)}, u32[]{:S(2)}, u32[]{:S(2)}) %collective-permute-start.1) | collective-permute-done | bytes 96 | tf_op jit(solution)/shard_map/ppermute | solution.py:367
  12.4 2.7 %collective-permute-start.2 = (s32[4,8]{1,0:T(4,128)S(1)}, s32[4,8]{1,0:T(4,128)S(1)}, u32[]{:S(2)}, u32[]{:S(2)}) collective-permute-start(s32[4,8]{1,0:T(4,128)S(1)} %pad_add_fusion.1), channel_id=1, source_target_pairs={{0,4},{1,5},{2,6},{3,7},{4,0},{5,1},{6,2},{7,3},{8,12},{9,13},{10,... | collective-permute-start | bytes 392 | tf_op jit(solution)/shard_map/ppermute | solution.py:367
  15.0 1.9 %collective-permute-done.2 = s32[4,8]{1,0:T(4,128)S(1)} collective-permute-done((s32[4,8]{1,0:T(4,128)S(1)}, s32[4,8]{1,0:T(4,128)S(1)}, u32[]{:S(2)}, u32[]{:S(2)}) %collective-permute-start.2) | collective-permute-done | bytes 160 | tf_op jit(solution)/shard_map/ppermute | solution.py:367
  17.0 3.1 %cut.3 = (bf16[768,768]{1,0:T(8,128)(2,1)}, bf16[768,768]{1,0:T(8,128)(2,1)}) custom-call(bf16[768,1536]{1,0:T(8,128)(2,1)} %bitcast.38, bf16[1536,768]{1,0:T(8,128)(2,1)} %bitcast.41), custom_call_target="tpu_custom_call" | custom-call | tf_op jit(solution)/shard_map/cut/pallas_call | solution.py:401
  20.0 2.2 %collective-permute-done.3.rest_12_ = bf16[464,768]{1,0:T(8,128)(2,1)S(1)} collective-permute-done((bf16[464,768]{1,0:T(8,128)(2,1)}, bf16[464,768]{1,0:T(8,128)(2,1)S(1)}, u32[]{:S(2)}, u32[]{:S(2)}) %collective-permute-start.3) | collective-permute-done | bytes 712736 | tf_op jit(solution)/shard_map/ppermute | solution.py:362
  24.0 1.6 collective-permute-start.5
  30.9 14.1 %collective-permute-done.6.rest_1_ = bf16[464,768]{1,0:T(8,128)(2,1)S(1)} collective-permute-done((bf16[464,768]{1,0:T(8,128)(2,1)S(1)}, bf16[464,768]{1,0:T(8,128)(2,1)S(1)}, u32[]{:S(2)}, u32[]{:S(2)}) %collective-permute-start.6) | collective-permute-done | bytes 712736 | tf_op jit(solution)/shard_map/ppermute | solution.py:362
  48.9 2.2 %collective-permute-done.9.rest_4_ = bf16[464,768]{1,0:T(8,128)(2,1)S(1)} collective-permute-done((bf16[464,768]{1,0:T(8,128)(2,1)S(1)}, bf16[464,768]{1,0:T(8,128)(2,1)S(1)}, u32[]{:S(2)}, u32[]{:S(2)}) %collective-permute-start.9) | collective-permute-done | bytes 712736 | tf_op jit(solution)/shard_map/ppermute | solution.py:367
  51.1 18.9 %collective-permute-done.11.rest_6_ = bf16[608,768]{1,0:T(8,128)(2,1)S(1)} collective-permute-done((bf16[608,768]{1,0:T(8,128)(2,1)S(1)}, bf16[608,768]{1,0:T(8,128)(2,1)S(1)}, u32[]{:S(2)}, u32[]{:S(2)}) %collective-permute-start.11) | collective-permute-done | bytes 933920 | tf_op jit(solution)/shard_map/ppermute | solution.py:367
  71.2 5.3 %collective-permute-done.16.rest_9_ = bf16[608,768]{1,0:T(8,128)(2,1)S(1)} collective-permute-done((bf16[608,768]{1,0:T(8,128)(2,1)S(1)}, bf16[608,768]{1,0:T(8,128)(2,1)S(1)}, u32[]{:S(2)}, u32[]{:S(2)}) %collective-permute-start.16) | collective-permute-done | bytes 933920 | tf_op jit(solution)/shard_map/ppermute | solution.py:367
  78.3 16.5 %encode.1 = (bf16[512,768]{1,0:T(8,128)(2,1)}, s32[8]{0:T(128)S(1)}, bf16[2,128,256]{2,1,0:T(8,128)(2,1)S(1)}, bf16[2,128,256]{2,1,0:T(8,128)(2,1)S(1)}, bf16[2,...) custom-call(s32[8]{0:T(128)S(1)} %bitcast.33, s32[8]{0:T(128)S(1)} %bitcast.35, ...), custom_call_target="tpu_custom_call" | custom-call | tf_op jit(solution)/shard_map/encode/pallas_call | solution.py:178
  95.0 2.6 %collective-permute-start.22 = (bf16[2,128,256]{2,1,0:T(8,128)(2,1)S(1)}, bf16[2,128,256]{2,1,0:T(8,128)(2,1)S(1)}, u32[]{:S(2)}, u32[]{:S(2)}) collective-permute-start(bf16[2,128,256]{2,1,0:T(8,128)(2,1)S(1)} %get-tuple-element.103), channel_id=1, source_target_pairs={{0,4},{1,5},{2,6},{3,7},{4,0},{5,1},{6,2},{7,3},{8,12},{9,13},{10,... | collective-permute-start | bytes 393224 | tf_op jit(solution)/shard_map/ppermute | solution.py:367
  98.5 8.8 %collective-permute-done.22.rest_4_ = bf16[2,128,256]{2,1,0:T(8,128)(2,1)S(1)} collective-permute-done((bf16[2,128,256]{2,1,0:T(8,128)(2,1)S(1)}, bf16[2,128,256]{2,1,0:T(8,128)(2,1)S(1)}, u32[]{:S(2)}, u32[]{:S(2)}) %collective-permute-start.22) | collective-permute-done | bytes 131104 | tf_op jit(solution)/shard_map/ppermute | solution.py:367
  111.4 5.1 %heads.1 = (bf16[640,256]{1,0:T(8,128)(2,1)}, bf16[8,256,256]{2,1,0:T(8,128)(2,1)S(1)}, bf16[2,128,256]{2,1,0:T(8,128)(2,1)S(1)}, bf16[2,128,256]{2,1,0:T(8,128)...) custom-call(s32[8]{0:T(128)S(1)} %get-tuple-element.98.targets_ref, ...), custom_call_target="tpu_custom_call" | custom-call | tf_op jit(solution)/shard_map/heads/pallas_call | solution.py:297
  117.4 3.5 %collective-permute-start.28 = (bf16[2,128,256]{2,1,0:T(8,128)(2,1)}, bf16[2,128,256]{2,1,0:T(8,128)(2,1)S(1)}, u32[]{:S(2)}, u32[]{:S(2)}) collective-permute-start(bf16[2,128,256]{2,1,0:T(8,128)(2,1)} %copy-done.14), channel_id=1, source_target_pairs={{0,4},{1,5},{2,6},{3,7},{4,0},{5,1},{6,2},{7,3},{8,12},{9,13},{10,... | collective-permute-start | bytes 393224 | tf_op jit(solution)/shard_map/ppermute | solution.py:367
  124.3 6.8 %collective-permute-done.28.rest_4_ = bf16[2,128,256]{2,1,0:T(8,128)(2,1)S(1)} collective-permute-done((bf16[2,128,256]{2,1,0:T(8,128)(2,1)}, bf16[2,128,256]{2,1,0:T(8,128)(2,1)S(1)}, u32[]{:S(2)}, u32[]{:S(2)}) %collective-permute-start.28) | collective-permute-done | bytes 131104 | tf_op jit(solution)/shard_map/ppermute | solution.py:367
  132.6 3.4 %collective-permute-done.33 = bf16[256,256]{1,0:T(8,128)(2,1)S(1)} collective-permute-done((bf16[256,256]{1,0:T(8,128)(2,1)S(1)}, bf16[256,256]{1,0:T(8,128)(2,1)S(1)}, u32[]{:S(2)}, u32[]{:S(2)}) %collective-permute-start.33) | collective-permute-done | bytes 131104 | tf_op jit(solution)/shard_map/ppermute | solution.py:362
  137.6 3.5 %collective-permute-done.34 = bf16[256,256]{1,0:T(8,128)(2,1)S(1)} collective-permute-done((bf16[256,256]{1,0:T(8,128)(2,1)S(1)}, bf16[256,256]{1,0:T(8,128)(2,1)S(1)}, u32[]{:S(2)}, u32[]{:S(2)}) %collective-permute-start.34) | collective-permute-done | bytes 131104 | tf_op jit(solution)/shard_map/ppermute | solution.py:367
  145.4 2.6 %collective-permute-done.35 = bf16[256,256]{1,0:T(8,128)(2,1)S(1)} collective-permute-done((bf16[256,256]{1,0:T(8,128)(2,1)S(1)}, bf16[256,256]{1,0:T(8,128)(2,1)S(1)}, u32[]{:S(2)}, u32[]{:S(2)}) %collective-permute-start.35) | collective-permute-done | bytes 131104 | tf_op jit(solution)/shard_map/ppermute | solution.py:367
  150.2 2.8 %collective-permute-done.36 = bf16[256,256]{1,0:T(8,128)(2,1)S(1)} collective-permute-done((bf16[256,256]{1,0:T(8,128)(2,1)S(1)}, bf16[256,256]{1,0:T(8,128)(2,1)S(1)}, u32[]{:S(2)}, u32[]{:S(2)}) %collective-permute-start.36) | collective-permute-done | bytes 131104 | tf_op jit(solution)/shard_map/ppermute | solution.py:362
  154.8 4.7 %collective-permute-done.37 = bf16[2,256,256]{2,1,0:T(8,128)(2,1)S(1)} collective-permute-done((bf16[2,256,256]{2,1,0:T(8,128)(2,1)S(1)}, bf16[2,256,256]{2,1,0:T(8,128)(2,1)S(1)}, u32[]{:S(2)}, u32[]{:S(2)}) %collective-permute-start.37) | collective-permute-done | bytes 262176 | tf_op jit(solution)/shard_map/ppermute | solution.py:362
  161.3 1.9 %collective-permute-start.50 = (bf16[96,256]{1,0:T(8,128)(2,1)S(1)}, bf16[96,256]{1,0:T(8,128)(2,1)S(1)}, u32[]{:S(2)}, u32[]{:S(2)}) collective-permute-start(bf16[96,256]{1,0:T(8,128)(2,1)S(1)} %add_convert_fusion.5), channel_id=1, source_target_pairs={{0,24},{8,16},{16,8},{24,0},{1,25},{9,17},{17,9},{25,1},{2,26},{10... | collective-permute-start | bytes 147464 | tf_op jit(solution)/shard_map/ppermute | solution.py:362
  (179 shorter events, 46.0 us)
Async XLA Ops:
  3.1 19.2 %collective-permute-start.3 = (bf16[464,768]{1,0:T(8,128)(2,1)}, bf16[464,768]{1,0:T(8,128)(2,1)S(1)}, u32[]{:S(2)}, u32[]{:S(2)}) collective-permute-start(bf16[464,768]{1,0:T(8,128)(2,1)} %get-tuple-element.72), channel_id=1, source_target_pairs={{0,8},{8,0},{16,24},{24,16},{1,9},{9,1},{17,25},{25,17},{2,10},{10... | collective-permute-start | bytes 2138120 | tf_op jit(solution)/shard_map/ppermute | solution.py:362
  6.1 17.6 %collective-permute-start.4 = (bf16[464,768]{1,0:T(8,128)(2,1)}, bf16[464,768]{1,0:T(8,128)(2,1)S(1)}, u32[]{:S(2)}, u32[]{:S(2)}) collective-permute-start(bf16[464,768]{1,0:T(8,128)(2,1)} %get-tuple-element.73), channel_id=1, source_target_pairs={{0,16},{8,24},{16,0},{24,8},{1,17},{9,25},{17,1},{25,9},{2,18},{10... | collective-permute-start | bytes 2138120 | tf_op jit(solution)/shard_map/ppermute | solution.py:362
  24.0 22.5 %collective-permute-start.5 = (bf16[608,768]{1,0:T(8,128)(2,1)S(1)}, bf16[608,768]{1,0:T(8,128)(2,1)S(1)}, u32[]{:S(2)}, u32[]{:S(2)}) collective-permute-start(bf16[608,768]{1,0:T(8,128)(2,1)S(1)} %pad_maximum_fusion), channel_id=1, source_target_pairs={{0,2},{1,3},{2,0},{3,1},{4,6},{5,7},{6,4},{7,5},{8,10},{9,11},{10,... | collective-permute-start | bytes 2801672 | tf_op jit(solution)/shard_map/ppermute | solution.py:367
  26.1 18.8 %collective-permute-start.6 = (bf16[464,768]{1,0:T(8,128)(2,1)S(1)}, bf16[464,768]{1,0:T(8,128)(2,1)S(1)}, u32[]{:S(2)}, u32[]{:S(2)}) collective-permute-start(bf16[464,768]{1,0:T(8,128)(2,1)S(1)} %collective-permute-done.3.rest_12_), channel_id=1, source_target_pairs={{0,16},{8,24},{16,0},{24,8},{1,17},{9,25},{17,1},{25,9},{2,18},{10... | collective-permute-start | bytes 2138120 | tf_op jit(solution)/shard_map/ppermute | solution.py:362
  27.6 18.9 %collective-permute-start.7 = (bf16[464,768]{1,0:T(8,128)(2,1)S(1)}, bf16[464,768]{1,0:T(8,128)(2,1)S(1)}, u32[]{:S(2)}, u32[]{:S(2)}) collective-permute-start(bf16[464,768]{1,0:T(8,128)(2,1)S(1)} %collective-permute-done.4.rest_13_), channel_id=1, source_target_pairs={{0,8},{8,0},{16,24},{24,16},{1,9},{9,1},{17,25},{25,17},{2,10},{10... | collective-permute-start | bytes 2138120 | tf_op jit(solution)/shard_map/ppermute | solution.py:362
  28.8 41.7 %collective-permute-start.14 = (bf16[768,768]{1,0:T(8,128)(2,1)S(1)}, bf16[768,768]{1,0:T(8,128)(2,1)S(1)}, u32[]{:S(2)}, u32[]{:S(2)}) collective-permute-start(bf16[768,768]{1,0:T(8,128)(2,1)S(1)} %copy-done.29), channel_id=1, source_target_pairs={{0,8},{8,0},{16,24},{24,16},{1,9},{9,1},{17,25},{25,17},{2,10},{10... | collective-permute-start | bytes 3538952 | tf_op jit(solution)/shard_map/ppermute | solution.py:362
  29.8 40.7 %collective-permute-start.15 = (bf16[768,768]{1,0:T(8,128)(2,1)S(1)}, bf16[768,768]{1,0:T(8,128)(2,1)S(1)}, u32[]{:S(2)}, u32[]{:S(2)}) collective-permute-start(bf16[768,768]{1,0:T(8,128)(2,1)S(1)} %copy-done.28), channel_id=1, source_target_pairs={{0,16},{8,24},{16,0},{24,8},{1,17},{9,25},{17,1},{25,9},{2,18},{10... | collective-permute-start | bytes 3538952 | tf_op jit(solution)/shard_map/ppermute | solution.py:362
  46.8 23.2 %collective-permute-start.11 = (bf16[608,768]{1,0:T(8,128)(2,1)S(1)}, bf16[608,768]{1,0:T(8,128)(2,1)S(1)}, u32[]{:S(2)}, u32[]{:S(2)}) collective-permute-start(bf16[608,768]{1,0:T(8,128)(2,1)S(1)} %pad_maximum_fusion.1), channel_id=1, source_target_pairs={{0,2},{1,3},{2,0},{3,1},{4,6},{5,7},{6,4},{7,5},{8,10},{9,11},{10,... | collective-permute-start | bytes 2801672 | tf_op jit(solution)/shard_map/ppermute | solution.py:367
  47.4 22.6 %collective-permute-start.10 = (bf16[608,768]{1,0:T(8,128)(2,1)S(1)}, bf16[608,768]{1,0:T(8,128)(2,1)S(1)}, u32[]{:S(2)}, u32[]{:S(2)}) collective-permute-start(bf16[608,768]{1,0:T(8,128)(2,1)S(1)} %collective-permute-done.5.rest_2_), channel_id=1, source_target_pairs={{0,1},{1,0},{2,3},{3,2},{4,5},{5,4},{6,7},{7,6},{8,9},{9,8},{10,11... | collective-permute-start | bytes 2801672 | tf_op jit(solution)/shard_map/ppermute | solution.py:367
  70.5 5.9 %collective-permute-start.17 = (bf16[768,768]{1,0:T(8,128)(2,1)S(1)}, bf16[768,768]{1,0:T(8,128)(2,1)S(1)}, u32[]{:S(2)}, u32[]{:S(2)}) collective-permute-start(bf16[768,768]{1,0:T(8,128)(2,1)S(1)} %collective-permute-done.14.rest_7_), channel_id=1, source_target_pairs={{0,1},{1,0},{2,3},{3,2},{4,5},{5,4},{6,7},{7,6},{8,9},{9,8},{10,11... | collective-permute-start | bytes 3538952 | tf_op jit(solution)/shard_map/ppermute | solution.py:367
  95.0 12.3 %collective-permute-start.22 = (bf16[2,128,256]{2,1,0:T(8,128)(2,1)S(1)}, bf16[2,128,256]{2,1,0:T(8,128)(2,1)S(1)}, u32[]{:S(2)}, u32[]{:S(2)}) collective-permute-start(bf16[2,128,256]{2,1,0:T(8,128)(2,1)S(1)} %get-tuple-element.103), channel_id=1, source_target_pairs={{0,4},{1,5},{2,6},{3,7},{4,0},{5,1},{6,2},{7,3},{8,12},{9,13},{10,... | collective-permute-start | bytes 393224 | tf_op jit(solution)/shard_map/ppermute | solution.py:367
  97.6 9.7 %collective-permute-start.24 = (bf16[2,128,256]{2,1,0:T(8,128)(2,1)S(1)}, bf16[2,128,256]{2,1,0:T(8,128)(2,1)S(1)}, u32[]{:S(2)}, u32[]{:S(2)}) collective-permute-start(bf16[2,128,256]{2,1,0:T(8,128)(2,1)S(1)} %get-tuple-element.104), channel_id=1, source_target_pairs={{0,6},{1,7},{2,4},{3,5},{4,2},{5,3},{6,0},{7,1},{8,14},{9,15},{10,... | collective-permute-start | bytes 393224 | tf_op jit(solution)/shard_map/ppermute | solution.py:367
  97.8 10.8 %collective-permute-start.20 = (bf16[2,128,256]{2,1,0:T(8,128)(2,1)S(1)}, bf16[2,128,256]{2,1,0:T(8,128)(2,1)S(1)}, u32[]{:S(2)}, u32[]{:S(2)}) collective-permute-start(bf16[2,128,256]{2,1,0:T(8,128)(2,1)S(1)} %get-tuple-element.102), channel_id=1, source_target_pairs={{0,2},{1,3},{2,0},{3,1},{4,6},{5,7},{6,4},{7,5},{8,10},{9,11},{10,... | collective-permute-start | bytes 393224 | tf_op jit(solution)/shard_map/ppermute | solution.py:367
  117.4 13.7 %collective-permute-start.28 = (bf16[2,128,256]{2,1,0:T(8,128)(2,1)}, bf16[2,128,256]{2,1,0:T(8,128)(2,1)S(1)}, u32[]{:S(2)}, u32[]{:S(2)}) collective-permute-start(bf16[2,128,256]{2,1,0:T(8,128)(2,1)} %copy-done.14), channel_id=1, source_target_pairs={{0,4},{1,5},{2,6},{3,7},{4,0},{5,1},{6,2},{7,3},{8,12},{9,13},{10,... | collective-permute-start | bytes 393224 | tf_op jit(solution)/shard_map/ppermute | solution.py:367
  120.9 10.8 %collective-permute-start.29 = (bf16[2,128,256]{2,1,0:T(8,128)(2,1)}, bf16[2,128,256]{2,1,0:T(8,128)(2,1)S(1)}, u32[]{:S(2)}, u32[]{:S(2)}) collective-permute-start(bf16[2,128,256]{2,1,0:T(8,128)(2,1)} %copy-done.13), channel_id=1, source_target_pairs={{0,6},{1,7},{2,4},{3,5},{4,2},{5,3},{6,0},{7,1},{8,14},{9,15},{10,... | collective-permute-start | bytes 393224 | tf_op jit(solution)/shard_map/ppermute | solution.py:367
  122.2 9.8 %collective-permute-start.27 = (bf16[2,128,256]{2,1,0:T(8,128)(2,1)}, bf16[2,128,256]{2,1,0:T(8,128)(2,1)S(1)}, u32[]{:S(2)}, u32[]{:S(2)}) collective-permute-start(bf16[2,128,256]{2,1,0:T(8,128)(2,1)} %copy-done.12), channel_id=1, source_target_pairs={{0,2},{1,3},{2,0},{3,1},{4,6},{5,7},{6,4},{7,5},{8,10},{9,11},{10,... | collective-permute-start | bytes 393224 | tf_op jit(solution)/shard_map/ppermute | solution.py:367
  122.4 9.6 %collective-permute-start.31 = (bf16[256,256]{1,0:T(8,128)(2,1)S(1)}, bf16[256,256]{1,0:T(8,128)(2,1)S(1)}, u32[]{:S(2)}, u32[]{:S(2)}) collective-permute-start(bf16[256,256]{1,0:T(8,128)(2,1)S(1)} %get-tuple-element.134), channel_id=1, source_target_pairs={{0,24},{8,16},{16,8},{24,0},{1,25},{9,17},{17,9},{25,1},{2,26},{10... | collective-permute-start | bytes 393224 | tf_op jit(solution)/shard_map/ppermute | solution.py:362
  122.7 9.3 %collective-permute-start.32 = (bf16[256,256]{1,0:T(8,128)(2,1)S(1)}, bf16[256,256]{1,0:T(8,128)(2,1)S(1)}, u32[]{:S(2)}, u32[]{:S(2)}) collective-permute-start(bf16[256,256]{1,0:T(8,128)(2,1)S(1)} %get-tuple-element.132), channel_id=1, source_target_pairs={{0,8},{8,0},{16,24},{24,16},{1,9},{9,1},{17,25},{25,17},{2,10},{10... | collective-permute-start | bytes 393224 | tf_op jit(solution)/shard_map/ppermute | solution.py:362
  141.2 6.8 %collective-permute-start.35 = (bf16[256,256]{1,0:T(8,128)(2,1)S(1)}, bf16[256,256]{1,0:T(8,128)(2,1)S(1)}, u32[]{:S(2)}, u32[]{:S(2)}) collective-permute-start(bf16[256,256]{1,0:T(8,128)(2,1)S(1)} %add_convert_fusion.3), channel_id=1, source_target_pairs={{0,4},{1,5},{2,6},{3,7},{4,0},{5,1},{6,2},{7,3},{8,12},{9,13},{10,... | collective-permute-start | bytes 393224 | tf_op jit(solution)/shard_map/ppermute | solution.py:367
  141.8 6.9 %collective-permute-start.43 = (bf16[96,256]{1,0:T(8,128)(2,1)S(1)}, bf16[96,256]{1,0:T(8,128)(2,1)S(1)}, u32[]{:S(2)}, u32[]{:S(2)}) collective-permute-start(bf16[96,256]{1,0:T(8,128)(2,1)S(1)} %get-tuple-element.138), channel_id=1, source_target_pairs={{0,24},{8,16},{16,8},{24,0},{1,25},{9,17},{17,9},{25,1},{2,26},{10... | collective-permute-start | bytes 147464 | tf_op jit(solution)/shard_map/ppermute | solution.py:362
  142.5 6.3 %collective-permute-start.44 = (bf16[96,256]{1,0:T(8,128)(2,1)S(1)}, bf16[96,256]{1,0:T(8,128)(2,1)S(1)}, u32[]{:S(2)}, u32[]{:S(2)}) collective-permute-start(bf16[96,256]{1,0:T(8,128)(2,1)S(1)} %get-tuple-element.140), channel_id=1, source_target_pairs={{0,8},{8,0},{16,24},{24,16},{1,9},{9,1},{17,25},{25,17},{2,10},{10... | collective-permute-start | bytes 147464 | tf_op jit(solution)/shard_map/ppermute | solution.py:362
  153.1 6.4 %collective-permute-start.37 = (bf16[2,256,256]{2,1,0:T(8,128)(2,1)S(1)}, bf16[2,256,256]{2,1,0:T(8,128)(2,1)S(1)}, u32[]{:S(2)}, u32[]{:S(2)}) collective-permute-start(bf16[2,256,256]{2,1,0:T(8,128)(2,1)S(1)} %pad_maximum_fusion.3), channel_id=1, source_target_pairs={{0,8},{8,0},{16,24},{24,16},{1,9},{9,1},{17,25},{25,17},{2,10},{10... | collective-permute-start | bytes 786440 | tf_op jit(solution)/shard_map/ppermute | solution.py:362
  153.7 6.0 %collective-permute-start.47 = (bf16[96,256]{1,0:T(8,128)(2,1)S(1)}, bf16[96,256]{1,0:T(8,128)(2,1)S(1)}, u32[]{:S(2)}, u32[]{:S(2)}) collective-permute-start(bf16[96,256]{1,0:T(8,128)(2,1)S(1)} %add_convert_fusion.6), channel_id=1, source_target_pairs={{0,4},{1,5},{2,6},{3,7},{4,0},{5,1},{6,2},{7,3},{8,12},{9,13},{10,... | collective-permute-start | bytes 147464 | tf_op jit(solution)/shard_map/ppermute | solution.py:367
  159.6 6.8 %collective-permute-start.38 = (bf16[4,256,256]{2,1,0:T(8,128)(2,1)S(1)}, bf16[4,256,256]{2,1,0:T(8,128)(2,1)S(1)}, u32[]{:S(2)}, u32[]{:S(2)}) collective-permute-start(bf16[4,256,256]{2,1,0:T(8,128)(2,1)S(1)} %pad_maximum_fusion.2.gathered_ref), channel_id=1, source_target_pairs={{0,1},{1,0},{2,3},{3,2},{4,5},{5,4},{6,7},{7,6},{8,9},{9,8},{10,11... | collective-permute-start | bytes 1572872 | tf_op jit(solution)/shard_map/ppermute | solution.py:367
  (58 other events, 507.1 us)
